TPU v7x, 32 devices: a whole 2x2x4 slice. The times are simulated.
32 devices in a mesh: seq: 4 (over y, core), fsdp: 8 (over z, x).
Axes of the slice: x: 2, y: 2, z: 4, core: 2. Of those that a mesh axis runs over, the one named last changes fastest.
Arguments:
- tokens: bfloat16 [8, 2048, 1024], P('fsdp', 'seq'), may hold values from -6 to 6
- value_routes: int32 [8, 2048, 4, 2], P('fsdp', 'seq'), may hold values from 0 to 4, all different within a row
- output_routes: int32 [8, 2048, 4, 2], P('fsdp', 'seq'), may hold values from 0 to 4, all different within a row
- cont_gap: int32 [2, 4], replicated, may hold values from 0 to 4095
- query_weight: bfloat16 [1024, 448], P('fsdp'), may hold values from -0.1875 to 0.1875
- key_weight: bfloat16 [1024, 448], P('fsdp'), may hold values from -0.1875 to 0.1875
- value_weight: bfloat16 [1024, 2240], P('fsdp'), may hold values from -0.1875 to 0.1875
- value_router: bfloat16 [1024, 20], P('fsdp'), may hold values from -0.125 to 0.125
- output_router: bfloat16 [1024, 20], P('fsdp'), may hold values from -0.125 to 0.125
- output_weight: bfloat16 [2240, 1024], P('fsdp'), may hold values from -2 to 2
- norm_gain: bfloat16 [1024], P('fsdp'), may hold values from 0.5 to 1.5
- norm_bias: bfloat16 [1024], P('fsdp'), may hold values from -2 to 2
- inner_weight: bfloat16 [1024, 4096], P('fsdp'), may hold values from -0.1875 to 0.1875
- outer_weight: bfloat16 [4096, 1024], P('fsdp'), may hold values from -0.09375 to 0.09375
- cotangent: bfloat16 [8, 2048, 1024], P('fsdp', 'seq'), may hold values from -6 to 6
Outputs:
- layer_out: bfloat16 [8, 2048, 1024], P('fsdp', 'seq')
- d_tokens: float32 [8, 2048, 1024], P('fsdp', 'seq')
- grad_query_weight: float32 [1024, 448], P('fsdp')
- grad_key_weight: float32 [1024, 448], P('fsdp')
- grad_value_weight: float32 [1024, 2240], P('fsdp')
- grad_value_router: float32 [1024, 20], P('fsdp')
- grad_output_router: float32 [1024, 20], P('fsdp')
- grad_output_weight: float32 [2240, 1024], P('fsdp')
- grad_norm_gain: float32 [1024], P('fsdp')
- grad_norm_bias: float32 [1024], P('fsdp')
- grad_inner_weight: float32 [1024, 4096], P('fsdp')
- grad_outer_weight: float32 [4096, 1024], P('fsdp')
All inputs are finite; a program needn't handle non-finite values.
Results may differ from a plain program's by a relative error of at most 0.017.
Values may be sent and summed in bfloat16 or wider, within the bound.
A program may use at most 192 MiB of HBM per device.

v0:
```python
import jax
import jax.numpy as jnp
from jax import lax
from jax.sharding import PartitionSpec as P

HEADS = 4
DH = 112
EXP = 5
CONT = 1024
GSLOTS = 4
PSLOTS = 2
BLOCK = 512


EPSILON = 1e-05
NEGATIVE = -1e30


def shifted(value, axis, steps):
    count = lax.axis_size(axis)
    initial, last = (max(0, -steps), min(count, count - steps))
    return lax.ppermute(value, axis, [(source, source + steps) for source in range(initial, last)])


def smooth_gate(value):
    return jax.nn.gelu(value, approximate=True)


def route_mask(routes):
    chosen = routes[0]
    expert_ids = jnp.arange(EXP, dtype=jnp.int32)
    matched = jnp.any(chosen[:, :, :, None] == expert_ids, axis=2)
    return matched.astype(jnp.float32).reshape(chosen.shape[0], HEADS * EXP)


def visible(query_place, query_segment, key_place, key_segment):
    before = key_place[None, :] <= query_place[:, None]
    from_prompt = (key_segment[None, :] == 0) & ((query_segment[:, None] > 0) | before)
    same_part = (key_segment[None, :] == query_segment[:, None]) & before
    return from_prompt | same_part


def block_scores(query_block, key_block, query_place, query_segment, key_place, key_segment, slope):
    raw_scores = jnp.einsum("qd,kd->qk", query_block, key_block, preferred_element_type=jnp.float32)
    distance = jnp.maximum(query_place[:, None] - key_place[None, :], 0).astype(jnp.float32)
    scores = raw_scores * DH ** (-0.5) + slope * jnp.log1p(distance)
    return (scores, visible(query_place, query_segment, key_place, key_segment))


def sweep(update, running, bounds):
    first_end, second_start, second_end = bounds
    running = lax.fori_loop(0, first_end, update, running)
    return lax.fori_loop(second_start, second_end, update, running)


def rows_at(array, row_start):
    return lax.dynamic_slice_in_dim(array, row_start, BLOCK, 0)


def pick_piece(slot_index, own_pair, received, source):
    chosen = jnp.where(slot_index == source, own_pair, jnp.zeros_like(own_pair))
    for distance in range(1, len(received) + 1):
        chosen = jnp.where(slot_index - distance == source, received[distance - 1], chosen)
    return chosen


def head_forward(queries, key_store, value_store, places, bounds_of, slope):
    own_place, own_segment, key_place, key_segment = places
    head_size = queries.shape[1]

    def one_block(block_index):
        row_start = block_index * BLOCK
        query_block = rows_at(queries, row_start)
        query_place = rows_at(own_place, row_start)
        query_segment = rows_at(own_segment, row_start)

        def online_update(key_index, running):
            running_top, running_total, accumulated = running
            key_start = key_index * BLOCK
            scores, allowed = block_scores(
                query_block,
                rows_at(key_store, key_start),
                query_place,
                query_segment,
                rows_at(key_place, key_start),
                rows_at(key_segment, key_start),
                slope,
            )
            new_top = jnp.maximum(
                running_top, jnp.max(jnp.where(allowed, scores, NEGATIVE), axis=1)
            )
            factor = jnp.exp(running_top - new_top)
            exp_terms = jnp.where(allowed, jnp.exp(scores - new_top[:, None]), 0.0)
            accumulated = accumulated * factor[:, None] + jnp.dot(
                exp_terms.astype(jnp.bfloat16),
                rows_at(value_store, key_start),
                preferred_element_type=jnp.float32,
            )
            return (new_top, running_total * factor + jnp.sum(exp_terms, axis=1), accumulated)

        start_state = (
            jnp.full((BLOCK,), NEGATIVE, jnp.float32),
            jnp.zeros((BLOCK,), jnp.float32),
            jnp.zeros((BLOCK, head_size), jnp.float32),
        )
        running_top, running_total, accumulated = sweep(
            online_update, start_state, bounds_of(block_index)
        )
        log_total = running_top + jnp.log(running_total)
        return (accumulated / running_total[:, None], log_total)

    block_count = queries.shape[0] // BLOCK
    outputs, log_totals = lax.map(one_block, jnp.arange(block_count, dtype=jnp.int32))
    return (
        outputs.reshape(block_count * BLOCK, head_size),
        log_totals.reshape(block_count * BLOCK),
    )


def head_backward(
    queries, key_store, value_store, places, bounds_of, slope, grad_heads, outputs, log_totals
):
    own_place, own_segment, key_place, key_segment = places
    head_size = queries.shape[1]
    delta_rows = jnp.sum(grad_heads.astype(jnp.float32) * outputs, axis=1)

    def one_block(block_index, totals):
        grad_query, grad_key, grad_value = totals
        row_start = block_index * BLOCK
        query_block = rows_at(queries, row_start)
        grad_block = rows_at(grad_heads, row_start)
        query_place = rows_at(own_place, row_start)
        query_segment = rows_at(own_segment, row_start)
        log_block = rows_at(log_totals, row_start)
        delta_block = rows_at(delta_rows, row_start)

        def key_update(key_index, running):
            query_sum, key_sums, value_sums = running
            key_start = key_index * BLOCK
            key_block = rows_at(key_store, key_start)
            value_block = rows_at(value_store, key_start)
            scores, allowed = block_scores(
                query_block,
                key_block,
                query_place,
                query_segment,
                rows_at(key_place, key_start),
                rows_at(key_segment, key_start),
                slope,
            )
            weights = jnp.where(allowed, jnp.exp(scores - log_block[:, None]), 0.0)
            weights_low = weights.astype(jnp.bfloat16)
            grad_weights = jnp.einsum(
                "qd,kd->qk", grad_block, value_block, preferred_element_type=jnp.float32
            )
            grad_raw = (weights * (grad_weights - delta_block[:, None]) * DH ** (-0.5)).astype(
                jnp.bfloat16
            )
            query_sum = query_sum + jnp.dot(grad_raw, key_block, preferred_element_type=jnp.float32)
            key_part = jnp.einsum(
                "qk,qd->kd", grad_raw, query_block, preferred_element_type=jnp.float32
            )
            value_part = jnp.einsum(
                "qk,qd->kd", weights_low, grad_block, preferred_element_type=jnp.float32
            )
            key_sums = lax.dynamic_update_slice_in_dim(
                key_sums, rows_at(key_sums, key_start) + key_part, key_start, 0
            )
            value_sums = lax.dynamic_update_slice_in_dim(
                value_sums, rows_at(value_sums, key_start) + value_part, key_start, 0
            )
            return (query_sum, key_sums, value_sums)

        start_sums = (jnp.zeros((BLOCK, head_size), jnp.float32), grad_key, grad_value)
        query_sum, grad_key, grad_value = sweep(key_update, start_sums, bounds_of(block_index))
        grad_query = lax.dynamic_update_slice_in_dim(grad_query, query_sum, row_start, 0)
        return (grad_query, grad_key, grad_value)

    block_count = queries.shape[0] // BLOCK
    empty_store = jnp.zeros((key_store.shape[0], head_size), jnp.float32)
    start_totals = (jnp.zeros(queries.shape, jnp.float32), empty_store, empty_store)
    return lax.fori_loop(0, block_count, one_block, start_totals)


def on_device(
    tokens,
    value_routes,
    output_routes,
    cont_gap,
    query_weight,
    key_weight,
    value_weight,
    value_router,
    output_router,
    output_weight,
    norm_gain,
    norm_bias,
    inner_weight,
    outer_weight,
    cotangent,
):
    seq_count = lax.axis_size("seq")
    seq_index = lax.axis_index("seq")
    fsdp_index = lax.axis_index("fsdp")
    local_rows = tokens.shape[1]
    slot_tok = local_rows * seq_count
    heads_here = HEADS // seq_count
    head_width = heads_here * DH
    slot_index = fsdp_index % GSLOTS
    group_index = fsdp_index // GSLOTS
    is_prompt = slot_index < PSLOTS
    prompt_len = PSLOTS * slot_tok
    (
        query_full,
        key_full,
        value_full,
        value_gate_full,
        output_gate_full,
        output_full,
        gain_full,
        bias_full,
        inner_full,
        outer_full,
    ) = (
        lax.all_gather(query_weight, "fsdp", axis=0, tiled=True),
        lax.all_gather(key_weight, "fsdp", axis=0, tiled=True),
        lax.all_gather(value_weight, "fsdp", axis=0, tiled=True),
        lax.all_gather(value_router, "fsdp", axis=0, tiled=True),
        lax.all_gather(output_router, "fsdp", axis=0, tiled=True),
        lax.all_gather(output_weight, "fsdp", axis=0, tiled=True),
        lax.all_gather(norm_gain, "fsdp", axis=0, tiled=True),
        lax.all_gather(norm_bias, "fsdp", axis=0, tiled=True),
        lax.all_gather(inner_weight, "fsdp", axis=0, tiled=True),
        lax.all_gather(outer_weight, "fsdp", axis=0, tiled=True),
    )
    inputs = tokens[0]
    value_mask = route_mask(value_routes)
    output_mask = route_mask(output_routes)
    queries = jnp.dot(inputs, query_full, preferred_element_type=jnp.float32).astype(jnp.bfloat16)
    key_rows = jnp.dot(inputs, key_full, preferred_element_type=jnp.float32).astype(jnp.bfloat16)
    expert_values = jnp.dot(inputs, value_full, preferred_element_type=jnp.float32)
    value_sigmoid = jax.nn.sigmoid(
        jnp.dot(inputs, value_gate_full, preferred_element_type=jnp.float32)
    )
    value_gates = value_sigmoid * value_mask
    mixed_values = (
        jnp.sum(
            value_gates.reshape(local_rows, HEADS, EXP, 1)
            * expert_values.reshape(local_rows, HEADS, EXP, DH),
            axis=2,
        )
        .reshape(local_rows, HEADS * DH)
        .astype(jnp.bfloat16)
    )
    output_sigmoid = jax.nn.sigmoid(
        jnp.dot(inputs, output_gate_full, preferred_element_type=jnp.float32)
    )
    output_gates = output_sigmoid * output_mask
    head_queries, head_keys, head_values = (
        lax.all_to_all(queries, "seq", split_axis=1, concat_axis=0, tiled=True),
        lax.all_to_all(key_rows, "seq", split_axis=1, concat_axis=0, tiled=True),
        lax.all_to_all(mixed_values, "seq", split_axis=1, concat_axis=0, tiled=True),
    )
    own_pair = jnp.concatenate([head_keys, head_values], axis=1)
    received = []
    for distance in range(1, GSLOTS):
        received.append(shifted(own_pair, "fsdp", distance))
    prompt_pieces = [pick_piece(slot_index, own_pair, received, source) for source in range(PSLOTS)]
    pair_store = jnp.concatenate(prompt_pieces + [own_pair], axis=0)
    local_index = jnp.arange(slot_tok, dtype=jnp.int32)
    offset = jnp.maximum((slot_index - PSLOTS) * slot_tok + local_index, 0)
    cont_index = offset // CONT
    gaps = lax.dynamic_slice_in_dim(cont_gap, group_index, 1, 0)[0]
    cont_ids = jnp.arange(gaps.shape[0], dtype=jnp.int32)
    gap_rows = jnp.sum(
        jnp.where(cont_index[:, None] == cont_ids[None, :], gaps[None, :], 0), axis=1
    )
    own_place = jnp.where(
        is_prompt, slot_index * slot_tok + local_index, prompt_len + gap_rows + offset % CONT
    )
    own_segment = jnp.where(is_prompt, 0, cont_index + 1)
    key_place = jnp.concatenate([jnp.arange(prompt_len, dtype=jnp.int32), own_place])
    key_segment = jnp.concatenate([jnp.zeros((prompt_len,), jnp.int32), own_segment])
    places = (own_place, own_segment, key_place, key_segment)
    per_slot = slot_tok // BLOCK
    prompt_blocks = PSLOTS * per_slot

    def bounds_of(block_index):
        cont_first = block_index * BLOCK // CONT * (CONT // BLOCK)
        first_end = jnp.where(is_prompt, slot_index * per_slot + block_index + 1, prompt_blocks)
        second_start = jnp.where(is_prompt, 0, prompt_blocks + cont_first)
        second_end = jnp.where(is_prompt, 0, prompt_blocks + block_index + 1)
        return (first_end, second_start, second_end)

    local_head = 0
    head_number = seq_index * heads_here + local_head
    slope_value = jnp.float32(0.0)
    for candidate in range(HEADS):
        slope_value = jnp.where(head_number == candidate, -0.5 * 0.5**candidate, slope_value)
    slopes = [slope_value]
    first_col = local_head * DH
    outputs, log_totals = head_forward(
        head_queries,
        pair_store[:, first_col : first_col + DH],
        pair_store[:, head_width + first_col : head_width + first_col + DH],
        places,
        bounds_of,
        slope_value,
    )
    head_outputs = [outputs]
    head_logs = [log_totals]
    attended_low = head_outputs[0].astype(jnp.bfloat16)
    token_attended = lax.all_to_all(attended_low, "seq", split_axis=0, concat_axis=1, tiled=True)
    attended_wide = token_attended.astype(jnp.float32).reshape(local_rows, HEADS, 1, DH)
    mixed = (
        (output_gates.reshape(local_rows, HEADS, EXP, 1) * attended_wide)
        .reshape(local_rows, HEADS * EXP * DH)
        .astype(jnp.bfloat16)
    )
    branch = jnp.dot(mixed, output_full, preferred_element_type=jnp.float32)
    residual = inputs.astype(jnp.float32) + branch
    average = jnp.mean(residual, axis=1, keepdims=True)
    centred = residual - average
    inverse = lax.rsqrt(jnp.mean(centred * centred, axis=1, keepdims=True) + EPSILON)
    normed = centred * inverse
    gain_wide = gain_full.astype(jnp.float32)
    scaled_low = (normed * gain_wide + bias_full.astype(jnp.float32)).astype(jnp.bfloat16)
    inner = jnp.dot(scaled_low, inner_full, preferred_element_type=jnp.float32)
    active, gate_pullback = jax.vjp(smooth_gate, inner)
    active_low = active.astype(jnp.bfloat16)
    layer_out = (
        residual + jnp.dot(active_low, outer_full, preferred_element_type=jnp.float32)
    ).astype(jnp.bfloat16)
    grad_top = cotangent[0]
    grad_outer_w = jnp.einsum("rf,rd->fd", active_low, grad_top, preferred_element_type=jnp.float32)
    grad_active = jnp.einsum("rd,fd->rf", grad_top, outer_full, preferred_element_type=jnp.float32)
    grad_inner_low = gate_pullback(grad_active)[0].astype(jnp.bfloat16)
    grad_inner_w = jnp.einsum(
        "rd,rf->df", scaled_low, grad_inner_low, preferred_element_type=jnp.float32
    )
    grad_scaled = jnp.einsum(
        "rf,df->rd", grad_inner_low, inner_full, preferred_element_type=jnp.float32
    )
    grad_gain = jnp.sum(grad_scaled * normed, axis=0)
    grad_bias = jnp.sum(grad_scaled, axis=0)
    grad_normed = grad_scaled * gain_wide
    grad_residual = grad_top.astype(jnp.float32) + inverse * (
        grad_normed
        - jnp.mean(grad_normed, axis=1, keepdims=True)
        - normed * jnp.mean(grad_normed * normed, axis=1, keepdims=True)
    )
    grad_branch = grad_residual.astype(jnp.bfloat16)
    grad_output_w = jnp.einsum("rm,rd->md", mixed, grad_branch, preferred_element_type=jnp.float32)
    grad_mixed = jnp.einsum(
        "rd,md->rm", grad_branch, output_full, preferred_element_type=jnp.float32
    ).reshape(local_rows, HEADS, EXP, DH)
    grad_attended = (
        jnp.sum(output_gates.reshape(local_rows, HEADS, EXP, 1) * grad_mixed, axis=2)
        .reshape(local_rows, HEADS * DH)
        .astype(jnp.bfloat16)
    )
    grad_output_gate = jnp.sum(grad_mixed * attended_wide, axis=3).reshape(local_rows, HEADS * EXP)
    grad_output_logit = (
        grad_output_gate * output_mask * output_sigmoid * (1.0 - output_sigmoid)
    ).astype(jnp.bfloat16)
    grad_heads_in = lax.all_to_all(grad_attended, "seq", split_axis=1, concat_axis=0, tiled=True)
    local_head = 0
    first_col = local_head * DH
    grad_query_h, grad_key_h, grad_value_h = head_backward(
        head_queries,
        pair_store[:, first_col : first_col + DH],
        pair_store[:, head_width + first_col : head_width + first_col + DH],
        places,
        bounds_of,
        slopes[local_head],
        grad_heads_in,
        head_outputs[local_head],
        head_logs[local_head],
    )
    grad_key_parts = [grad_key_h]
    grad_value_parts = [grad_value_h]
    grad_pairs = jnp.concatenate(grad_key_parts + grad_value_parts, axis=1)
    piece_grads = [
        grad_pairs[source * slot_tok : (source + 1) * slot_tok] for source in range(PSLOTS)
    ]
    own_grad = grad_pairs[prompt_len:]
    for source in range(PSLOTS):
        own_grad = own_grad + jnp.where(slot_index == source, piece_grads[source], 0.0)
    for distance in range(1, GSLOTS):
        outgoing = jnp.zeros_like(own_grad)
        for source in range(PSLOTS):
            outgoing = outgoing + jnp.where(
                slot_index - distance == source, piece_grads[source], 0.0
            )
        own_grad = own_grad + shifted(outgoing.astype(jnp.bfloat16), "fsdp", -distance).astype(
            outgoing.dtype
        )
    own_low = own_grad.astype(jnp.bfloat16)
    grad_query_heads = grad_query_h.astype(jnp.bfloat16)
    back_queries, back_keys, back_values = (
        lax.all_to_all(grad_query_heads, "seq", split_axis=0, concat_axis=1, tiled=True),
        lax.all_to_all(own_low[:, :head_width], "seq", split_axis=0, concat_axis=1, tiled=True),
        lax.all_to_all(own_low[:, head_width:], "seq", split_axis=0, concat_axis=1, tiled=True),
    )
    back_wide = back_values.astype(jnp.float32).reshape(local_rows, HEADS, 1, DH)
    grad_experts = (
        (value_gates.reshape(local_rows, HEADS, EXP, 1) * back_wide)
        .reshape(local_rows, HEADS * EXP * DH)
        .astype(jnp.bfloat16)
    )
    grad_value_gate = jnp.sum(
        expert_values.reshape(local_rows, HEADS, EXP, DH) * back_wide, axis=3
    ).reshape(local_rows, HEADS * EXP)
    grad_value_logit = (
        grad_value_gate * value_mask * value_sigmoid * (1.0 - value_sigmoid)
    ).astype(jnp.bfloat16)
    grad_query_w = jnp.einsum("rd,rc->dc", inputs, back_queries, preferred_element_type=jnp.float32)
    grad_key_w = jnp.einsum("rd,rc->dc", inputs, back_keys, preferred_element_type=jnp.float32)
    grad_value_w = jnp.einsum("rd,rc->dc", inputs, grad_experts, preferred_element_type=jnp.float32)
    grad_value_gate_w = jnp.einsum(
        "rd,rc->dc", inputs, grad_value_logit, preferred_element_type=jnp.float32
    )
    grad_output_gate_w = jnp.einsum(
        "rd,rc->dc", inputs, grad_output_logit, preferred_element_type=jnp.float32
    )
    grad_input = grad_residual + jnp.einsum(
        "rc,dc->rd", back_queries, query_full, preferred_element_type=jnp.float32
    )
    grad_input = grad_input + jnp.einsum(
        "rc,dc->rd", back_keys, key_full, preferred_element_type=jnp.float32
    )
    grad_input = grad_input + jnp.einsum(
        "rc,dc->rd", grad_experts, value_full, preferred_element_type=jnp.float32
    )
    grad_input = grad_input + jnp.einsum(
        "rc,dc->rd", grad_value_logit, value_gate_full, preferred_element_type=jnp.float32
    )
    grad_input = grad_input + jnp.einsum(
        "rc,dc->rd", grad_output_logit, output_gate_full, preferred_element_type=jnp.float32
    )
    reduced = (
        lax.psum_scatter(grad_query_w, "fsdp", scatter_dimension=0, tiled=True),
        lax.psum_scatter(grad_key_w, "fsdp", scatter_dimension=0, tiled=True),
        lax.psum_scatter(grad_value_w, "fsdp", scatter_dimension=0, tiled=True),
        lax.psum_scatter(grad_value_gate_w, "fsdp", scatter_dimension=0, tiled=True),
        lax.psum_scatter(grad_output_gate_w, "fsdp", scatter_dimension=0, tiled=True),
        lax.psum_scatter(grad_output_w, "fsdp", scatter_dimension=0, tiled=True),
        lax.psum_scatter(grad_gain, "fsdp", scatter_dimension=0, tiled=True),
        lax.psum_scatter(grad_bias, "fsdp", scatter_dimension=0, tiled=True),
        lax.psum_scatter(grad_inner_w, "fsdp", scatter_dimension=0, tiled=True),
        lax.psum_scatter(grad_outer_w, "fsdp", scatter_dimension=0, tiled=True),
    )
    final = (
        lax.psum(reduced[0].astype(jnp.bfloat16), "seq").astype(jnp.float32),
        lax.psum(reduced[1].astype(jnp.bfloat16), "seq").astype(jnp.float32),
        lax.psum(reduced[2].astype(jnp.bfloat16), "seq").astype(jnp.float32),
        lax.psum(reduced[3].astype(jnp.bfloat16), "seq").astype(jnp.float32),
        lax.psum(reduced[4].astype(jnp.bfloat16), "seq").astype(jnp.float32),
        lax.psum(reduced[5].astype(jnp.bfloat16), "seq").astype(jnp.float32),
        lax.psum(reduced[6].astype(jnp.bfloat16), "seq").astype(jnp.float32),
        lax.psum(reduced[7].astype(jnp.bfloat16), "seq").astype(jnp.float32),
        lax.psum(reduced[8].astype(jnp.bfloat16), "seq").astype(jnp.float32),
        lax.psum(reduced[9].astype(jnp.bfloat16), "seq").astype(jnp.float32),
    )
    return (
        layer_out[None],
        grad_input[None],
        final[0],
        final[1],
        final[2],
        final[3],
        final[4],
        final[5],
        final[6],
        final[7],
        final[8],
        final[9],
    )


def solution(mesh):
    return jax.shard_map(
        on_device,
        mesh=mesh,
        in_specs=(
            P("fsdp", "seq", None),
            P("fsdp", "seq", None, None),
            P("fsdp", "seq", None, None),
            P(),
            P("fsdp", None),
            P("fsdp", None),
            P("fsdp", None),
            P("fsdp", None),
            P("fsdp", None),
            P("fsdp", None),
            P("fsdp"),
            P("fsdp"),
            P("fsdp", None),
            P("fsdp", None),
            P("fsdp", "seq", None),
        ),
        out_specs=(
            P("fsdp", "seq", None),
            P("fsdp", "seq", None),
            P("fsdp", None),
            P("fsdp", None),
            P("fsdp", None),
            P("fsdp", None),
            P("fsdp", None),
            P("fsdp", None),
            P("fsdp"),
            P("fsdp"),
            P("fsdp", None),
            P("fsdp", None),
        ),
        check_vma=False,
    )
```

profile of v0, /device:TPU:0, one launch (start us, length us, event | category | flops | bytes accessed | tf_op | source)
XLA Modules:
  0.0 2134.0 jit_solution(2377234677451424760)
XLA Ops:
  9.4 37.7 %all_gather.32 = bf16[1024,448]{0,1:T(8,128)(2,1)S(1)} all-gather(bf16[128,448]{0,1:T(8,128)(2,1)} %param.32), channel_id=1, replica_groups=mesh['seq'=4,'fsdp'=8] {'fsdp'}, dimensions={0}, use_global_device_ids=true | all-gather | bytes 1032192 | tf_op jit(solution)/shard_map/all_gather | solution.py:226
  49.6 3.5 all-to-all-start.1
  53.2 28.9 %all_gather.33 = bf16[1024,20]{0,1:T(8,128)(2,1)S(1)} all-gather(bf16[128,20]{0,1:T(8,128)(2,1)S(1)} %copy-done.50), channel_id=1, replica_groups=mesh['seq'=4,'fsdp'=8] {'fsdp'}, dimensions={0}, use_global_device_ids=true | all-gather | bytes 46080 | tf_op jit(solution)/shard_map/all_gather | solution.py:228
  83.8 19.1 all-gather.7.cloned.1.call-done
  102.9 8.0 multiply_reduce_fusion.3
  110.9 3.5 all-to-all-start.2
  114.4 40.8 %all_gather.31 = bf16[1024,448]{0,1:T(8,128)(2,1)S(1)} all-gather(bf16[128,448]{0,1:T(8,128)(2,1)S(1)} %copy-done.38), channel_id=1, replica_groups=mesh['seq'=4,'fsdp'=8] {'fsdp'}, dimensions={0}, use_global_device_ids=true | all-gather | bytes 1032192 | tf_op jit(solution)/shard_map/all_gather | solution.py:225
  155.3 2.3 collective-permute-start
  157.7 3.5 collective-permute-start.1
  161.2 3.8 collective-permute-start.2
  166.4 3.5 all-to-all-start
  173.3 4.8 all-to-all-done
  179.0 18.1 collective-permute-done
  197.1 30.1 %collective-permute-done.1 = bf16[2048,224]{0,1:T(8,128)(2,1)} collective-permute-done((bf16[2048,224]{0,1:T(8,128)(2,1)S(1)}, bf16[2048,224]{0,1:T(8,128)(2,1)}, u32[]{:S(2)}, u32[]{:S(2)}) %collective-permute-start.1) | collective-permute-done | bytes 917536 | tf_op jit(solution)/shard_map/ppermute | solution.py:22
  234.2 61.0 %while.181 = (s32[]{:T(128)}, f32[4,512,112]{1,2,0:T(8,128)}, f32[4,512]{1,0:T(4,128)}, s32[4]{0:T(128)}, pred[]{:T(512)}, /*index=5*/s32[]{:T(128)}, bf16[2048,...) while((s32[]{:T(128)}, f32[4,512,112]{1,2,0:T(8,128)}, ...), condition=%wide.region_13.14_spmd, body=%wide.region_4.13_spmd.sunk | while | flops 251949600 | bytes 9082205 | solution.py:113
  238.5 3.3 while.185
  248.9 6.5 while.185
  262.5 9.8 while.185
  279.4 13.0 while.185
  295.2 2.8 convert_element_type.212
  298.0 4.1 all-to-all-start.3
  302.9 186.9 %all_gather.30 = bf16[1024,20]{0,1:T(8,128)(2,1)S(1)} all-gather(bf16[128,20]{0,1:T(8,128)(2,1)} %param.35), channel_id=1, replica_groups=mesh['seq'=4,'fsdp'=8] {'fsdp'}, dimensions={0}, use_global_device_ids=true | all-gather | bytes 46080 | tf_op jit(solution)/shard_map/all_gather | solution.py:229
  491.5 18.1 all-gather.1
  509.6 16.6 all-gather
  530.2 6.0 fusion.123
  536.6 10.7 fusion.120
  547.3 13.0 fusion.76
  560.4 5.6 multiply_reduce_fusion.4
  566.9 5.7 fusion.108
  574.3 5.5 all-to-all-start.4
  580.7 7.2 all-to-all-done.4
  592.0 86.7 %while.184 = (s32[]{:T(128)}, bf16[2048,112]{0,1:T(8,128)(2,1)}, f32[6144,112]{0,1:T(8,128)S(1)}, f32[6144,112]{0,1:T(8,128)}, pred[]{:T(512)}, /*index=5*/s32[]...) while((s32[]{:T(128)}, bf16[2048,112]{0,1:T(8,128)(2,1)}, ...), condition=%wide.region_25.26_spmd, body=%wide.region_20.25_spmd.sunk | while | flops 597510144 | bytes 15141325 | solution.py:182
  594.2 7.6 while.187
  604.4 15.2 while.187
  622.2 22.8 %while.187 = (s32[]{:T(128)}, f32[512,112]{0,1:T(8,128)S(1)}, f32[6144,112]{0,1:T(8,128)S(1)}, f32[6144,112]{0,1:T(8,128)}, s32[]{:T(128)}, /*index=5*/s32[6144]...) while((s32[]{:T(128)}, f32[512,112]{0,1:T(8,128)S(1)}, ...), condition=%wide.region_22.22_spmd, body=%wide.region_21.21_spmd.sunk | while | flops 298755072 | bytes 6988551 | solution.py:52
  647.7 30.3 %while.187 = (s32[]{:T(128)}, f32[512,112]{0,1:T(8,128)S(1)}, f32[6144,112]{0,1:T(8,128)S(1)}, f32[6144,112]{0,1:T(8,128)}, s32[]{:T(128)}, /*index=5*/s32[6144]...) while((s32[]{:T(128)}, f32[512,112]{0,1:T(8,128)S(1)}, ...), condition=%wide.region_22.22_spmd, body=%wide.region_21.21_spmd.sunk | while | flops 298755072 | bytes 6988551 | solution.py:52
  680.5 3.5 all-to-all-start.5
  685.7 6.4 all-to-all-done.5
  692.1 3.3 convolution_bitcast_fusion.2
  697.1 2.9 add_convert_fusion.4
  704.0 244.2 %collective-permute-done.5 = bf16[2048,224]{0,1:T(8,128)(2,1)S(1)} collective-permute-done((bf16[2048,224]{0,1:T(8,128)(2,1)S(1)}, bf16[2048,224]{0,1:T(8,128)(2,1)S(1)}, u32[]{:S(2)}, u32[]{:S(2)}) %collective-permute-start.5) | collective-permute-done | bytes 917536 | tf_op jit(solution)/shard_map/ppermute | solution.py:22
  950.0 10.5 all_to_all.131
  963.2 7.8 fusion.106
  972.1 10.7 all_to_all.132
  982.9 3.2 multiply_convert_fusion.1
  987.5 6.1 convolution_bitcast_fusion
  994.3 13.4 fusion.119
  1008.0 15.3 fusion.91
  1025.2 59.4 %all-reduce.3 = (bf16[1024]{0:T(1024)(128)(2,1)S(1)}, bf16[1024]{0:T(1024)(128)(2,1)S(1)}) all-reduce(f32[1024]{0:T(1024)S(1)} %copy-done.51, f32[1024]{0:T(1024)S(1)} %copy-done.52), channel_id=8, replica_groups=mesh['seq'=4,'fsdp'=8] {'fsdp'}, use_global_device_ids=true, to_apply=%region_41.42.clone | all-reduce | flops 2048 | bytes 12288
  1084.7 12.5 fusion.82
  1104.3 141.0 %reduce-scatter.19.cloned.1.call-done = f32[280,1024]{1,0:T(8,128)} async-done(((f32[2240,1024]{1,0:T(8,128)}), f32[280,1024]{1,0:T(8,128)}) %reduce-scatter.19.cloned.1.call-update) | async-done | bytes 1146896 | tf_op jit(solution)/shard_map/reduce_scatter | solution.py:447
  1245.3 2.1 convert_element_type.251
  1247.4 161.3 %reduce-scatter.13.cloned.1.call-done = f32[128,2240]{0,1:T(8,128)} async-done(((f32[1024,2240]{0,1:T(8,128)}), f32[128,2240]{0,1:T(8,128)}) %reduce-scatter.13.cloned.1.call-update) | async-done | bytes 1146896 | tf_op jit(solution)/shard_map/reduce_scatter | solution.py:444
  1408.7 2.1 convert_element_type.245
  1410.8 282.9 %reduce-scatter.21.cloned.1.call-done = f32[128,4096]{1,0:T(8,128)} async-done(((f32[1024,4096]{1,0:T(8,128)}), f32[128,4096]{1,0:T(8,128)}) %reduce-scatter.21.cloned.1.call-update) | async-done | bytes 2097168 | tf_op jit(solution)/shard_map/reduce_scatter | solution.py:450
  1693.7 2.7 convert_element_type.257
  1696.4 283.0 %reduce-scatter.23.cloned.1.call-done = f32[512,1024]{1,0:T(8,128)} async-done(((f32[4096,1024]{1,0:T(8,128)}), f32[512,1024]{1,0:T(8,128)}) %reduce-scatter.23.cloned.1.call-update) | async-done | bytes 2097168 | tf_op jit(solution)/shard_map/reduce_scatter | solution.py:451
  1979.4 2.7 convert_element_type.259
  1984.8 4.7 fusion.125
  1989.5 2.5 add_bitcast_fusion
  1992.0 47.6 %reduce-scatter.15.cloned.1.call-done = f32[128,20]{0,1:T(8,128)} async-done(((f32[1024,20]{0,1:T(8,128)}), f32[128,20]{0,1:T(8,128)}) %reduce-scatter.15.cloned.1.call-update) | async-done | bytes 10256 | tf_op jit(solution)/shard_map/reduce_scatter | solution.py:445
  2040.3 10.1 all-reduce.4
  2052.7 64.6 %all-reduce.8.cloned.1.call-done = (bf16[128,448]{0,1:T(8,128)(2,1)}, bf16[128,448]{0,1:T(8,128)(2,1)}, bf16[128,2240]{0,1:T(8,128)(2,1)}, bf16[280,1024]{1,0:T(...) async-done(((bf16[128,448]{0,1:T(8,128)(2,1)}, bf16[128,448]{0,1:T(8,128)(2,1)}, bf16[128,2240]{0,1:T(8,128)(2,1)}, bf16[280,1024]{1,0:T(8,128)(2,1)}, ...) | async-done | bytes 3473424 | tf_op jit(solution)/shard_map/psum | solution.py:454
  2120.6 2.1 convert_element_type.246
  (473 shorter events, 210.5 us)
Async XLA Ops:
  7.2 163.4 %copy-start = (s32[2,4]{1,0:T(2,128)S(1)}, s32[2,4]{1,0:T(2,128)}, u32[]{:S(2)}) copy-start(s32[2,4]{1,0:T(2,128)} %param.30) | copy-start | bytes 100
  7.2 41.0 %copy-start.5 = (bf16[1,512,1024]{2,1,0:T(8,128)(2,1)S(1)}, bf16[1,512,1024]{2,1,0:T(8,128)(2,1)}, u32[]{:S(2)}) copy-start(bf16[1,512,1024]{2,1,0:T(8,128)(2,1)} %param.27) | copy-start | bytes 3145732
  7.2 95.7 %all-gather.7.cloned.1.call-start = ((), (), s32[]{:S(2)}) async-start(), calls=%async_computation.16 | async-start | bytes 5160960 | tf_op jit(solution)/shard_map/all_gather | solution.py:227
  7.9 522.3 %all-gather.9.cloned.1.call-start = ((), (), s32[]{:S(2)}) async-start(), calls=%async_computation.17 | async-start | bytes 5160960 | tf_op jit(solution)/shard_map/all_gather | solution.py:230
  8.7 527.9 %all-gather.11.cloned.1.call-start = ((), (), s32[]{:S(2)}) async-start(), calls=%async_computation.18 | async-start | bytes 9437184 | tf_op jit(solution)/shard_map/all_gather | solution.py:233
  9.4 43.6 %copy-start.45 = (s32[1,512,4,2]{1,3,2,0:T(2,128)S(1)}, s32[1,512,4,2]{1,3,2,0:T(2,128)}, u32[]{:S(2)}) copy-start(s32[1,512,4,2]{1,3,2,0:T(2,128)} %param.28) | copy-start | bytes 49156
  9.4 43.7 %copy-start.50 = (bf16[128,20]{0,1:T(8,128)(2,1)S(1)}, bf16[128,20]{0,1:T(8,128)(2,1)}, u32[]{:S(2)}) copy-start(bf16[128,20]{0,1:T(8,128)(2,1)} %param.34) | copy-start | bytes 15364
  49.6 61.3 %all-to-all-start.1 = ((bf16[512,4,112]{0,2,1:T(8,128)(2,1)}), bf16[512,4,112]{0,2,1:T(8,128)(2,1)S(1)}, u32[]{:S(2)}, u32[]{:S(2)}) async-start(bf16[512,4,112]{0,2,1:T(8,128)(2,1)} %bitcast.15), calls=%async_computation.1 | async-start | bytes 917504 | tf_op jit(solution)/shard_map/all_to_all | solution.py:261
  53.2 30.6 %copy-start.39 = (pred[512,20]{0,1:T(8,128)(4,1)}, pred[512,20]{0,1:T(8,128)(4,1)S(1)}, u32[]{:S(2)}) copy-start(pred[512,20]{0,1:T(8,128)(4,1)S(1)} %reduce_or.25) | copy-start | bytes 30724
  83.8 27.1 %copy-start.33 = (f32[512,4,5]{0,2,1:T(8,128)}, f32[512,4,5]{0,2,1:T(8,128)S(1)}, u32[]{:S(2)}) copy-start(f32[512,4,5]{0,2,1:T(8,128)S(1)} %mul.335) | copy-start | bytes 122884
  102.9 11.5 copy-start.38
  110.9 44.3 %all-to-all-start.2 = ((bf16[512,4,112]{0,2,1:T(8,128)(2,1)}), bf16[512,4,112]{0,2,1:T(8,128)(2,1)S(1)}, u32[]{:S(2)}, u32[]{:S(2)}) async-start(bf16[512,4,112]{0,2,1:T(8,128)(2,1)} %get-tuple-element.1334), calls=%async_computation.2 | async-start | bytes 917504 | tf_op jit(solution)/shard_map/all_to_all | solution.py:262
  155.1 11.3 copy-start.22
  155.3 17.3 copy-start.46
  155.3 41.8 %collective-permute-start = (bf16[2048,224]{0,1:T(8,128)(2,1)S(1)}, bf16[2048,224]{0,1:T(8,128)(2,1)}, u32[]{:S(2)}, u32[]{:S(2)}) collective-permute-start(bf16[2048,224]{0,1:T(8,128)(2,1)S(1)} %constant_dynamic-update-slice_fusion.1), channel_id=1, source_target_pairs={{0,3},{1,4},{2,5},{3,6},{4,7},{8,11},{9,12},{10,13},{11,14},{12,15... | collective-permute-start | bytes 2752520 | tf_op jit(solution)/shard_map/ppermute | solution.py:22
  157.7 69.5 %collective-permute-start.1 = (bf16[2048,224]{0,1:T(8,128)(2,1)S(1)}, bf16[2048,224]{0,1:T(8,128)(2,1)}, u32[]{:S(2)}, u32[]{:S(2)}) collective-permute-start(bf16[2048,224]{0,1:T(8,128)(2,1)S(1)} %constant_dynamic-update-slice_fusion.1), channel_id=1, source_target_pairs={{0,2},{1,3},{2,4},{3,5},{4,6},{5,7},{8,10},{9,11},{10,12},{11,13},... | collective-permute-start | bytes 2752520 | tf_op jit(solution)/shard_map/ppermute | solution.py:22
  161.2 66.0 %collective-permute-start.2 = (bf16[2048,224]{0,1:T(8,128)(2,1)S(1)}, bf16[2048,224]{0,1:T(8,128)(2,1)}, u32[]{:S(2)}, u32[]{:S(2)}) collective-permute-start(bf16[2048,224]{0,1:T(8,128)(2,1)S(1)} %constant_dynamic-update-slice_fusion.1), channel_id=1, source_target_pairs={{0,1},{1,2},{2,3},{3,4},{4,5},{5,6},{6,7},{8,9},{9,10},{10,11},{11... | collective-permute-start | bytes 2752520 | tf_op jit(solution)/shard_map/ppermute | solution.py:22
  166.4 11.6 all-to-all-start
  169.9 377.4 %all-gather.13.cloned.1.call-start = ((), (), s32[]{:S(2)}) async-start(), calls=%async_computation.19 | async-start | bytes 9437184 | tf_op jit(solution)/shard_map/all_gather | solution.py:234
  295.1 235.0 %copy-start.3 = (bf16[6144,112]{1,0:T(8,128)(2,1)}, bf16[6144,112]{1,0:T(8,128)(2,1)S(1)}, u32[]{:S(2)}) copy-start(bf16[6144,112]{1,0:T(8,128)(2,1)S(1)} %get-tuple-element.2535) | copy-start | bytes 4128772
  295.1 235.0 %copy-start.4 = (bf16[6144,112]{1,0:T(8,128)(2,1)}, bf16[6144,112]{1,0:T(8,128)(2,1)S(1)}, u32[]{:S(2)}) copy-start(bf16[6144,112]{1,0:T(8,128)(2,1)S(1)} %get-tuple-element.2540) | copy-start | bytes 4128772
  295.2 196.3 %copy-start.55 = (bf16[128]{0:T(256)(128)(2,1)S(1)}, bf16[128]{0:T(256)(128)(2,1)}, u32[]{:S(2)}) copy-start(bf16[128]{0:T(256)(128)(2,1)} %param.38) | copy-start | bytes 772
  295.2 214.5 %copy-start.56 = (bf16[128]{0:T(256)(128)(2,1)S(1)}, bf16[128]{0:T(256)(128)(2,1)}, u32[]{:S(2)}) copy-start(bf16[128]{0:T(256)(128)(2,1)} %param.37) | copy-start | bytes 772
  295.2 231.0 %copy-start.47 = (f32[4,512]{1,0:T(4,128)S(1)}, f32[4,512]{1,0:T(4,128)}, u32[]{:S(2)}) copy-start(f32[4,512]{1,0:T(4,128)} %get-tuple-element.913) | copy-start | bytes 24580
  298.0 228.2 %all-to-all-start.3 = ((bf16[4,512,112]{1,2,0:T(8,128)(2,1)}), bf16[4,512,112]{1,2,0:T(8,128)(2,1)}, u32[]{:S(2)}, u32[]{:S(2)}) async-start(bf16[4,512,112]{1,2,0:T(8,128)(2,1)} %convert_element_type.212), calls=%async_computation.3 | async-start | bytes 917504 | tf_op jit(solution)/shard_map/all_to_all | solution.py:313
  509.6 27.0 %copy-start.53 = (f32[8,1,128]{2,1,0:T(1,128)}, f32[8,1,128]{2,1,0:T(1,128)S(1)}, u32[]{:S(2)}) copy-start(f32[8,1,128]{2,1,0:T(1,128)S(1)} %convert_element_type.264) | copy-start | bytes 12292
  526.2 39.8 %copy-start.43 = (f32[8,1,128]{2,1,0:T(1,128)}, f32[8,1,128]{2,1,0:T(1,128)S(1)}, u32[]{:S(2)}) copy-start(f32[8,1,128]{2,1,0:T(1,128)S(1)} %convert_element_type.263) | copy-start | bytes 12292
  536.2 29.8 %copy-start.11 = (f32[512,1024]{1,0:T(8,128)}, f32[512,1024]{1,0:T(8,128)S(1)}, u32[]{:S(2)}) copy-start(f32[512,1024]{1,0:T(8,128)S(1)} %get-tuple-element.1339) | copy-start | bytes 6291460
  536.2 29.8 %copy-start.41 = (f32[512]{0:T(512)}, f32[512]{0:T(512)S(1)}, u32[]{:S(2)}) copy-start(f32[512]{0:T(512)S(1)} %broadcast_multiply_fusion.2) | copy-start | bytes 6148
  536.5 29.5 %copy-start.48 = (f32[512]{0:T(512)}, f32[512]{0:T(512)S(1)}, u32[]{:S(2)}) copy-start(f32[512]{0:T(512)S(1)} %add_rsqrt_fusion) | copy-start | bytes 6148
  536.6 10.7 copy-start.27
  547.3 13.1 copy-start.57
  560.4 5.6 copy-start.59
  566.8 5.7 copy-start.9
  566.8 5.7 copy-start.14
  572.6 7.2 copy-start.6
  574.3 14.6 copy-start.19
  574.3 13.6 all-to-all-start.4
  579.8 520.6 %reduce-scatter.17.cloned.1.call-start = ((), (), s32[]{:S(2)}) async-start(), calls=%async_computation.24 | async-start | bytes 110592 | tf_op jit(solution)/shard_map/reduce_scatter | solution.py:446
  579.8 9.3 copy-start.35
  680.5 11.6 all-to-all-start.5
  684.0 417.1 %reduce-scatter.9.cloned.1.call-start = ((), (), s32[]{:S(2)}) async-start(), calls=%async_computation.20 | async-start | bytes 2064384 | tf_op jit(solution)/shard_map/reduce_scatter | solution.py:442
  685.7 9.7 copy-start.2
  692.1 5.1 copy-start.15
  695.4 407.3 %reduce-scatter.11.cloned.1.call-start = ((), (), s32[]{:S(2)}) async-start(), calls=%async_computation.21 | async-start | bytes 2064384 | tf_op jit(solution)/shard_map/reduce_scatter | solution.py:443
  697.1 251.0 %copy-start.8 = (f32[6144,224]{0,1:T(8,128)S(1)}, f32[6144,224]{0,1:T(8,128)}, u32[]{:S(2)}) copy-start(f32[6144,224]{0,1:T(8,128)} %constant_dynamic-update-slice_fusion.3) | copy-start | bytes 16515076
  700.1 248.1 %collective-permute-start.5 = (bf16[2048,224]{0,1:T(8,128)(2,1)S(1)}, bf16[2048,224]{0,1:T(8,128)(2,1)S(1)}, u32[]{:S(2)}, u32[]{:S(2)}) collective-permute-start(bf16[2048,224]{0,1:T(8,128)(2,1)S(1)} %get-tuple-element.1322), channel_id=1, source_target_pairs={{3,0},{4,1},{5,2},{6,3},{7,4},{11,8},{12,9},{13,10},{14,11},{15,12... | collective-permute-start | bytes 2752520 | tf_op jit(solution)/shard_map/ppermute | solution.py:22
  701.4 246.8 %collective-permute-start.4 = (bf16[2048,224]{0,1:T(8,128)(2,1)S(1)}, bf16[2048,224]{0,1:T(8,128)(2,1)S(1)}, u32[]{:S(2)}, u32[]{:S(2)}) collective-permute-start(bf16[2048,224]{0,1:T(8,128)(2,1)S(1)} %get-tuple-element.1323), channel_id=1, source_target_pairs={{2,0},{3,1},{4,2},{5,3},{6,4},{7,5},{10,8},{11,9},{12,10},{13,11},... | collective-permute-start | bytes 2752520 | tf_op jit(solution)/shard_map/ppermute | solution.py:22
  702.7 245.5 %collective-permute-start.3 = (bf16[2048,224]{0,1:T(8,128)(2,1)S(1)}, bf16[2048,224]{0,1:T(8,128)(2,1)S(1)}, u32[]{:S(2)}, u32[]{:S(2)}) collective-permute-start(bf16[2048,224]{0,1:T(8,128)(2,1)S(1)} %get-tuple-element.1321), channel_id=1, source_target_pairs={{1,0},{2,1},{3,2},{4,3},{5,4},{6,5},{7,6},{9,8},{10,9},{11,10},{12... | collective-permute-start | bytes 2752520 | tf_op jit(solution)/shard_map/ppermute | solution.py:22
  949.1 12.2 copy-start.7
  963.1 282.2 %reduce-scatter.19.cloned.1.call-start = ((), (), s32[]{:S(2)}) async-start(), calls=%async_computation.25 | async-start | bytes 10321920 | tf_op jit(solution)/shard_map/reduce_scatter | solution.py:447
  971.0 11.9 copy-start.34
  971.0 437.7 %reduce-scatter.13.cloned.1.call-start = ((), (), s32[]{:S(2)}) async-start(), calls=%async_computation.22 | async-start | bytes 10321920 | tf_op jit(solution)/shard_map/reduce_scatter | solution.py:444
  993.7 700.1 %reduce-scatter.21.cloned.1.call-start = ((), (), s32[]{:S(2)}) async-start(), calls=%async_computation.26 | async-start | bytes 18874368 | tf_op jit(solution)/shard_map/reduce_scatter | solution.py:450
  1007.7 971.7 %reduce-scatter.23.cloned.1.call-start = ((), (), s32[]{:S(2)}) async-start(), calls=%async_computation.27 | async-start | bytes 18874368 | tf_op jit(solution)/shard_map/reduce_scatter | solution.py:451
  1023.3 1016.3 %reduce-scatter.15.cloned.1.call-start = ((), (), s32[]{:S(2)}) async-start(), calls=%async_computation.23 | async-start | bytes 110592 | tf_op jit(solution)/shard_map/reduce_scatter | solution.py:445
  1084.7 12.5 copy-start.37
  1084.7 12.6 copy-start.40
  1084.7 13.9 copy-start.32
  1084.7 13.9 copy-start.36
  1098.2 1019.0 %all-reduce.8.cloned.1.call-start = ((), (), s32[]{:S(2)}) async-start(), calls=%async_computation.28 | async-start | bytes 6946816 | tf_op jit(solution)/shard_map/psum | solution.py:454
  1696.4 285.7 %copy-start.16 = (bf16[4,512,112]{1,2,0:T(8,128)(2,1)S(1)}, bf16[4,512,112]{1,2,0:T(8,128)(2,1)}, u32[]{:S(2)}) copy-start(bf16[4,512,112]{1,2,0:T(8,128)(2,1)} %copy-done.15) | copy-start | bytes 1376260
  2117.3 5.5 copy-start.28
  2117.3 6.6 copy-start.26
  (21 other events, 40.9 us)
Sparse Core Ops, SparseCore 0:
  10.1 92.7 all-gather.6
  105.0 114.9 all-gather.8
  222.2 159.5 all-gather.10
  383.7 124.0 all-gather.12
  584.1 57.5 reduce-scatter.16
  695.5 317.7 reduce-scatter.8
  1017.2 65.6 reduce-scatter.10
  1086.6 158.6 reduce-scatter.18
  1249.4 159.2 reduce-scatter.12
  1412.3 281.3 reduce-scatter.20
  1698.0 281.3 reduce-scatter.22
  1982.5 57.0 reduce-scatter.14
  2043.5 73.7 all-reduce.7
where the time goes:
time: 2150 us; the launch traced here: 2130 us
  waiting for transfers between devices  1310 us (61%)
  blocking collectives  420 us (20%)
  matrix products  213 us (10%)
  other arithmetic  69.8 us (3%)
  local copies, waits for them, and re-layouts  55 us (3%)
  starting transfers between devices  38.2 us (2%)
    ppermute x6, waiting for transfers between devices, shifted(): lax.ppermute(value, axis, [(source, source + steps) for source in range(i...  292 us
    reduce_scatter x1, waiting for transfers between devices, on_device(): lax.psum_scatter(grad_outer_w, 'fsdp', scatter_dimension=0, tiled=True)  283 us
    reduce_scatter x1, waiting for transfers between devices, on_device(): lax.psum_scatter(grad_inner_w, 'fsdp', scatter_dimension=0, tiled=True)  283 us
    all_gather x1, blocking collectives, on_device(): lax.all_gather(output_router, 'fsdp', axis=0, tiled=True)  187 us
    reduce_scatter x1, waiting for transfers between devices, on_device(): lax.psum_scatter(grad_value_w, 'fsdp', scatter_dimension=0, tiled=True)  161 us
    reduce_scatter x1, waiting for transfers between devices, on_device(): lax.psum_scatter(grad_output_w, 'fsdp', scatter_dimension=0, tiled=True)  141 us
    psum x1, waiting for transfers between devices, on_device(): lax.psum(reduced[0].astype(jnp.bfloat16), 'seq').astype(jnp.float32)  64.6 us
    unnamed x1, blocking collectives  59.4 us
  transfers between devices with their start and end apart: 25, of which 13 were waited for; matrix products, arithmetic and copies ran while one was open for 14% of the time, Pallas kernels for 0%

commit v1 on v0

v1 whole, which is shorter than its diff:
```python
import functools
import jax
import jax.numpy as jnp
from jax import lax
from jax.experimental import pallas as pl
from jax.experimental.pallas import tpu as pltpu
from jax.sharding import PartitionSpec as P

HEADS = 4
DH = 112
EXP = 5
CONT = 1024
GSLOTS = 4
PSLOTS = 2
BLOCK = 512
LANES = 128
EPSILON = 1e-05
NEGATIVE = -1e30
LOG2E = 1.4426950408889634
MESH = pl.DeviceIdType.MESH
ANY = pl.BlockSpec(memory_space=pl.ANY)
VMEM = pl.BlockSpec(memory_space=pltpu.VMEM)
SMEM = pl.BlockSpec(memory_space=pltpu.SMEM)
DMA = pltpu.SemaphoreType.DMA

QCOLS = HEADS * DH
VCOLS = HEADS * EXP * DH
ROUTERS = 2 * QCOLS + VCOLS
NORM = ROUTERS + 2 * HEADS * EXP
JOINT = 3328
SPLITS = {"joint": (640, 512), "output": (0, 256), "inner": (768, 640), "outer": (256, 128)}


def ring_place(index, count):
    return (index // 2) * (1 - index % 2) + (count - 1 - index // 2) * (index % 2)


def ring_index(place, count):
    upper = place // (count // 2)
    return 2 * place * (1 - upper) + (2 * (count - 1 - place) + 1) * upper


def enter(devices):
    barrier = pltpu.get_barrier_semaphore()
    for device in devices:
        pl.semaphore_signal(barrier, inc=1, device_id=device, device_id_type=MESH)
    pl.semaphore_wait(barrier, len(devices))


class Ring:
    def __init__(self, count, splits):
        self.count, self.splits = count, splits
        self.seq, self.fsdp = lax.axis_index("seq"), lax.axis_index("fsdp")
        self.plane, self.core = self.seq // 2, self.seq % 2
        self.place = ring_place(self.fsdp, count)
        self.right = (self.seq, ring_index((self.place + 1) % count, count))
        self.left = (self.seq, ring_index((self.place + count - 1) % count, count))
        self.core_mate = (self.seq + 1 - 2 * self.core, self.fsdp)
        self.plane_mate = ((self.seq + 2) % 4, self.fsdp)
        self.far = count // 2

    def neighbours(self):
        return [self.right, self.left, self.core_mate, self.plane_mate]

    def reach(self, kind, way):
        return self.far if kind == way else self.count - 1 - self.far

    def kinds(self, t):
        return [kind for kind in (1, 0) if self.splits[t][kind] > 0]

    def half(self, t):
        return self.splits[t][0] + 2 * self.splits[t][1]

    def cols(self, t, kind, plane, core):
        both, single = self.splits[t]
        if kind == 0:
            return pl.ds(pl.multiple_of(core * self.half(t), LANES), both)
        return pl.ds(pl.multiple_of(core * self.half(t) + both + plane * single, LANES), single)

    def behind(self, way, k):
        step = self.count - k if way == 0 else k
        return ring_index((self.place + step) % self.count, self.count)

    def next(self, way):
        return self.right if way == 0 else self.left

    def slot(self, kind, way, k):
        return k - 1 if way == 0 else self.reach(kind, 0) + k - 1


class Gather(Ring):
    def __init__(self, count, splits, shards, at, send, recv, local):
        super().__init__(count, splits)
        self.shards, self.at, self.send, self.recv, self.local = shards, at, send, recv, local

    @staticmethod
    def sems(count, tensors):
        return [DMA((6 * tensors * (count - 1),)), DMA((6 * tensors * (count - 1),)), DMA((tensors,))]

    def copy(self, src, dst, group, t, slot, device):
        i = (group * len(self.splits) + t) * (self.count - 1) + slot
        return pltpu.make_async_remote_copy(
            src, dst, self.send.at[i], self.recv.at[i], device_id=device, device_id_type=MESH
        )

    def same(self, group, t, kind, way, k, plane, core, device):
        ref = self.at(t, self.behind(way, k), self.cols(t, kind, plane, core))
        return self.copy(ref, ref, group, t, self.slot(kind, way, k), device)

    def hop(self, t, kind, way, k):
        if k > 1:
            ref = self.at(t, self.behind(way, k - 1), self.cols(t, kind, self.plane, self.core))
            return self.copy(ref, ref, kind, t, self.slot(kind, way, k), self.next(way))
        cols = self.cols(t, kind, self.plane, self.core)
        return self.copy(
            self.shards[t].at[:, cols], self.at(t, self.fsdp, cols), kind, t, self.slot(kind, way, 1), self.next(way)
        )

    def arrived(self, t, kind, way, k):
        return self.same(kind, t, kind, way, k, self.plane, self.core, self.next(way))

    def to_core(self, t, kind, way, k, core):
        return self.same(2 + kind, t, kind, way, k, self.plane, core, self.core_mate)

    def to_plane(self, t, way, k, plane):
        return self.same(4, t, 1, way, k, plane, self.core, self.plane_mate)

    def plane_to_core(self, t, way, k, core):
        return self.same(5, t, 1, way, k, 1 - self.plane, core, self.core_mate)

    def own(self, t):
        return pltpu.make_async_copy(self.shards[t], self.at(t, self.fsdp, slice(None)), self.local.at[t])

    def start(self, t):
        for kind in self.kinds(t):
            for way in (0, 1):
                if self.reach(kind, way):
                    self.hop(t, kind, way, 1).start()
        self.own(t).start()

    def arrive(self, t, k):
        for kind in self.kinds(t):
            for way in (0, 1):
                if k <= self.reach(kind, way):
                    self.arrived(t, kind, way, k).wait_recv()
                    if k < self.reach(kind, way):
                        self.hop(t, kind, way, k + 1).start()
                    if kind:
                        self.to_plane(t, way, k, self.plane).start()
                    self.to_core(t, kind, way, k, self.core).start()

    def plane_arrive(self, t, k):
        if 1 in self.kinds(t):
            for way in (0, 1):
                if k <= self.reach(1, way):
                    self.to_plane(t, way, k, 1 - self.plane).wait_recv()
                    self.plane_to_core(t, way, k, self.core).start()

    def finish(self, t):
        self.own(t).wait()
        for kind in self.kinds(t):
            for way in (0, 1):
                for k in range(1, self.reach(kind, way) + 1):
                    self.hop(t, kind, way, k).wait_send()
                    self.to_core(t, kind, way, k, self.core).wait_send()
                    self.to_core(t, kind, way, k, 1 - self.core).wait_recv()
                    if kind:
                        self.to_plane(t, way, k, self.plane).wait_send()
                        self.plane_to_core(t, way, k, self.core).wait_send()
                        self.plane_to_core(t, way, k, 1 - self.core).wait_recv()

    def events(self):
        tensors = range(len(self.splits))
        out = []
        for k in range(1, self.far + 1):
            for t in tensors:
                out.append(functools.partial(self.arrive, t, k))
                if k > 1:
                    out.append(functools.partial(self.plane_arrive, t, k - 1))
        for t in tensors:
            out.append(functools.partial(self.plane_arrive, t, self.far))
        for t in tensors:
            out.append(functools.partial(self.finish, t))
        return out


TABLE = 5632
TABLE_ZERO = 5120
TURNED_ZERO = 512


def route_lanes(routes, lane):
    hit = None
    for head in range(2 * HEADS):
        for choice in range(2):
            place = head * EXP + routes[:, 2 * head + choice : 2 * head + choice + 1]
            here = lane == place
            hit = here if hit is None else hit | here
    return hit.astype(jnp.float32)


def project_kernel(count, query, key, value, routers, tokens, routes, gaps, joint, qkv, experts, gates, norms, tables, turned_tables,
                   shard, product, send, recv, local):
    rows = shard.shape[0]
    splits = (SPLITS["joint"],)
    at = lambda t, g, cols: joint.at[pl.ds(pl.multiple_of(g * rows, rows), rows), cols]
    ring = Gather(count, splits, [shard], at, send, recv, local)
    wide = jnp.concatenate([ref[...].astype(jnp.float32) for ref in (query, key, value, routers)], axis=1)
    shard[...] = wide.astype(jnp.bfloat16)
    enter(ring.neighbours())
    ring.start(0)
    slope = jnp.float32(0.0)
    for head in range(HEADS):
        slope = jnp.where(ring.seq // 1 == head, -0.5 * 0.5**head * LOG2E, slope)
    group = ring.fsdp // GSLOTS
    pair = jnp.maximum(ring.fsdp % GSLOTS - PSLOTS, 0) * 2
    gap_values = [jnp.int32(0), gaps[group, pair], gaps[group, pair + 1]]

    def table_column(step, carry):
        start = pl.multiple_of(step * 256, 256)
        lanes = lax.broadcasted_iota(jnp.int32, (8, 256 + LANES), 1) + (start - LANES)
        for which in range(3):
            for turned in range(2):
                if turned:
                    distance = lanes - TURNED_ZERO + gap_values[which]
                else:
                    distance = TABLE_ZERO - lanes + gap_values[which]
                bias = slope * jnp.log(1.0 + jnp.maximum(distance, 0).astype(jnp.float32))
                bias = jnp.where(distance >= 0, bias, NEGATIVE)
                wide = jnp.broadcast_to(bias[:1], (LANES, 256 + LANES))
                rolled = pltpu.roll(wide, 0, 1, stride=1, stride_axis=0)
                target = turned_tables if turned else tables
                target[which, :, pl.ds(start, 256)] = rolled[:, LANES:]
        return carry

    events = ring.events()
    cut = max(1, (TABLE // 256) // max(1, ring.far))
    done = 0
    for i, event in enumerate(events):
        upto = min(TABLE // 256, (i + 1) * cut)
        if upto > done:
            lax.fori_loop(done, upto, table_column, 0)
            done = upto
        event()
    if done < TABLE // 256:
        lax.fori_loop(done, TABLE // 256, table_column, 0)

    def column(step, carry):
        cols = pl.ds(pl.multiple_of(step * 256, 256), 256)
        product[:, cols] = jnp.dot(tokens[...], joint[:, cols], preferred_element_type=jnp.float32)
        return carry

    lax.fori_loop(0, JOINT // 256, column, 0)
    norm_tile = NORM // LANES * LANES
    turned_norm = joint[:, norm_tile : norm_tile + LANES].astype(jnp.float32).T
    norms[...] = turned_norm[NORM - norm_tile : NORM - norm_tile + 8]
    logits = product[:, ROUTERS : ROUTERS + 2 * HEADS * EXP]
    local_rows = tokens.shape[0]
    wide = jnp.concatenate([logits, jnp.zeros((local_rows, LANES - 2 * HEADS * EXP), jnp.float32)], axis=1)
    lane = lax.broadcasted_iota(jnp.int32, (local_rows, LANES), 1)
    mask = route_lanes(routes[...], lane)
    gate = 1.0 / (1.0 + jnp.exp(-wide))
    gates[0] = gate * mask
    gates[1] = gate * mask * (1.0 - gate)
    pad = jnp.zeros((local_rows, LANES - DH), jnp.float32)
    ones = jnp.ones((local_rows, LANES - DH), jnp.float32)
    for head in range(HEADS):
        first = head * DH
        qkv[head, 0] = jnp.concatenate([product[:, first : first + DH], pad], axis=1).astype(jnp.bfloat16)
        first = QCOLS + head * DH
        qkv[head, 1] = jnp.concatenate([product[:, first : first + DH], pad], axis=1).astype(jnp.bfloat16)
        total = None
        for expert in range(EXP):
            which = head * EXP + expert
            first = 2 * QCOLS + which * DH
            piece = product[:, first : first + DH]
            experts[which] = jnp.concatenate([piece, pad], axis=1).astype(jnp.bfloat16)
            term = piece * gates[0, :, which : which + 1]
            total = term if total is None else total + term
        qkv[head, 2] = jnp.concatenate([total, ones], axis=1).astype(jnp.bfloat16)


def project(count, query, key, value, routers, tokens, routes, gaps):
    rows, (shard_rows, _) = tokens.shape[0], query.shape
    f32, bf = jnp.float32, jnp.bfloat16
    return pl.pallas_call(
        functools.partial(project_kernel, count),
        out_shape=[
            jax.ShapeDtypeStruct((shard_rows * count, JOINT), bf),
            jax.ShapeDtypeStruct((HEADS, 3, rows, LANES), bf),
            jax.ShapeDtypeStruct((HEADS * EXP, rows, LANES), bf),
            jax.ShapeDtypeStruct((2, rows, LANES), f32),
            jax.ShapeDtypeStruct((8, shard_rows * count), f32),
            jax.ShapeDtypeStruct((3, LANES, TABLE), f32),
            jax.ShapeDtypeStruct((3, LANES, TABLE), f32),
        ],
        in_specs=[VMEM] * 6 + [SMEM],
        out_specs=[VMEM] * 7,
        scratch_shapes=[pltpu.VMEM((shard_rows, JOINT), bf), pltpu.VMEM((rows, JOINT), f32)] + Gather.sems(count, 1),
        compiler_params=pltpu.CompilerParams(collective_id=1, has_side_effects=True, vmem_limit_bytes=56 << 20),
    )(query, key, value, routers, tokens, routes, gaps)


def seq_mates(ring):
    return [ring.core_mate, ring.plane_mate, (3 - ring.seq, ring.fsdp)]


def slot_mates(ring):
    f = ring.fsdp
    return [(ring.seq, f + 1 - 2 * (f % 2)), (ring.seq, f + 2 - 4 * ((f // 2) % 2))]


def tile_place(slot, seq, phase, key_block, query_block):
    cont = slot // PSLOTS
    own = 1 - jnp.minimum(phase, 1)
    piece = jnp.where(slot == 3, 2 - phase, phase - 1)
    source = jnp.where(phase == 0, 0, 1 + piece)
    first = cont * 2 * (query_block // 2)
    active = jnp.where(
        phase == 0,
        (key_block <= query_block) & (key_block >= first),
        jnp.where(phase == 1, slot >= 1, slot >= 2),
    )
    far_column = jnp.where(
        cont == 1,
        2048 * piece + BLOCK * key_block - BLOCK * (query_block % 2) - 4096,
        BLOCK * key_block - 2048 - BLOCK * query_block,
    )
    column = jnp.where(phase == 0, BLOCK * (key_block - query_block), far_column)
    table = jnp.where((phase > 0) & (cont == 1), 1 + query_block // 2, 0)
    return source, active, table, column


def block_rows(block):
    return pl.ds(pl.multiple_of(block * BLOCK, BLOCK), BLOCK)


def attend_kernel(count, splits, steps, qkv, tables, *refs):
    T = len(splits)
    shards, refs = refs[:T], refs[T:]
    att, store, outputs, logs = refs[:4]
    fulls, refs = refs[4 : 4 + T], refs[4 + T :]
    acc, top, att_low, kv_send, kv_recv, q_send, q_recv, sh_send, sh_recv, out_send, out_recv, here = refs[:12]
    at = lambda t, g, cols: fulls[t].at[g, :, cols]
    ring = Gather(count, splits, shards, at, *refs[12:])
    seq, slot = ring.seq, ring.fsdp % GSLOTS
    mates, (x_mate, z_mate) = seq_mates(ring), slot_mates(ring)
    enter(ring.neighbours() + mates[2:] + [x_mate, z_mate])

    def remote(src, dst, send, recv, device):
        return pltpu.make_async_remote_copy(src, dst, send, recv, device_id=device, device_id_type=MESH)

    mine = block_rows(seq)

    def kv_copy(mate):
        return remote(qkv.at[mate[0], pl.ds(1, 2)], store.at[pl.ds(1, 2), mine], kv_send.at[mate[0]], kv_recv.at[seq], mate)

    def q_copy(mate):
        return remote(qkv.at[mate[0], 0], store.at[0, mine], q_send.at[mate[0]], q_recv.at[seq], mate)

    for mate in mates[1:] + mates[:1]:
        kv_copy(mate).start()
    own_copy = pltpu.make_async_copy(qkv.at[seq], store.at[pl.ds(0, 3), mine], here.at[0])
    own_copy.start()
    for mate in mates[1:] + mates[:1]:
        q_copy(mate).start()
    acc[...] = jnp.zeros_like(acc)
    top[...] = jnp.full_like(top, NEGATIVE)

    def far_rows(piece, chunk):
        return store.at[pl.ds(3 + 2 * piece, 2), block_rows(chunk)]

    def first_hop(chunk, way):
        src = store.at[pl.ds(1, 2), block_rows(chunk)]
        piece = slot % 2
        return remote(src, far_rows(piece, chunk), sh_send.at[4 * way + chunk], sh_recv.at[4 * piece + chunk],
                      x_mate if way == 0 else z_mate)

    def second_hop(chunk):
        piece = slot % 2
        return remote(far_rows(piece, chunk), far_rows(piece, chunk), sh_send.at[8 + chunk], sh_recv.at[4 * piece + chunk], x_mate)

    def share(chunk):
        @pl.when(slot < 2)
        def _():
            first_hop(chunk, 1).start()

        @pl.when(slot == 0)
        def _():
            first_hop(chunk, 0).start()

    def pass_on(chunk):
        @pl.when(slot >= 1)
        def _():
            piece = jnp.where(slot == 3, 1, 0)
            remote(far_rows(piece, chunk), far_rows(piece, chunk), sh_send.at[chunk], sh_recv.at[4 * piece + chunk], x_mate).wait_recv()

        @pl.when(slot >= 2)
        def _():
            second_hop(chunk).start()

    def last_piece(chunk):
        @pl.when(slot >= 2)
        def _():
            piece = 3 - slot
            remote(far_rows(piece, chunk), far_rows(piece, chunk), sh_send.at[chunk], sh_recv.at[4 * piece + chunk], x_mate).wait_recv()

    own_copy.wait()
    share(seq)
    for mate in mates:
        other = mate[0]
        src = store.at[pl.ds(1, 2), block_rows(other)]
        remote(src, src, kv_send.at[other], kv_recv.at[other], mate).wait_recv()
        share(other)
    for mate in mates:
        src = store.at[0, block_rows(mate[0])]
        remote(src, src, q_send.at[mate[0]], q_recv.at[mate[0]], mate).wait_recv()

    def tile(step):
        phase, key_block, query_block = step // 16, (step // 4) % 4, step % 4
        source, active, table, column = tile_place(slot, seq, phase, key_block, query_block)

        @pl.when(active)
        def _():
            rows = block_rows(query_block)
            keys = store[1 + 2 * source, block_rows(key_block), :]
            values = store[2 + 2 * source, block_rows(key_block), :]
            scores = lax.dot_general(store[0, rows, :], keys, (((1,), (1,)), ((), ())), preferred_element_type=jnp.float32)
            bias = jnp.concatenate(
                [tables[table, :, pl.ds(pl.multiple_of(column + TABLE_ZERO - LANES * part, LANES), BLOCK)] for part in range(BLOCK // LANES)],
                axis=0,
            )
            scores = scores * (DH**-0.5 * LOG2E) + bias
            before = top[rows, :]
            after = jnp.maximum(before, jnp.max(scores, axis=1, keepdims=True))
            factor = jnp.exp2(before - after)
            terms = jnp.exp2(scores - after[:, :1])
            acc[rows, :] = acc[rows, :] * factor + jnp.dot(terms.astype(jnp.bfloat16), values, preferred_element_type=jnp.float32)
            top[rows, :] = after

    events = {}
    for chunk in range(4):
        events.setdefault(4 * chunk, []).append(functools.partial(pass_on, chunk))
        events.setdefault(32 + 4 * chunk, []).append(functools.partial(last_piece, chunk))
    begin, gap = steps
    events.setdefault(begin, []).extend([functools.partial(ring.start, t) for t in range(T)])
    rest = []
    for i, event in enumerate(ring.events()):
        step = begin + gap * (i + 1)
        if step < 48:
            events.setdefault(step, []).append(event)
        else:
            rest.append(event)

    def step_body(step, carry):
        for when, actions in sorted(events.items()):
            @pl.when(step == when)
            def _():
                for action in actions:
                    action()
        tile(step)
        return carry

    lax.fori_loop(0, 48, step_body, 0)
    total = acc[:, DH : DH + 1]
    result = acc[...] / total
    outputs[...] = result
    log_total = top[...] + jnp.log2(total)
    for block in range(4):
        logs[:, block * BLOCK : (block + 1) * BLOCK] = log_total[block * BLOCK : (block + 1) * BLOCK].T[:8]
    att_low[...] = result.astype(jnp.bfloat16)

    def out_copy(mate):
        return remote(att_low.at[block_rows(mate[0])], att.at[seq], out_send.at[mate[0]], out_recv.at[seq], mate)

    for mate in mates[1:] + mates[:1]:
        out_copy(mate).start()
    own_out = pltpu.make_async_copy(att_low.at[mine], att.at[seq], here.at[1])
    own_out.start()
    for event in rest:
        event()
    own_out.wait()
    for mate in mates:
        kv_copy(mate).wait_send()
        q_copy(mate).wait_send()
        out_copy(mate).wait_send()
        ref = att.at[mate[0]]
        remote(ref, ref, out_send.at[mate[0]], out_recv.at[mate[0]], mate).wait_recv()
    for chunk in range(4):
        @pl.when(slot < 2)
        def _():
            first_hop(chunk, 1).wait_send()

        @pl.when(slot == 0)
        def _():
            first_hop(chunk, 0).wait_send()

        @pl.when(slot >= 2)
        def _():
            second_hop(chunk).wait_send()


def attend(count, qkv, tables, shards, splits, steps=(8, 2)):
    rows = qkv.shape[2]
    own = 4 * rows
    T = len(shards)
    return pl.pallas_call(
        functools.partial(attend_kernel, count, splits, steps),
        out_shape=[
            jax.ShapeDtypeStruct((HEADS, rows, LANES), jnp.bfloat16),
            jax.ShapeDtypeStruct((7, own, LANES), jnp.bfloat16),
            jax.ShapeDtypeStruct((own, LANES), jnp.float32),
            jax.ShapeDtypeStruct((8, own), jnp.float32),
        ]
        + [jax.ShapeDtypeStruct((count,) + w.shape, w.dtype) for w in shards],
        in_specs=[VMEM, VMEM] + [ANY] * T,
        out_specs=[VMEM] * 4 + [ANY] * T,
        scratch_shapes=[
            pltpu.VMEM((own, LANES), jnp.float32),
            pltpu.VMEM((own, LANES), jnp.float32),
            pltpu.VMEM((own, LANES), jnp.bfloat16),
            DMA((4,)), DMA((4,)), DMA((4,)), DMA((4,)), DMA((12,)), DMA((8,)), DMA((4,)), DMA((4,)), DMA((2,)),
        ]
        + Gather.sems(count, T),
        compiler_params=pltpu.CompilerParams(collective_id=2, has_side_effects=True, vmem_limit_bytes=56 << 20),
    )(qkv, tables, *shards)


class Scatter(Ring):
    def __init__(self, count, splits, parts, outs, bufs, sems):
        super().__init__(count, splits)
        self.parts, self.outs = parts, outs
        T = len(splits)
        self.mine, self.plane_in = bufs[:T], bufs[T : 2 * T]
        self.ring0, self.ring1 = bufs[2 * T : 3 * T], bufs[3 * T : 4 * T]
        self.low, self.low_in, self.done = bufs[4 * T : 5 * T], bufs[5 * T : 6 * T], bufs[6 * T : 7 * T]
        (self.load, self.plane_s, self.plane_r, self.ring_s, self.ring_r, self.end_s, self.end_r, self.put) = sems

    @staticmethod
    def scratch(count, splits, rows):
        half = [a + 2 * b for a, b in splits]
        bf = jnp.bfloat16
        out = [pltpu.VMEM((count, r, h), bf) for r, h in zip(rows, half)]
        out += [pltpu.VMEM((count, r, b), bf) for r, (a, b) in zip(rows, splits)]
        out += [pltpu.VMEM((count - 1 if a else 1, r, max(a, LANES)), bf) for r, (a, b) in zip(rows, splits)]
        out += [pltpu.VMEM((count - 1, r, b), bf) for r, (a, b) in zip(rows, splits)]
        out += [pltpu.VMEM((r, a + b), bf) for r, (a, b) in zip(rows, splits)]
        out += [pltpu.VMEM((r, a + b), bf) for r, (a, b) in zip(rows, splits)]
        out += [pltpu.VMEM((r, h), jnp.float32) for r, h in zip(rows, half)]
        T = len(splits)
        return out + [DMA((T * count,))] * 3 + [DMA((2 * T * (count - 1),))] * 2 + [DMA((2 * T,))] * 2 + [DMA((T,))]

    def dest(self, rel):
        return ring_index((self.place + rel) % self.count, self.count)

    def load_copy(self, t, rel):
        return pltpu.make_async_copy(self.parts[t].at[self.dest(rel)], self.mine[t].at[rel], self.load.at[t * self.count + rel])

    def remote(self, src, dst, s, r, i, device):
        return pltpu.make_async_remote_copy(src, dst, s.at[i], r.at[i], device_id=device, device_id_type=MESH)

    def single(self, t, plane):
        both, single = self.splits[t]
        return pl.ds(pl.multiple_of(both + plane * single, LANES), single)

    def plane_copy(self, t, rel):
        src = self.mine[t].at[rel, :, self.single(t, 1 - self.plane)]
        return self.remote(src, self.plane_in[t].at[rel], self.plane_s, self.plane_r, t * self.count + rel, self.plane_mate)

    def rels(self, D):
        return sorted({D % self.count, (-D) % self.count})

    def order(self):
        out = []
        for D in range(self.far, -1, -1):
            out += self.rels(D)
        return out

    def start(self, t):
        for rel in self.order():
            self.load_copy(t, rel).start()

    def prepare(self, t, D):
        for rel in self.rels(D):
            if self.parts:
                self.load_copy(t, rel).wait()
            self.plane_copy(t, rel).start()

    def buffer(self, t, kind, slot):
        if kind:
            return self.ring1[t].at[slot]
        return self.ring0[t].at[slot]

    def own_ref(self, t, kind, rel):
        if kind:
            return self.mine[t].at[rel, :, self.single(t, self.plane)]
        return self.mine[t].at[rel, :, pl.ds(0, self.splits[t][0])]

    def ring_copy(self, t, kind, way, D):
        slot = self.slot(kind, way, D)
        if D == self.reach(kind, way):
            src = self.own_ref(t, kind, D % self.count if way == 0 else (-D) % self.count)
        else:
            src = self.buffer(t, kind, self.slot(kind, way, D + 1))
        i = (2 * t + kind) * (self.count - 1) + slot
        return self.remote(src, self.buffer(t, kind, slot), self.ring_s, self.ring_r, i, self.next(way))

    def ring_wait(self, t, kind, way, D):
        slot = self.slot(kind, way, D)
        ref = self.buffer(t, kind, slot)
        i = (2 * t + kind) * (self.count - 1) + slot
        self.remote(ref, ref, self.ring_s, self.ring_r, i, self.next(way)).wait_recv()

    def combine(self, t, D):
        for rel in self.rels(D):
            self.plane_copy(t, rel).wait_send()
            ref = self.plane_in[t].at[rel]
            self.remote(ref, ref, self.plane_s, self.plane_r, t * self.count + rel, self.plane_mate).wait_recv()
            own = self.own_ref(t, 1, rel)
            own[...] = (own[...].astype(jnp.float32) + self.plane_in[t][rel].astype(jnp.float32)).astype(jnp.bfloat16)

    def chain(self, t, D):
        for kind in self.kinds(t):
            for way in (0, 1):
                if D > self.reach(kind, way):
                    continue
                if D < self.reach(kind, way):
                    self.ring_wait(t, kind, way, D + 1)
                    rel = D % self.count if way == 0 else (-D) % self.count
                    ref = self.buffer(t, kind, self.slot(kind, way, D + 1))
                    ref[...] = (ref[...].astype(jnp.float32) + self.own_ref(t, kind, rel)[...].astype(jnp.float32)).astype(jnp.bfloat16)
                self.ring_copy(t, kind, way, D).start()

    def end_copy(self, t):
        return self.remote(self.low[t], self.low_in[t], self.end_s, self.end_r, 2 * t, self.plane_mate)

    def close(self, t):
        both, single = self.splits[t]
        for kind in self.kinds(t):
            total = self.own_ref(t, kind, 0)[...].astype(jnp.float32)
            for way in (0, 1):
                if self.reach(kind, way):
                    self.ring_wait(t, kind, way, 1)
                    total = total + self.buffer(t, kind, self.slot(kind, way, 1))[...].astype(jnp.float32)
            if kind:
                self.low[t][:, both:] = total.astype(jnp.bfloat16)
            else:
                self.low[t][:, :both] = total.astype(jnp.bfloat16)
        self.end_copy(t).start()

    def out_ref(self, t, core):
        half = self.half(t)
        return self.outs[t].at[:, pl.ds(pl.multiple_of(core * half, LANES), half)]

    def out_copy(self, t):
        return self.remote(self.done[t], self.out_ref(t, self.core), self.end_s, self.end_r, 2 * t + 1, self.core_mate)

    def put_copy(self, t):
        return pltpu.make_async_copy(self.done[t], self.out_ref(t, self.core), self.put.at[t])

    def deliver(self, t):
        both, single = self.splits[t]
        self.end_copy(t).wait_send()
        ref = self.low_in[t]
        self.remote(ref, ref, self.end_s, self.end_r, 2 * t, self.plane_mate).wait_recv()
        if both:
            self.done[t][:, :both] = self.low[t][:, :both].astype(jnp.float32) + self.low_in[t][:, :both].astype(jnp.float32)
        if single:
            self.done[t][:, self.single(t, self.plane)] = self.low[t][:, both:].astype(jnp.float32)
            self.done[t][:, self.single(t, 1 - self.plane)] = self.low_in[t][:, both:].astype(jnp.float32)
        self.out_copy(t).start()
        self.put_copy(t).start()

    def finish(self, t):
        for kind in self.kinds(t):
            for way in (0, 1):
                for D in range(1, self.reach(kind, way) + 1):
                    self.ring_copy(t, kind, way, D).wait_send()
        self.out_copy(t).wait_send()
        self.put_copy(t).wait()
        ref = self.out_ref(t, 1 - self.core)
        self.remote(ref, ref, self.end_s, self.end_r, 2 * t + 1, self.core_mate).wait_recv()

    def events(self):
        tensors = range(len(self.splits))
        part = functools.partial
        out = [part(self.prepare, t, self.far) for t in tensors]
        for D in range(self.far, 0, -1):
            for t in tensors:
                out.append(part(self.prepare, t, D - 1))
            for t in tensors:
                out.append(part(self.combine, t, D))
                out.append(part(self.chain, t, D))
        for t in tensors:
            out.append(part(self.combine, t, 0))
            out.append(part(self.close, t))
        for t in tensors:
            out.append(part(self.deliver, t))
        for t in tensors:
            out.append(part(self.finish, t))
        return out


def retreat_kernel(count, splits, steps, grad_att, turned, store, outputs, logs, *refs):
    T = len(splits)
    parts, refs = refs[:T], refs[T:]
    back, outs, refs = refs[0], refs[1 : 1 + T], refs[1 + T :]
    (grads, delta, grad_q, grad_kv, send_kv, kv_in0, kv_in1, low, in_send, in_recv, up_send, up_recv,
     out_send, out_recv, here) = refs[:15]
    refs = refs[15:]
    ring = Scatter(count, splits, parts, outs, refs[: 7 * T], refs[7 * T :]) if T else Ring(count, splits)
    seq, slot = ring.seq, ring.fsdp % GSLOTS
    mates, (x_mate, z_mate) = seq_mates(ring), slot_mates(ring)
    enter(ring.neighbours() + mates[2:] + [x_mate, z_mate])

    def remote(src, dst, send, recv, device):
        return pltpu.make_async_remote_copy(src, dst, send, recv, device_id=device, device_id_type=MESH)

    mine = block_rows(seq)

    def in_copy(mate):
        return remote(grad_att.at[mate[0]], grads.at[mine], in_send.at[mate[0]], in_recv.at[seq], mate)

    for mate in mates[1:] + mates[:1]:
        in_copy(mate).start()
    own_copy = pltpu.make_async_copy(grad_att.at[seq], grads.at[mine], here.at[0])
    own_copy.start()
    grad_q[...] = jnp.zeros_like(grad_q)
    grad_kv[...] = jnp.zeros_like(grad_kv)
    own_copy.wait()
    for mate in mates:
        ref = grads.at[block_rows(mate[0])]
        remote(ref, ref, in_send.at[mate[0]], in_recv.at[mate[0]], mate).wait_recv()
    for block in range(4):
        rows = pl.ds(block * BLOCK, BLOCK)
        sums = jnp.sum(grads[rows, :].astype(jnp.float32) * outputs[rows, :], axis=1, keepdims=True)
        delta[:, rows] = jnp.broadcast_to(sums, (BLOCK, LANES)).T[:8]

    def tile(step):
        phase, key_block, query_block = step // 16, (step // 4) % 4, step % 4
        piece = jnp.where(slot == 2, 1 - phase, phase)
        forward_phase = jnp.where(phase == 2, 0, jnp.where(slot == 3, 2 - piece, 1 + piece))
        source, active, table, column = tile_place(slot, seq, forward_phase, key_block, query_block)

        @pl.when(active)
        def _():
            rows, key_rows = block_rows(query_block), block_rows(key_block)
            keys, values = store[1 + 2 * source, key_rows, :], store[2 + 2 * source, key_rows, :]
            queries, tops = store[0, rows, :], grads[rows, :]
            scores = lax.dot_general(keys, queries, (((1,), (1,)), ((), ())), preferred_element_type=jnp.float32)
            bias = jnp.concatenate(
                [turned[table, :, pl.ds(pl.multiple_of(TURNED_ZERO - column - LANES * part, LANES), BLOCK)] for part in range(BLOCK // LANES)],
                axis=0,
            )
            weights = jnp.exp2(scores * (DH**-0.5 * LOG2E) + (bias - logs[:1, rows]))
            grad_weights = lax.dot_general(values, tops, (((1,), (1,)), ((), ())), preferred_element_type=jnp.float32)
            grad_scores = (weights * (grad_weights - delta[:1, rows])).astype(jnp.bfloat16)
            grad_kv[source, 1, key_rows, :] += jnp.dot(weights.astype(jnp.bfloat16), tops, preferred_element_type=jnp.float32)
            grad_kv[source, 0, key_rows, :] += jnp.dot(grad_scores, queries, preferred_element_type=jnp.float32)
            grad_q[rows, :] += lax.dot_general(grad_scores, keys, (((0,), (0,)), ((), ())), preferred_element_type=jnp.float32)

    scale = DH**-0.5

    def rounded(source, chunk, extra):
        rows = block_rows(chunk)
        keys = grad_kv[source, 0, rows, :] * scale
        values = grad_kv[source, 1, rows, :]
        for more in extra:
            keys = keys + more[0].astype(jnp.float32)
            values = values + more[1].astype(jnp.float32)
        return keys.astype(jnp.bfloat16), values.astype(jnp.bfloat16)

    def x_send(chunk):
        src = send_kv.at[0, :, block_rows(chunk)]
        return remote(src, kv_in0.at[:, block_rows(chunk)], up_send.at[chunk], up_recv.at[chunk], x_mate)

    def z_send(chunk):
        src = send_kv.at[1, :, block_rows(chunk)]
        return remote(src, kv_in1.at[:, block_rows(chunk)], up_send.at[4 + chunk], up_recv.at[4 + chunk], z_mate)

    def x_wait(chunk):
        ref = kv_in0.at[:, block_rows(chunk)]
        remote(ref, ref, up_send.at[chunk], up_recv.at[chunk], x_mate).wait_recv()

    def z_wait(chunk):
        ref = kv_in1.at[:, block_rows(chunk)]
        remote(ref, ref, up_send.at[4 + chunk], up_recv.at[4 + chunk], z_mate).wait_recv()

    def first_done(chunk):
        @pl.when(slot >= 1)
        def _():
            source = jnp.where(slot == 2, 2, 1)
            keys, values = rounded(source, chunk, [])
            send_kv[0, 0, block_rows(chunk), :] = keys
            send_kv[0, 1, block_rows(chunk), :] = values
            x_send(chunk).start()

    def second_done(chunk):
        @pl.when(slot >= 2)
        def _():
            x_wait(chunk)
            source = slot - 1
            keys, values = rounded(source, chunk, [kv_in0[:, block_rows(chunk), :]])
            send_kv[1, 0, block_rows(chunk), :] = keys
            send_kv[1, 1, block_rows(chunk), :] = values
            z_send(chunk).start()

    def out_copy(mate):
        src = low.at[:, block_rows(mate[0])]
        return remote(src, back.at[seq], out_send.at[mate[0]], out_recv.at[seq], mate)

    def own_done(chunk):
        rows = block_rows(chunk)
        low[0, rows, :] = (grad_q[rows, :] * scale).astype(jnp.bfloat16)

        @pl.when(slot == 0)
        def _():
            x_wait(chunk)
            z_wait(chunk)
            low[1, rows, :], low[2, rows, :] = rounded(0, chunk, [kv_in0[:, rows, :], kv_in1[:, rows, :]])

        @pl.when(slot == 1)
        def _():
            z_wait(chunk)
            low[1, rows, :], low[2, rows, :] = rounded(0, chunk, [kv_in1[:, rows, :]])

        @pl.when(slot >= 2)
        def _():
            low[1, rows, :], low[2, rows, :] = rounded(0, chunk, [])

    events = {}
    for chunk in range(4):
        events.setdefault(4 * chunk + 4, []).append(functools.partial(first_done, chunk))
        events.setdefault(20 + 4 * chunk, []).append(functools.partial(second_done, chunk))
    rest = []
    if T:
        begin, gap = steps
        events.setdefault(begin, []).extend([functools.partial(ring.start, t) for t in range(T)])
        for i, event in enumerate(ring.events()):
            step = begin + int(gap * (i + 1))
            if step < 48:
                events.setdefault(step, []).append(event)
            else:
                rest.append(event)

    def step_body(step, carry):
        for when, actions in sorted(events.items()):
            @pl.when(step == when)
            def _():
                for action in actions:
                    action()
        tile(step)
        return carry

    lax.fori_loop(0, 48, step_body, 0)
    for chunk in range(4):
        own_done(chunk)
    for mate in mates[1:] + mates[:1]:
        out_copy(mate).start()
    own_out = pltpu.make_async_copy(low.at[:, mine], back.at[seq], here.at[1])
    own_out.start()
    for event in rest:
        event()
    own_out.wait()
    for mate in mates:
        in_copy(mate).wait_send()
        out_copy(mate).wait_send()
        ref = back.at[mate[0]]
        remote(ref, ref, out_send.at[mate[0]], out_recv.at[mate[0]], mate).wait_recv()
    for chunk in range(4):
        @pl.when(slot >= 1)
        def _():
            x_send(chunk).wait_send()

        @pl.when(slot >= 2)
        def _():
            z_send(chunk).wait_send()


def retreat(count, grad_att, turned, store, outputs, logs, parts, splits, steps=(0, 1)):
    rows = grad_att.shape[1]
    own = 4 * rows
    T = len(parts)
    shard_rows = [p.shape[1] for p in parts]
    return pl.pallas_call(
        functools.partial(retreat_kernel, count, splits, steps),
        out_shape=[jax.ShapeDtypeStruct((HEADS, 3, rows, LANES), jnp.bfloat16)]
        + [jax.ShapeDtypeStruct((p.shape[1], 2 * p.shape[2]), jnp.float32) for p in parts],
        in_specs=[VMEM] * 5 + [ANY] * T,
        out_specs=[VMEM] + [ANY] * T,
        scratch_shapes=[
            pltpu.VMEM((own, LANES), jnp.bfloat16),
            pltpu.VMEM((8, own), jnp.float32),
            pltpu.VMEM((own, LANES), jnp.float32),
            pltpu.VMEM((3, 2, own, LANES), jnp.float32),
            pltpu.VMEM((2, 2, own, LANES), jnp.bfloat16),
            pltpu.VMEM((2, own, LANES), jnp.bfloat16),
            pltpu.VMEM((2, own, LANES), jnp.bfloat16),
            pltpu.VMEM((3, own, LANES), jnp.bfloat16),
            DMA((4,)), DMA((4,)), DMA((8,)), DMA((8,)), DMA((4,)), DMA((4,)), DMA((2,)),
        ]
        + (Scatter.scratch(count, splits, shard_rows) if T else []),
        compiler_params=pltpu.CompilerParams(collective_id=3, has_side_effects=True, vmem_limit_bytes=63 << 20),
    )(grad_att, turned, store, outputs, logs, *parts)


CHUNK = 512


def gelu_pair(v):
    root = 0.7978845608028654
    square = v * v
    t = jnp.tanh(root * (v + 0.044715 * square * v))
    up = 0.5 * (1.0 + t)
    return v * up, up + 0.5 * v * (1.0 - t * t) * (root * (1.0 + 3.0 * 0.044715 * square))


def contract(left, right, left_axis, right_axis):
    return lax.dot_general(left, right, (((left_axis,), (right_axis,)), ((), ())), preferred_element_type=jnp.float32)


def feed_kernel(att, gates, tokens, cotangent, norms, output_w, inner_w, outer_w,
                layer_out, grad_residual, grad_att, grad_logit, grad_norms, part_output, part_inner, part_outer,
                w_out, w_in, w_up, acts, act_in, slopes, slope_in, scaled, scaled_in, scaled_t, cot_in, cot_t,
                acc, normed, grad_scaled, branch_low, branch_in, branch_t, att_in, gates_in,
                stage_outer, stage_inner, stage_output,
                load_out, load_in, load_up, pair_s, pair_r, act_s, act_r, slope_s, slope_r, put_outer, put_inner, put_output):
    seq, fsdp = lax.axis_index("seq"), lax.axis_index("fsdp")
    core = seq % 2
    mate = (seq + 1 - 2 * core, fsdp)
    experts = HEADS * EXP
    half = cotangent.shape[1] // 2
    quarter = inner_w.shape[1] // CHUNK // 2

    def out_load(e):
        return pltpu.make_async_copy(output_w.at[pl.ds(e * DH, DH)], w_out.at[e, pl.ds(0, DH)], load_out.at[e])

    def ffn_load(chunk, slot):
        cols = pl.ds(pl.multiple_of(chunk * CHUNK, CHUNK), CHUNK)
        return (pltpu.make_async_copy(inner_w.at[:, cols], w_in.at[slot], load_in.at[slot]),
                pltpu.make_async_copy(outer_w.at[cols], w_up.at[slot], load_up.at[slot]))

    def chunk_of(i, sub):
        return (core * quarter if sub else (1 - core) * quarter) + i

    for e in range(experts):
        out_load(e).start()
    for sub in range(2):
        for copy in ffn_load(chunk_of(0, sub), sub):
            copy.start()
    enter([mate])

    def remote(src, dst, send, recv):
        return pltpu.make_async_remote_copy(src, dst, send, recv, device_id=mate, device_id_type=MESH)

    mine = pl.ds(pl.multiple_of(core * half, LANES), half)
    yours = pl.ds(pl.multiple_of((1 - core) * half, LANES), half)
    pair = [
        remote(att, att_in, pair_s.at[0], pair_r.at[0]),
        remote(gates.at[0], gates_in, pair_s.at[1], pair_r.at[1]),
        remote(cotangent.at[:, yours], cot_in, pair_s.at[2], pair_r.at[2]),
        remote(scaled, scaled_in, pair_s.at[3], pair_r.at[3]),
        remote(branch_low.at[:, yours], branch_in, pair_s.at[4], pair_r.at[4]),
    ]
    for copy in pair[:3]:
        copy.start()

    def mixed_pair(att_ref, gate, two):
        tiles = []
        for which in (2 * two, 2 * two + 1):
            column = gate[:, experts + which : experts + which + 1]
            tiles.append((att_ref[which // EXP].astype(jnp.float32) * column).astype(jnp.bfloat16))
        return jnp.concatenate(tiles, axis=1)

    w_out[:, DH:, :] = jnp.zeros((experts, LANES - DH, w_out.shape[2]), jnp.bfloat16)
    acc[...] = tokens[...].astype(jnp.float32)
    for two in range(experts // 2):
        out_load(2 * two).wait()
        out_load(2 * two + 1).wait()
        weights = w_out[2 * two : 2 * two + 2].reshape(2 * LANES, w_out.shape[2])
        acc[...] += jnp.dot(mixed_pair(att, gates.at[0], two), weights, preferred_element_type=jnp.float32)
    residual = acc[...]
    centred = residual - jnp.mean(residual, axis=1, keepdims=True)
    inverse = lax.rsqrt(jnp.mean(centred * centred, axis=1, keepdims=True) + EPSILON)
    normed[...] = centred * inverse
    scaled[...] = (normed[...] * norms[:1] + norms[1:2]).astype(jnp.bfloat16)
    pair[3].start()
    rows = tokens.shape[0]
    scaled_t[:, :rows] = scaled[...].T
    cot_t[:, :rows] = cotangent[:, mine].T
    grad_scaled[...] = jnp.zeros_like(grad_scaled)
    pair[2].wait_recv()
    cot_t[:, rows:] = cot_in[...].T
    pair[3].wait_recv()
    scaled_t[:, rows:] = scaled_in[...].T

    def act_copy(chunk, sub):
        return remote(acts.at[sub], act_in.at[chunk], act_s.at[sub], act_r.at[chunk])

    def slope_copy(i):
        return remote(slopes.at[0], slope_in.at[i], slope_s.at[0], slope_r.at[i])

    def put_outer_copy(chunk, sub):
        cols = pl.ds(pl.multiple_of(chunk * CHUNK, CHUNK), CHUNK)
        return pltpu.make_async_copy(stage_outer.at[sub], part_outer.at[cols], put_outer.at[sub])

    def put_inner_copy(i):
        cols = pl.ds(pl.multiple_of(i * CHUNK, CHUNK), CHUNK)
        return pltpu.make_async_copy(stage_inner, part_inner.at[:, cols], put_inner.at[0])

    def forward_backward(i, sub):
        chunk = chunk_of(i, sub)
        for copy in ffn_load(chunk, sub):
            copy.wait()

        @pl.when(i > 0)
        def _():
            act_copy(chunk, sub).wait_send()
            if sub == 0:
                slope_copy(i).wait_send()

        act, slope = gelu_pair(jnp.dot(scaled[...], w_in[sub], preferred_element_type=jnp.float32))
        acts[sub] = act.astype(jnp.bfloat16)
        act_copy(chunk, sub).start()
        slopes[sub] = (contract(cotangent[...], w_up[sub], 1, 1) * slope).astype(jnp.bfloat16)
        if sub == 0:
            slope_copy(i).start()
        acc[...] += jnp.dot(acts[sub], w_up[sub], preferred_element_type=jnp.float32)
        grad_scaled[...] += contract(slopes[sub], w_in[sub], 1, 1)

        @pl.when(i < quarter - 1)
        def _():
            for copy in ffn_load(chunk_of(i + 1, sub), sub):
                copy.start()

    def outer_part(i, sub):
        chunk = chunk_of(i, sub)
        ref = act_in.at[chunk]
        remote(ref, ref, act_s.at[sub], act_r.at[chunk]).wait_recv()

        @pl.when(i > 0)
        def _():
            put_outer_copy(chunk, sub).wait()

        total = jnp.dot(cot_t[:, :rows], acts[sub], preferred_element_type=jnp.float32)
        total = total + jnp.dot(cot_t[:, rows:], act_in[chunk], preferred_element_type=jnp.float32)
        stage_outer[sub] = total.astype(jnp.bfloat16).T
        put_outer_copy(chunk, sub).start()

    def inner_part(i):
        ref = slope_in.at[i]
        remote(ref, ref, slope_s.at[0], slope_r.at[i]).wait_recv()

        @pl.when(i > 0)
        def _():
            put_inner_copy(i).wait()

        total = jnp.dot(scaled_t[:, :rows], slopes[1], preferred_element_type=jnp.float32)
        total = total + jnp.dot(scaled_t[:, rows:], slope_in[i], preferred_element_type=jnp.float32)
        stage_inner[...] = total.astype(jnp.bfloat16)
        put_inner_copy(i).start()

    def iteration(i, carry):
        forward_backward(i, 0)
        forward_backward(i, 1)
        outer_part(i, 1)
        inner_part(i)
        outer_part(i, 0)
        return carry

    lax.fori_loop(0, quarter, iteration, 0)
    layer_out[...] = acc[...].astype(jnp.bfloat16)
    slope = grad_scaled[...]
    grad_norms[...] = jnp.concatenate(
        [jnp.sum(slope * normed[...], axis=0, keepdims=True), jnp.sum(slope, axis=0, keepdims=True),
         jnp.zeros((6, slope.shape[1]), jnp.float32)], axis=0)
    slope = slope * norms[:1]
    total = cotangent[...].astype(jnp.float32) + inverse * (
        slope - jnp.mean(slope, axis=1, keepdims=True)
        - normed[...] * jnp.mean(slope * normed[...], axis=1, keepdims=True))
    grad_residual[...] = total
    branch_low[...] = total.astype(jnp.bfloat16)
    pair[4].start()
    branch_t[:, :rows] = branch_low[:, mine].T
    lane = lax.broadcasted_iota(jnp.int32, (rows, LANES), 1)
    logit = jnp.zeros((rows, LANES), jnp.float32)
    head_total = None
    for which in range(experts):
        if which % 2 == 0:
            weights = w_out[which : which + 2].reshape(2 * LANES, w_out.shape[2])
            both = contract(branch_low[...], weights, 1, 1)
        grad_mixed = both[:, which % 2 * LANES : (which % 2 + 1) * LANES]
        head, expert = which // EXP, which % EXP
        column = slice(experts + which, experts + which + 1)
        term = grad_mixed * gates[0, :, column]
        head_total = term if expert == 0 else head_total + term
        if expert == EXP - 1:
            grad_att[head] = head_total.astype(jnp.bfloat16)
        sums = jnp.sum(grad_mixed * att[head].astype(jnp.float32), axis=1, keepdims=True)
        logit = jnp.where(lane == experts + which, sums, logit)
    grad_logit[...] = logit * gates[1]
    pair[0].wait_recv()
    pair[1].wait_recv()
    pair[4].wait_recv()
    branch_t[:, rows:] = branch_in[...].T

    def put_output_copy(which):
        return pltpu.make_async_copy(stage_output.at[which % 4, pl.ds(0, DH)], part_output.at[pl.ds(which * DH, DH)], put_output.at[which % 4])

    for two in range(experts // 2):
        total = jnp.dot(branch_t[:, :rows], mixed_pair(att, gates.at[0], two), preferred_element_type=jnp.float32)
        total = total + jnp.dot(branch_t[:, rows:], mixed_pair(att_in, gates_in, two), preferred_element_type=jnp.float32)
        turned = total.astype(jnp.bfloat16).T
        for side in range(2):
            which = 2 * two + side
            if which >= 4:
                put_output_copy(which - 4).wait()
            stage_output[which % 4] = turned[side * LANES : (side + 1) * LANES]
            put_output_copy(which).start()
    for which in range(experts - 4, experts):
        put_output_copy(which).wait()
    for sub in range(2):
        put_outer_copy(0, sub).wait()
        act_copy(0, sub).wait_send()
    put_inner_copy(0).wait()
    slope_copy(0).wait_send()
    for copy in pair:
        copy.wait_send()


def feed(att, gates, tokens, cotangent, norms, output_w, inner_w, outer_w):
    rows, width = tokens.shape
    wide = inner_w.shape[1]
    half = width // 2
    f32, bf = jnp.float32, jnp.bfloat16
    experts, chunks = HEADS * EXP, wide // CHUNK
    V = pltpu.VMEM
    return pl.pallas_call(
        feed_kernel,
        out_shape=[
            jax.ShapeDtypeStruct((rows, width), bf),
            jax.ShapeDtypeStruct((rows, width), f32),
            jax.ShapeDtypeStruct((HEADS, rows, LANES), bf),
            jax.ShapeDtypeStruct((rows, LANES), f32),
            jax.ShapeDtypeStruct((8, width), f32),
            jax.ShapeDtypeStruct((VCOLS, half), bf),
            jax.ShapeDtypeStruct((width, wide // 2), bf),
            jax.ShapeDtypeStruct((wide, half), bf),
        ],
        in_specs=[VMEM] * 5 + [ANY] * 3,
        out_specs=[VMEM] * 5 + [ANY] * 3,
        scratch_shapes=[
            V((experts, LANES, width), bf), V((2, width, CHUNK), bf), V((2, CHUNK, width), bf),
            V((2, rows, CHUNK), bf), V((chunks, rows, CHUNK), bf), V((2, rows, CHUNK), bf), V((chunks // 2, rows, CHUNK), bf),
            V((rows, width), bf), V((rows, width), bf), V((width, 2 * rows), bf), V((rows, half), bf), V((half, 2 * rows), bf),
            V((rows, width), f32), V((rows, width), f32), V((rows, width), f32),
            V((rows, width), bf), V((rows, half), bf), V((half, 2 * rows), bf), V((HEADS, rows, LANES), bf), V((rows, LANES), f32),
            V((2, CHUNK, half), bf), V((width, CHUNK), bf), V((4, LANES, half), bf),
            DMA((experts,)), DMA((2,)), DMA((2,)), DMA((5,)), DMA((5,)), DMA((2,)), DMA((chunks,)), DMA((1,)), DMA((chunks // 2,)),
            DMA((2,)), DMA((1,)), DMA((4,)),
        ],
        compiler_params=pltpu.CompilerParams(collective_id=4, has_side_effects=True, vmem_limit_bytes=62 << 20),
    )(att, gates, tokens, cotangent, norms, output_w, inner_w, outer_w)


def settle_kernel(count, back, experts, gates, grad_logit, tokens, joint, grad_residual, grad_norms,
                  grad_tokens, joint_out, grads, grads_in, tokens_in, tokens_t, norms_in, norm_columns, *refs):
    splits = (SPLITS["joint"],)
    pair_s, pair_r = refs[-2:]
    ring = Scatter(count, splits, [], [joint_out], refs[:7], refs[7:-2])
    enter(ring.neighbours())
    core = ring.core
    half = JOINT // 2

    def remote(src, dst, i):
        return pltpu.make_async_remote_copy(src, dst, pair_s.at[i], pair_r.at[i], device_id=ring.core_mate, device_id_type=MESH)

    mine = pl.ds(pl.multiple_of(core * half, LANES), half)
    yours = pl.ds(pl.multiple_of((1 - core) * half, LANES), half)
    pair = [remote(tokens, tokens_in, 0), remote(grad_norms, norms_in, 1), remote(grads.at[:, yours], grads_in, 2)]
    pair[0].start()
    pair[1].start()
    rows = tokens.shape[0]
    lane = lax.broadcasted_iota(jnp.int32, (LANES, LANES), 1)
    width = HEADS * EXP

    def assemble(block, carry):
        part = pl.ds(pl.multiple_of(block * LANES, LANES), LANES)
        pieces = [back[head, which, part, :][:, :DH].astype(jnp.float32) for which in range(2) for head in range(HEADS)]
        logit = grad_logit[part, :]
        for head in range(HEADS):
            values = back[head, 2, part, :].astype(jnp.float32)
            for expert in range(EXP):
                which = head * EXP + expert
                pieces.append((values * gates[0, part, which : which + 1])[:, :DH])
                sums = jnp.sum(values * experts[which, part, :].astype(jnp.float32), axis=1, keepdims=True)
                logit = jnp.where(lane == which, sums * gates[1, part, which : which + 1], logit)
        pieces.append(jnp.where(lane < 2 * width, logit, 0.0))
        pieces.append(jnp.zeros((LANES, JOINT - ROUTERS - LANES), jnp.float32))
        grads[part, :] = jnp.concatenate(pieces, axis=1).astype(jnp.bfloat16)
        return carry

    lax.fori_loop(0, rows // LANES, assemble, 0)
    pair[2].start()
    tokens_t[:, :rows] = tokens[...].T
    for copy in pair[:2]:
        copy.wait_recv()
    tokens_t[:, rows:] = tokens_in[...].T
    norm_tile = NORM // LANES * LANES - half
    first = NORM - half - norm_tile
    both = grad_norms[...] + norms_in[...]
    for block in range(both.shape[1] // LANES):
        columns = jnp.concatenate([both[:, block * LANES : (block + 1) * LANES], jnp.zeros((LANES - 8, LANES), jnp.float32)], axis=0)
        norm_columns[block * LANES : (block + 1) * LANES, :] = columns.T
    pair[2].wait_recv()
    shard_rows = tokens_t.shape[0] // count
    tile_lane = lax.broadcasted_iota(jnp.int32, (shard_rows, LANES), 1)

    def fill(rel):
        part = pl.ds(pl.multiple_of(ring.dest(rel) * shard_rows, shard_rows), shard_rows)
        total = jnp.dot(tokens_t[part, :rows], grads[:, mine], preferred_element_type=jnp.float32)
        total = total + jnp.dot(tokens_t[part, rows:], grads_in[...], preferred_element_type=jnp.float32)
        ring.mine[0][rel] = total.astype(jnp.bfloat16)
        extra = jnp.where(tile_lane == first, norm_columns[part, 0:1], 0.0) + jnp.where(tile_lane == first + 1, norm_columns[part, 1:2], 0.0)
        tile = total[:, norm_tile : norm_tile + LANES] + extra * core.astype(jnp.float32)
        ring.mine[0][rel, :, norm_tile : norm_tile + LANES] = tile.astype(jnp.bfloat16)

    for rel in ring.order():
        fill(rel)
    events = ring.events()
    for event in events[:2]:
        event()
    grad_tokens[...] = grad_residual[...] + contract(grads[...], joint[...], 1, 1)
    for event in events[2:]:
        event()
    for copy in pair:
        copy.wait_send()


def settle(count, back, experts, gates, grad_logit, tokens, joint, grad_residual, grad_norms):
    rows, width = tokens.shape
    shard_rows = width // count
    f32, bf = jnp.float32, jnp.bfloat16
    V = pltpu.VMEM
    return pl.pallas_call(
        functools.partial(settle_kernel, count),
        out_shape=[jax.ShapeDtypeStruct((rows, width), f32), jax.ShapeDtypeStruct((shard_rows, JOINT), f32)],
        in_specs=[VMEM] * 8,
        out_specs=[VMEM] * 2,
        scratch_shapes=[V((rows, JOINT), bf), V((rows, JOINT // 2), bf), V((rows, width), bf), V((width, 2 * rows), bf), V((8, width), f32), V((width, LANES), f32)]
        + Scatter.scratch(count, (SPLITS["joint"],), [shard_rows])
        + [DMA((3,)), DMA((3,))],
        compiler_params=pltpu.CompilerParams(collective_id=5, has_side_effects=True, vmem_limit_bytes=60 << 20),
    )(back, experts, gates, grad_logit, tokens, joint, grad_residual, grad_norms)


def on_device(
    tokens, value_routes, output_routes, cont_gap, query_weight, key_weight, value_weight, value_router,
    output_router, output_weight, norm_gain, norm_bias, inner_weight, outer_weight, cotangent,
):
    count = lax.axis_size("fsdp")
    inputs = tokens[0]
    rows, width = inputs.shape
    routers = jnp.concatenate(
        [value_router, output_router, norm_gain[:, None], norm_bias[:, None],
         jnp.zeros((query_weight.shape[0], JOINT - NORM - 2), jnp.bfloat16)], axis=1)
    routes = jnp.concatenate([value_routes[0].reshape(rows, -1), output_routes[0].reshape(rows, -1)], axis=1)
    joint, qkv, experts, gates, norms, tables, turned = project(
        count, query_weight, key_weight, value_weight, routers, inputs, routes, cont_gap)
    splits = tuple(SPLITS[name] for name in ("output", "inner", "outer"))
    att, store, outputs, logs, output_full, inner_full, outer_full = attend(
        count, qkv, tables, (output_weight, inner_weight, outer_weight), splits)
    layer_out, grad_residual, grad_att, grad_logit, grad_norms, *parts = feed(
        att, gates, inputs, cotangent[0], norms, output_full.reshape(VCOLS, width), inner_full.reshape(width, -1),
        outer_full.reshape(-1, width))
    parts = tuple(part.reshape(count, -1, part.shape[1]) for part in parts)
    back, out_w, in_w, outer_w = retreat(count, grad_att, turned, store, outputs, logs, parts, splits)
    grad_input, joint_w = settle(count, back, experts, gates, grad_logit, inputs, joint, grad_residual, grad_norms)
    return (
        layer_out[None], grad_input[None], joint_w[:, :QCOLS], joint_w[:, QCOLS : 2 * QCOLS], joint_w[:, 2 * QCOLS : ROUTERS],
        joint_w[:, ROUTERS : ROUTERS + HEADS * EXP], joint_w[:, ROUTERS + HEADS * EXP : NORM], out_w, joint_w[:, NORM],
        joint_w[:, NORM + 1], in_w, outer_w,
    )


def solution(mesh):
    wide = P("fsdp", None)
    part = P("fsdp", "seq", None)
    routes = P("fsdp", "seq", None, None)
    return jax.shard_map(
        on_device,
        mesh=mesh,
        in_specs=(part, routes, routes, P()) + (wide,) * 6 + (P("fsdp"), P("fsdp"), wide, wide, part),
        out_specs=(part, part) + (wide,) * 6 + (P("fsdp"), P("fsdp"), wide, wide),
        check_vma=False,
    )
```

time: 2150 us -> 511 us (0.24)
  waiting for transfers between devices: 1310 us -> 0 us
  Pallas kernels: 0 us -> 468 us
  blocking collectives: 420 us -> 0 us
  matrix products: 213 us -> 0 us
  other arithmetic: 69.8 us -> 0.01 us
  starting transfers between devices: 38.2 us -> 0 us
  local copies, waits for them, and re-layouts: 55 us -> 31.7 us
    reduce_scatter x8 -> x0, waiting for transfers between devices: 916 us -> none  [the longest x1 283 us: on_device(): lax.psum_scatter(grad_outer_w, 'fsdp', scatter_dimension=0, tiled=True)]
    pallas_call x0 -> x5, Pallas kernels: none -> 468 us  [the longest x1 155 us: retreat(): pl.pallas_call(functools.partial(retreat_kernel, count, splits, steps), o...]
    all_gather x6 -> x0, blocking collectives: 329 us -> none  [the longest x1 187 us: on_device(): lax.all_gather(output_router, 'fsdp', axis=0, tiled=True)]
    ppermute x6 -> x0, waiting for transfers between devices: 292 us -> none  [shifted(): lax.ppermute(value, axis, [(source, source + steps) for source in range(i...]
    dot_general x94 -> x0, matrix products: 213 us -> none  [the longest x20 30.8 us: block_scores(): jnp.einsum('qd,kd->qk', query_block, key_block, preferred_element_type=jn...]
    psum x1 -> x0, waiting for transfers between devices: 64.6 us -> none  [on_device(): lax.psum(reduced[0].astype(jnp.bfloat16), 'seq').astype(jnp.float32)]
    unnamed x1 -> x0, blocking collectives: 59.4 us -> none
    convert_element_type x29 -> x0, other arithmetic: 39.1 us -> none  [the longest x1 3.15 us: on_device(): grad_experts = (value_gates.reshape(local_rows, HEADS, EXP, 1) * back_wid...]
  transfers between devices with their start and end apart: 25 -> 0, of which waited for: 13 -> 0; matrix products, arithmetic and copies ran while one was open for 14% -> 0% of each run, Pallas kernels for 0% -> 0%
where the time goes in v1:
time: 511 us; the launch traced here: 501 us
  Pallas kernels  468 us (92%)
  local copies, waits for them, and re-layouts  31.7 us (6%)
    pallas_call x1, Pallas kernels, retreat(): pl.pallas_call(functools.partial(retreat_kernel, count, splits, steps), o...  155 us
    pallas_call x1, Pallas kernels, attend(): pl.pallas_call(functools.partial(attend_kernel, count, splits, steps), ou...  120 us
    pallas_call x1, Pallas kernels, settle(): pl.pallas_call(functools.partial(settle_kernel, count), out_shape=[jax.Sh...  79 us
    pallas_call x1, Pallas kernels, feed(): pl.pallas_call(feed_kernel, out_shape=[jax.ShapeDtypeStruct((rows, width)...  61.3 us
    pallas_call x1, Pallas kernels, project(): pl.pallas_call(functools.partial(project_kernel, count), out_shape=[jax.S...  52.4 us
    unnamed x25, local copies, waits for them, and re-layouts  21.2 us

profile of v1, /device:TPU:0, one launch (start us, length us, event | category | flops | bytes accessed | tf_op | source)
XLA Modules:
  0.0 501.0 jit_solution(17614826824578387082)
XLA Ops:
  0.6 0.7 reshape_squeeze.6
  1.4 0.7 reshape_squeeze.7
  2.1 0.8 copy.55
  2.9 0.8 copy.56
  3.8 0.8 copy.57
  4.5 0.8 copy.58
  5.3 0.8 concatenate.6.routers
  6.1 1.7 copy.59.query
  7.8 1.7 copy.60.key
  9.4 0.8 copy.62.routes
  10.3 2.1 copy.61.value
  12.4 52.4 %shard_map.238 = (bf16[1024,3328]{1,0:T(8,128)(2,1)}, bf16[4,3,512,128]{3,2,1,0:T(8,128)(2,1)}, bf16[20,512,128]{2,1,0:T(8,128)(2,1)}, f32[2,512,128]{2,1,0:T(8,...) custom-call(bf16[128,448]{1,0:T(8,128)(2,1)} %copy.59.query, ...), custom_call_target="tpu_custom_call" | custom-call | tf_op jit(solution)/shard_map/pallas_call | solution.py:286
  64.7 120.1 %shard_map.239 = (bf16[4,512,128]{2,1,0:T(8,128)(2,1)}, bf16[7,2048,128]{2,1,0:T(8,128)(2,1)}, f32[2048,128]{1,0:T(8,128)}, f32[8,2048]{1,0:T(8,128)}, bf16[8,28...) custom-call(bf16[4,3,512,128]{3,2,1,0:T(8,128)(2,1)} %get-tuple-element.40.qkv, ...), custom_call_target="tpu_custom_call" | custom-call | tf_op jit(solution)/shard_map/pallas_call | solution.py:507
  184.8 61.3 %shard_map.240 = (bf16[512,1024]{1,0:T(8,128)(2,1)}, f32[512,1024]{1,0:T(8,128)}, bf16[4,512,128]{2,1,0:T(8,128)(2,1)}, f32[512,128]{1,0:T(8,128)}, f32[8,1024]{...) custom-call(bf16[4,512,128]{2,1,0:T(8,128)(2,1)} %get-tuple-element.42.att, ...), custom_call_target="tpu_custom_call" | custom-call | tf_op jit(solution)/shard_map/pallas_call | solution.py:1138
  246.2 155.5 %shard_map.241 = (bf16[4,3,512,128]{3,2,1,0:T(8,128)(2,1)}, f32[280,1024]{1,0:T(8,128)}, f32[128,4096]{1,0:T(8,128)}, f32[512,1024]{1,0:T(8,128)}) custom-call(bf16[4,512,128]{2,1,0:T(8,128)(2,1)} %get-tuple-element.49.grad_att, f32[3,128,5632]{2,1,0:T(8,128)} %get-tuple-element.50.turned, bf16[7,2048,128]{2,1,0:T(8,128)(2,1)} %get-tuple-element.51.store, ...), custom_call_target="tpu_custom_call" | custom-call | tf_op jit(solution)/shard_map/pallas_call | solution.py:885
  401.7 79.0 %shard_map.242 = (f32[512,1024]{1,0:T(8,128)}, f32[128,3328]{1,0:T(8,128)}) custom-call(bf16[4,3,512,128]{3,2,1,0:T(8,128)(2,1)} %get-tuple-element.57.back, bf16[20,512,128]{2,1,0:T(8,128)(2,1)} %get-tuple-element.58.experts, f32[2,512,128]{2,1,0:T(8,128)} %get-tuple-element.43.gates, f32[512,128]{1,0:T(8,128)} %get-tuple-element.59.grad_logit, ...), custom_call_target="tpu_custom_call" | custom-call | tf_op jit(solution)/shard_map/pallas_call | solution.py:1245
  480.6 1.6 slice_reduce_fusion
  482.2 1.0 fusion
  483.3 0.7 copy.67
  483.9 0.7 copy.66
  484.6 1.9 fusion.1
  486.5 1.3 slice.23
  487.9 0.0 copy-start.4
  487.9 1.4 copy.65
  489.2 0.0 copy-start.2
  489.2 1.9 copy.64
  491.2 0.8 copy.63
  492.0 0.0 copy-done.4
  492.0 1.0 copy.73
  493.0 0.0 copy-done.2
  493.0 0.0 copy-start.3
  493.0 1.3 copy.74
  494.3 0.7 copy-done.3
  495.0 0.0 copy-start.1
  495.0 1.0 copy.75
  496.0 1.0 copy-done.1
  497.0 0.0 copy-start
  497.0 1.3 copy.76
  498.3 1.0 copy-done
  499.3 1.3 copy.77
  (2 shorter events, 0.0 us)
Async XLA Ops:
  487.9 4.1 copy-start.4
  489.2 3.7 copy-start.2
  493.0 2.0 copy-start.3
  495.0 2.0 copy-start.1
  497.0 2.3 copy-start

commit v2 on v1

--- a/solution.py
+++ b/solution.py
@@ -28,7 +28,8 @@
 ROUTERS = 2 * QCOLS + VCOLS
 NORM = ROUTERS + 2 * HEADS * EXP
 JOINT = 3328
-SPLITS = {"joint": (640, 512), "output": (0, 256), "inner": (768, 640), "outer": (256, 128)}
+SPLITS = {"joint": (640, 512), "output": (256, 128), "inner": (768, 640), "outer": (256, 128)}
+INNER_PARTS = ((512, 256), (512, 256))
 
 
 def ring_place(index, count):
@@ -199,12 +200,17 @@
     return hit.astype(jnp.float32)
 
 
-def project_kernel(count, query, key, value, routers, tokens, routes, gaps, joint, qkv, experts, gates, norms, tables, turned_tables,
+def project_kernel(count, query, key, value, routers, tokens, routes, output_shard, gaps, joint, output_w, qkv, experts, gates, norms, tables, turned_tables,
                    shard, product, send, recv, local):
     rows = shard.shape[0]
-    splits = (SPLITS["joint"],)
-    at = lambda t, g, cols: joint.at[pl.ds(pl.multiple_of(g * rows, rows), rows), cols]
-    ring = Gather(count, splits, [shard], at, send, recv, local)
+    splits = (SPLITS["joint"], SPLITS["output"])
+
+    def at(t, g, cols):
+        if t:
+            return output_w.at[g, :, cols]
+        return joint.at[pl.ds(pl.multiple_of(g * rows, rows), rows), cols]
+
+    ring = Gather(count, splits, [shard, output_shard], at, send, recv, local)
     wide = jnp.concatenate([ref[...].astype(jnp.float32) for ref in (query, key, value, routers)], axis=1)
     shard[...] = wide.astype(jnp.bfloat16)
     enter(ring.neighbours())
@@ -233,24 +239,41 @@
                 target[which, :, pl.ds(start, 256)] = rolled[:, LANES:]
         return carry
 
-    events = ring.events()
-    cut = max(1, (TABLE // 256) // max(1, ring.far))
+    late = max(1, ring.far - 1)
+    steps, later = [], []
+    for k in range(1, ring.far + 1):
+        steps.append(functools.partial(ring.arrive, 0, k))
+        if k > 1:
+            steps.append(functools.partial(ring.plane_arrive, 0, k - 1))
+        if k == late:
+            steps.append(functools.partial(ring.start, 1))
+        later.append(functools.partial(ring.arrive, 1, k))
+        if k > 1:
+            later.append(functools.partial(ring.plane_arrive, 1, k - 1))
+    steps += [functools.partial(ring.plane_arrive, 0, ring.far), functools.partial(ring.finish, 0)]
+    later += [functools.partial(ring.plane_arrive, 1, ring.far)]
+    early = later[:1]
+    later = later[1:]
+    steps = steps[:-1] + early + steps[-1:]
+    cut = max(1, TABLE // 256 // len(steps))
     done = 0
-    for i, event in enumerate(events):
-        upto = min(TABLE // 256, (i + 1) * cut)
+    for i, event in enumerate(steps):
+        upto = TABLE // 256 if i == len(steps) - 1 else min(TABLE // 256, (i + 1) * cut)
         if upto > done:
             lax.fori_loop(done, upto, table_column, 0)
             done = upto
         event()
-    if done < TABLE // 256:
-        lax.fori_loop(done, TABLE // 256, table_column, 0)
 
     def column(step, carry):
         cols = pl.ds(pl.multiple_of(step * 256, 256), 256)
         product[:, cols] = jnp.dot(tokens[...], joint[:, cols], preferred_element_type=jnp.float32)
         return carry
 
-    lax.fori_loop(0, JOINT // 256, column, 0)
+    columns = JOINT // 256
+    for i in range(3):
+        lax.fori_loop(i * columns // 3, (i + 1) * columns // 3, column, 0)
+        for event in later[i * len(later) // 4 : (i + 1) * len(later) // 4]:
+            event()
     norm_tile = NORM // LANES * LANES
     turned_norm = joint[:, norm_tile : norm_tile + LANES].astype(jnp.float32).T
     norms[...] = turned_norm[NORM - norm_tile : NORM - norm_tile + 8]
@@ -278,15 +301,19 @@
             term = piece * gates[0, :, which : which + 1]
             total = term if total is None else total + term
         qkv[head, 2] = jnp.concatenate([total, ones], axis=1).astype(jnp.bfloat16)
-
-
-def project(count, query, key, value, routers, tokens, routes, gaps):
+    for event in later[3 * len(later) // 4 :]:
+        event()
+    ring.finish(1)
+
+
+def project(count, query, key, value, routers, tokens, routes, output_shard, gaps):
     rows, (shard_rows, _) = tokens.shape[0], query.shape
     f32, bf = jnp.float32, jnp.bfloat16
     return pl.pallas_call(
         functools.partial(project_kernel, count),
         out_shape=[
             jax.ShapeDtypeStruct((shard_rows * count, JOINT), bf),
+            jax.ShapeDtypeStruct((count,) + output_shard.shape, bf),
             jax.ShapeDtypeStruct((HEADS, 3, rows, LANES), bf),
             jax.ShapeDtypeStruct((HEADS * EXP, rows, LANES), bf),
             jax.ShapeDtypeStruct((2, rows, LANES), f32),
@@ -294,11 +321,11 @@
             jax.ShapeDtypeStruct((3, LANES, TABLE), f32),
             jax.ShapeDtypeStruct((3, LANES, TABLE), f32),
         ],
-        in_specs=[VMEM] * 6 + [SMEM],
-        out_specs=[VMEM] * 7,
-        scratch_shapes=[pltpu.VMEM((shard_rows, JOINT), bf), pltpu.VMEM((rows, JOINT), f32)] + Gather.sems(count, 1),
+        in_specs=[VMEM] * 6 + [ANY, SMEM],
+        out_specs=[VMEM, ANY] + [VMEM] * 6,
+        scratch_shapes=[pltpu.VMEM((shard_rows, JOINT), bf), pltpu.VMEM((rows, JOINT), f32)] + Gather.sems(count, 2),
         compiler_params=pltpu.CompilerParams(collective_id=1, has_side_effects=True, vmem_limit_bytes=56 << 20),
-    )(query, key, value, routers, tokens, routes, gaps)
+    )(query, key, value, routers, tokens, routes, output_shard, gaps)
 
 
 def seq_mates(ring):
@@ -554,7 +581,9 @@
         return ring_index((self.place + rel) % self.count, self.count)
 
     def load_copy(self, t, rel):
-        return pltpu.make_async_copy(self.parts[t].at[self.dest(rel)], self.mine[t].at[rel], self.load.at[t * self.count + rel])
+        part, first = self.parts[t]
+        src = part.at[self.dest(rel), :, pl.ds(first, self.half(t))]
+        return pltpu.make_async_copy(src, self.mine[t].at[rel], self.load.at[t * self.count + rel])
 
     def remote(self, src, dst, s, r, i, device):
         return pltpu.make_async_remote_copy(src, dst, s.at[i], r.at[i], device_id=device, device_id_type=MESH)
@@ -580,11 +609,21 @@
         for rel in self.order():
             self.load_copy(t, rel).start()
 
-    def prepare(self, t, D):
-        for rel in self.rels(D):
-            if self.parts:
-                self.load_copy(t, rel).wait()
-            self.plane_copy(t, rel).start()
+    def ready(self, t, rel):
+        if self.parts[t]:
+            self.load_copy(t, rel).wait()
+        self.plane_copy(t, rel).start()
+
+    def all_ready(self, t):
+        for rel in self.order():
+            self.ready(t, rel)
+
+    def step(self, t, D):
+        self.combine(t, D)
+        if D:
+            self.chain(t, D)
+        else:
+            self.close(t)
 
     def buffer(self, t, kind, slot):
         if kind:
@@ -649,8 +688,8 @@
         self.end_copy(t).start()
 
     def out_ref(self, t, core):
-        half = self.half(t)
-        return self.outs[t].at[:, pl.ds(pl.multiple_of(core * half, LANES), half)]
+        out, whole, first = self.outs[t]
+        return out.at[:, pl.ds(pl.multiple_of(core * whole + first, LANES), self.half(t))]
 
     def out_copy(self, t):
         return self.remote(self.done[t], self.out_ref(t, self.core), self.end_s, self.end_r, 2 * t + 1, self.core_mate)
@@ -681,34 +720,17 @@
         ref = self.out_ref(t, 1 - self.core)
         self.remote(ref, ref, self.end_s, self.end_r, 2 * t + 1, self.core_mate).wait_recv()
 
-    def events(self):
-        tensors = range(len(self.splits))
-        part = functools.partial
-        out = [part(self.prepare, t, self.far) for t in tensors]
-        for D in range(self.far, 0, -1):
-            for t in tensors:
-                out.append(part(self.prepare, t, D - 1))
-            for t in tensors:
-                out.append(part(self.combine, t, D))
-                out.append(part(self.chain, t, D))
-        for t in tensors:
-            out.append(part(self.combine, t, 0))
-            out.append(part(self.close, t))
-        for t in tensors:
-            out.append(part(self.deliver, t))
-        for t in tensors:
-            out.append(part(self.finish, t))
-        return out
-
-
-def retreat_kernel(count, splits, steps, grad_att, turned, store, outputs, logs, *refs):
+
+def retreat_kernel(count, splits, steps, grad_att, turned, store, outputs, logs, part, back, out, *refs):
     T = len(splits)
-    parts, refs = refs[:T], refs[T:]
-    back, outs, refs = refs[0], refs[1 : 1 + T], refs[1 + T :]
     (grads, delta, grad_q, grad_kv, send_kv, kv_in0, kv_in1, low, in_send, in_recv, up_send, up_recv,
      out_send, out_recv, here) = refs[:15]
     refs = refs[15:]
-    ring = Scatter(count, splits, parts, outs, refs[: 7 * T], refs[7 * T :]) if T else Ring(count, splits)
+    halves = [a + 2 * b for a, b in splits]
+    firsts = [sum(halves[:t]) for t in range(T)]
+    ring = Scatter(
+        count, splits, [(part, first) for first in firsts], [(out, sum(halves), first) for first in firsts],
+        refs[: 7 * T], refs[7 * T :])
     seq, slot = ring.seq, ring.fsdp % GSLOTS
     mates, (x_mate, z_mate) = seq_mates(ring), slot_mates(ring)
     enter(ring.neighbours() + mates[2:] + [x_mate, z_mate])
@@ -832,16 +854,22 @@
     for chunk in range(4):
         events.setdefault(4 * chunk + 4, []).append(functools.partial(first_done, chunk))
         events.setdefault(20 + 4 * chunk, []).append(functools.partial(second_done, chunk))
+    begin, ready, first, hop, lag = steps
     rest = []
-    if T:
-        begin, gap = steps
-        events.setdefault(begin, []).extend([functools.partial(ring.start, t) for t in range(T)])
-        for i, event in enumerate(ring.events()):
-            step = begin + int(gap * (i + 1))
-            if step < 48:
-                events.setdefault(step, []).append(event)
+    for t in range(T):
+        plan = [(begin, functools.partial(ring.start, t)), (ready, functools.partial(ring.all_ready, t))]
+        when = first + lag * t
+        for D in range(ring.far, -1, -1):
+            plan.append((when, functools.partial(ring.step, t, D)))
+            when += hop
+        plan.append((when, functools.partial(ring.deliver, t)))
+        plan.append((when + hop, functools.partial(ring.finish, t)))
+        for when, event in plan:
+            if when < 48:
+                events.setdefault(int(when), []).append(event)
             else:
-                rest.append(event)
+                rest.append((when, event))
+    rest = [event for when, event in sorted(rest, key=lambda pair: pair[0])]
 
     def step_body(step, carry):
         for when, actions in sorted(events.items()):
@@ -877,17 +905,15 @@
             z_send(chunk).wait_send()
 
 
-def retreat(count, grad_att, turned, store, outputs, logs, parts, splits, steps=(0, 1)):
+def retreat(count, grad_att, turned, store, outputs, logs, part, splits, steps=(0, 1, 6, 6, 2)):
     rows = grad_att.shape[1]
     own = 4 * rows
-    T = len(parts)
-    shard_rows = [p.shape[1] for p in parts]
+    _, shard_rows, half = part.shape
     return pl.pallas_call(
         functools.partial(retreat_kernel, count, splits, steps),
-        out_shape=[jax.ShapeDtypeStruct((HEADS, 3, rows, LANES), jnp.bfloat16)]
-        + [jax.ShapeDtypeStruct((p.shape[1], 2 * p.shape[2]), jnp.float32) for p in parts],
-        in_specs=[VMEM] * 5 + [ANY] * T,
-        out_specs=[VMEM] + [ANY] * T,
+        out_shape=[jax.ShapeDtypeStruct((HEADS, 3, rows, LANES), jnp.bfloat16), jax.ShapeDtypeStruct((shard_rows, 2 * half), jnp.float32)],
+        in_specs=[VMEM] * 5 + [ANY],
+        out_specs=[VMEM, ANY],
         scratch_shapes=[
             pltpu.VMEM((own, LANES), jnp.bfloat16),
             pltpu.VMEM((8, own), jnp.float32),
@@ -899,9 +925,9 @@
             pltpu.VMEM((3, own, LANES), jnp.bfloat16),
             DMA((4,)), DMA((4,)), DMA((8,)), DMA((8,)), DMA((4,)), DMA((4,)), DMA((2,)),
         ]
-        + (Scatter.scratch(count, splits, shard_rows) if T else []),
-        compiler_params=pltpu.CompilerParams(collective_id=3, has_side_effects=True, vmem_limit_bytes=63 << 20),
-    )(grad_att, turned, store, outputs, logs, *parts)
+        + Scatter.scratch(count, splits, [shard_rows] * len(splits)),
+        compiler_params=pltpu.CompilerParams(collective_id=3, has_side_effects=True, vmem_limit_bytes=60 << 20),
+    )(grad_att, turned, store, outputs, logs, part)
 
 
 CHUNK = 512
@@ -919,18 +945,19 @@
     return lax.dot_general(left, right, (((left_axis,), (right_axis,)), ((), ())), preferred_element_type=jnp.float32)
 
 
-def feed_kernel(att, gates, tokens, cotangent, norms, output_w, inner_w, outer_w,
-                layer_out, grad_residual, grad_att, grad_logit, grad_norms, part_output, part_inner, part_outer,
+def feed_kernel(count, att, gates, tokens, cotangent, norms, output_w, inner_w, outer_w,
+                layer_out, grad_residual, grad_att, grad_logit, grad_norms, part_output, part_inner, outer_out,
                 w_out, w_in, w_up, acts, act_in, slopes, slope_in, scaled, scaled_in, scaled_t, cot_in, cot_t,
                 acc, normed, grad_scaled, branch_low, branch_in, branch_t, att_in, gates_in,
-                stage_outer, stage_inner, stage_output,
-                load_out, load_in, load_up, pair_s, pair_r, act_s, act_r, slope_s, slope_r, put_outer, put_inner, put_output):
-    seq, fsdp = lax.axis_index("seq"), lax.axis_index("fsdp")
-    core = seq % 2
-    mate = (seq + 1 - 2 * core, fsdp)
+                stage_inner, stage_output,
+                load_out, load_in, load_up, pair_s, pair_r, act_s, act_r, slope_s, slope_r, put_inner, put_output, *refs):
+    half = cotangent.shape[1] // 2
+    ring = Scatter(count, (SPLITS["outer"],), [None], [(outer_out, half, 0)], refs[:7], refs[7:])
+    core, mate = ring.core, ring.core_mate
     experts = HEADS * EXP
-    half = cotangent.shape[1] // 2
-    quarter = inner_w.shape[1] // CHUNK // 2
+    chunks = inner_w.shape[1] // CHUNK
+    small = CHUNK // 2
+    shards = max(1, count // chunks)
 
     def out_load(e):
         return pltpu.make_async_copy(output_w.at[pl.ds(e * DH, DH)], w_out.at[e, pl.ds(0, DH)], load_out.at[e])
@@ -940,15 +967,19 @@
         return (pltpu.make_async_copy(inner_w.at[:, cols], w_in.at[slot], load_in.at[slot]),
                 pltpu.make_async_copy(outer_w.at[cols], w_up.at[slot], load_up.at[slot]))
 
-    def chunk_of(i, sub):
-        return (core * quarter if sub else (1 - core) * quarter) + i
+    def chunk_of(step):
+        if count != chunks:
+            return step
+        D = ring.far - (step + 1) // 2
+        odd = step % 2
+        return ring.dest((odd * D + (1 - odd) * (count - D)) % count)
 
     for e in range(experts):
         out_load(e).start()
     for sub in range(2):
-        for copy in ffn_load(chunk_of(0, sub), sub):
+        for copy in ffn_load(chunk_of(sub), sub):
             copy.start()
-    enter([mate])
+    enter(ring.neighbours())
 
     def remote(src, dst, send, recv):
         return pltpu.make_async_remote_copy(src, dst, send, recv, device_id=mate, device_id_type=MESH)
@@ -994,81 +1025,97 @@
     pair[3].wait_recv()
     scaled_t[:, rows:] = scaled_in[...].T
 
-    def act_copy(chunk, sub):
-        return remote(acts.at[sub], act_in.at[chunk], act_s.at[sub], act_r.at[chunk])
-
-    def slope_copy(i):
-        return remote(slopes.at[0], slope_in.at[i], slope_s.at[0], slope_r.at[i])
-
-    def put_outer_copy(chunk, sub):
-        cols = pl.ds(pl.multiple_of(chunk * CHUNK, CHUNK), CHUNK)
-        return pltpu.make_async_copy(stage_outer.at[sub], part_outer.at[cols], put_outer.at[sub])
-
-    def put_inner_copy(i):
-        cols = pl.ds(pl.multiple_of(i * CHUNK, CHUNK), CHUNK)
-        return pltpu.make_async_copy(stage_inner, part_inner.at[:, cols], put_inner.at[0])
-
-    def forward_backward(i, sub):
-        chunk = chunk_of(i, sub)
-        for copy in ffn_load(chunk, sub):
+    small_mine = pl.ds(pl.multiple_of(core * small, LANES), small)
+    small_yours = pl.ds(pl.multiple_of((1 - core) * small, LANES), small)
+
+    def act_copy(step, sub):
+        return remote(acts.at[sub], act_in.at[step], act_s.at[sub], act_r.at[step])
+
+    def slope_copy(step, sub):
+        return remote(slopes.at[sub, :, small_yours], slope_in.at[step], slope_s.at[sub], slope_r.at[step])
+
+    def put_inner_copy(step, sub):
+        cols = pl.ds(pl.multiple_of(chunk_of(step) * small, small), small)
+        return pltpu.make_async_copy(stage_inner.at[sub], part_inner.at[:, cols], put_inner.at[sub])
+
+    def forward_backward(step, sub):
+        for copy in ffn_load(chunk_of(step), sub):
             copy.wait()
 
-        @pl.when(i > 0)
-        def _():
-            act_copy(chunk, sub).wait_send()
-            if sub == 0:
-                slope_copy(i).wait_send()
+        @pl.when(step > 1)
+        def _():
+            act_copy(step, sub).wait_send()
+            slope_copy(step, sub).wait_send()
 
         act, slope = gelu_pair(jnp.dot(scaled[...], w_in[sub], preferred_element_type=jnp.float32))
         acts[sub] = act.astype(jnp.bfloat16)
-        act_copy(chunk, sub).start()
+        act_copy(step, sub).start()
         slopes[sub] = (contract(cotangent[...], w_up[sub], 1, 1) * slope).astype(jnp.bfloat16)
-        if sub == 0:
-            slope_copy(i).start()
+        slope_copy(step, sub).start()
         acc[...] += jnp.dot(acts[sub], w_up[sub], preferred_element_type=jnp.float32)
         grad_scaled[...] += contract(slopes[sub], w_in[sub], 1, 1)
 
-        @pl.when(i < quarter - 1)
-        def _():
-            for copy in ffn_load(chunk_of(i + 1, sub), sub):
+        @pl.when(step + 2 < chunks)
+        def _():
+            for copy in ffn_load(chunk_of(step + 2), sub):
                 copy.start()
 
-    def outer_part(i, sub):
-        chunk = chunk_of(i, sub)
-        ref = act_in.at[chunk]
-        remote(ref, ref, act_s.at[sub], act_r.at[chunk]).wait_recv()
+    def weight_parts(step, sub):
+        remote(act_in.at[step], act_in.at[step], act_s.at[sub], act_r.at[step]).wait_recv()
+        total = jnp.dot(cot_t[:, :rows], acts[sub], preferred_element_type=jnp.float32)
+        total = total + jnp.dot(cot_t[:, rows:], act_in[step], preferred_element_type=jnp.float32)
+        turned = total.astype(jnp.bfloat16).T
+        shard_rows = CHUNK // shards
+        for q in range(shards):
+            rel = (ring_place(chunk_of(step) * shards + q, count) - ring.place + count) % count
+            ring.mine[0][rel] = turned[q * shard_rows : (q + 1) * shard_rows]
+        remote(slope_in.at[step], slope_in.at[step], slope_s.at[sub], slope_r.at[step]).wait_recv()
+
+        @pl.when(step > 1)
+        def _():
+            put_inner_copy(step, sub).wait()
+
+        total = jnp.dot(scaled_t[:, :rows], slopes[sub, :, small_mine], preferred_element_type=jnp.float32)
+        total = total + jnp.dot(scaled_t[:, rows:], slope_in[step], preferred_element_type=jnp.float32)
+        stage_inner[sub] = total.astype(jnp.bfloat16)
+        put_inner_copy(step, sub).start()
+
+    events = {}
+    if count == chunks:
+        for step, rel in enumerate(ring.order()):
+            events.setdefault(step, []).append(functools.partial(ring.ready, 0, rel))
+        for D in range(ring.far, 0, -1):
+            events.setdefault(2 * (ring.far - D) + 1, []).append(functools.partial(ring.step, 0, D))
+
+    def after_parts(step):
+        for when, actions in sorted(events.items()):
+            @pl.when(step == when)
+            def _():
+                for action in actions:
+                    action()
+
+    def iteration(i, carry):
+        forward_backward(2 * i, 0)
 
         @pl.when(i > 0)
         def _():
-            put_outer_copy(chunk, sub).wait()
-
-        total = jnp.dot(cot_t[:, :rows], acts[sub], preferred_element_type=jnp.float32)
-        total = total + jnp.dot(cot_t[:, rows:], act_in[chunk], preferred_element_type=jnp.float32)
-        stage_outer[sub] = total.astype(jnp.bfloat16).T
-        put_outer_copy(chunk, sub).start()
-
-    def inner_part(i):
-        ref = slope_in.at[i]
-        remote(ref, ref, slope_s.at[0], slope_r.at[i]).wait_recv()
-
-        @pl.when(i > 0)
-        def _():
-            put_inner_copy(i).wait()
-
-        total = jnp.dot(scaled_t[:, :rows], slopes[1], preferred_element_type=jnp.float32)
-        total = total + jnp.dot(scaled_t[:, rows:], slope_in[i], preferred_element_type=jnp.float32)
-        stage_inner[...] = total.astype(jnp.bfloat16)
-        put_inner_copy(i).start()
-
-    def iteration(i, carry):
-        forward_backward(i, 0)
-        forward_backward(i, 1)
-        outer_part(i, 1)
-        inner_part(i)
-        outer_part(i, 0)
+            weight_parts(2 * i - 1, 1)
+            after_parts(2 * i - 1)
+
+        forward_backward(2 * i + 1, 1)
+        weight_parts(2 * i, 0)
+        after_parts(2 * i)
         return carry
 
-    lax.fori_loop(0, quarter, iteration, 0)
+    lax.fori_loop(0, chunks // 2, iteration, 0)
+    weight_parts(chunks - 1, 1)
+    if count == chunks:
+        for action in events[chunks - 1]:
+            action()
+    else:
+        ring.all_ready(0)
+        for D in range(ring.far, 0, -1):
+            ring.step(0, D)
     layer_out[...] = acc[...].astype(jnp.bfloat16)
     slope = grad_scaled[...]
     grad_norms[...] = jnp.concatenate(
@@ -1082,6 +1129,7 @@
     branch_low[...] = total.astype(jnp.bfloat16)
     pair[4].start()
     branch_t[:, :rows] = branch_low[:, mine].T
+    ring.step(0, 0)
     lane = lax.broadcasted_iota(jnp.int32, (rows, LANES), 1)
     logit = jnp.zeros((rows, LANES), jnp.float32)
     head_total = None
@@ -1099,6 +1147,7 @@
         sums = jnp.sum(grad_mixed * att[head].astype(jnp.float32), axis=1, keepdims=True)
         logit = jnp.where(lane == experts + which, sums, logit)
     grad_logit[...] = logit * gates[1]
+    ring.deliver(0)
     pair[0].wait_recv()
     pair[1].wait_recv()
     pair[4].wait_recv()
@@ -1120,15 +1169,15 @@
     for which in range(experts - 4, experts):
         put_output_copy(which).wait()
     for sub in range(2):
-        put_outer_copy(0, sub).wait()
-        act_copy(0, sub).wait_send()
-    put_inner_copy(0).wait()
-    slope_copy(0).wait_send()
+        put_inner_copy(sub, sub).wait()
+        act_copy(sub, sub).wait_send()
+        slope_copy(sub, sub).wait_send()
+    ring.finish(0)
     for copy in pair:
         copy.wait_send()
 
 
-def feed(att, gates, tokens, cotangent, norms, output_w, inner_w, outer_w):
+def feed(count, att, gates, tokens, cotangent, norms, output_w, inner_w, outer_w):
     rows, width = tokens.shape
     wide = inner_w.shape[1]
     half = width // 2
@@ -1136,7 +1185,7 @@
     experts, chunks = HEADS * EXP, wide // CHUNK
     V = pltpu.VMEM
     return pl.pallas_call(
-        feed_kernel,
+        functools.partial(feed_kernel, count),
         out_shape=[
             jax.ShapeDtypeStruct((rows, width), bf),
             jax.ShapeDtypeStruct((rows, width), f32),
@@ -1145,32 +1194,35 @@
             jax.ShapeDtypeStruct((8, width), f32),
             jax.ShapeDtypeStruct((VCOLS, half), bf),
             jax.ShapeDtypeStruct((width, wide // 2), bf),
-            jax.ShapeDtypeStruct((wide, half), bf),
+            jax.ShapeDtypeStruct((wide // count, width), f32),
         ],
         in_specs=[VMEM] * 5 + [ANY] * 3,
         out_specs=[VMEM] * 5 + [ANY] * 3,
         scratch_shapes=[
             V((experts, LANES, width), bf), V((2, width, CHUNK), bf), V((2, CHUNK, width), bf),
-            V((2, rows, CHUNK), bf), V((chunks, rows, CHUNK), bf), V((2, rows, CHUNK), bf), V((chunks // 2, rows, CHUNK), bf),
+            V((2, rows, CHUNK), bf), V((chunks, rows, CHUNK), bf), V((2, rows, CHUNK), bf), V((chunks, rows, CHUNK // 2), bf),
             V((rows, width), bf), V((rows, width), bf), V((width, 2 * rows), bf), V((rows, half), bf), V((half, 2 * rows), bf),
             V((rows, width), f32), V((rows, width), f32), V((rows, width), f32),
             V((rows, width), bf), V((rows, half), bf), V((half, 2 * rows), bf), V((HEADS, rows, LANES), bf), V((rows, LANES), f32),
-            V((2, CHUNK, half), bf), V((width, CHUNK), bf), V((4, LANES, half), bf),
-            DMA((experts,)), DMA((2,)), DMA((2,)), DMA((5,)), DMA((5,)), DMA((2,)), DMA((chunks,)), DMA((1,)), DMA((chunks // 2,)),
-            DMA((2,)), DMA((1,)), DMA((4,)),
-        ],
-        compiler_params=pltpu.CompilerParams(collective_id=4, has_side_effects=True, vmem_limit_bytes=62 << 20),
+            V((2, width, CHUNK // 2), bf), V((4, LANES, half), bf),
+            DMA((experts,)), DMA((2,)), DMA((2,)), DMA((5,)), DMA((5,)), DMA((2,)), DMA((chunks,)), DMA((2,)), DMA((chunks,)),
+            DMA((2,)), DMA((4,)),
+        ]
+        + Scatter.scratch(count, (SPLITS["outer"],), [wide // count]),
+        compiler_params=pltpu.CompilerParams(collective_id=4, has_side_effects=True, vmem_limit_bytes=63 << 20),
     )(att, gates, tokens, cotangent, norms, output_w, inner_w, outer_w)
 
 
-def settle_kernel(count, back, experts, gates, grad_logit, tokens, joint, grad_residual, grad_norms,
-                  grad_tokens, joint_out, grads, grads_in, tokens_in, tokens_t, norms_in, norm_columns, *refs):
-    splits = (SPLITS["joint"],)
+def settle_kernel(count, back, experts, gates, grad_logit, tokens, joint, grad_residual, grad_norms, part_output,
+                  grad_tokens, joint_out, output_out, grads, grads_in, tokens_in, tokens_t, norms_in, norm_columns, *refs):
+    splits = (SPLITS["joint"], SPLITS["output"])
     pair_s, pair_r = refs[-2:]
-    ring = Scatter(count, splits, [], [joint_out], refs[:7], refs[7:-2])
+    half, output_half = JOINT // 2, part_output.shape[2]
+    outs = [(joint_out, half, 0), (output_out, output_half, 0)]
+    ring = Scatter(count, splits, [None, (part_output, 0)], outs, refs[:14], refs[14:-2])
+    ring.start(1)
     enter(ring.neighbours())
     core = ring.core
-    half = JOINT // 2
 
     def remote(src, dst, i):
         return pltpu.make_async_remote_copy(src, dst, pair_s.at[i], pair_r.at[i], device_id=ring.core_mate, device_id_type=MESH)
@@ -1180,6 +1232,7 @@
     pair = [remote(tokens, tokens_in, 0), remote(grad_norms, norms_in, 1), remote(grads.at[:, yours], grads_in, 2)]
     pair[0].start()
     pair[1].start()
+    ring.all_ready(1)
     rows = tokens.shape[0]
     lane = lax.broadcasted_iota(jnp.int32, (LANES, LANES), 1)
     width = HEADS * EXP
@@ -1202,6 +1255,7 @@
 
     lax.fori_loop(0, rows // LANES, assemble, 0)
     pair[2].start()
+    ring.step(1, ring.far)
     tokens_t[:, :rows] = tokens[...].T
     for copy in pair[:2]:
         copy.wait_recv()
@@ -1227,31 +1281,74 @@
 
     for rel in ring.order():
         fill(rel)
-    events = ring.events()
-    for event in events[:2]:
-        event()
-    grad_tokens[...] = grad_residual[...] + contract(grads[...], joint[...], 1, 1)
-    for event in events[2:]:
-        event()
+        ring.ready(0, rel)
+    ring.step(0, ring.far)
+    for D in range(ring.far - 1, 0, -1):
+        ring.step(1, D)
+        ring.step(0, D)
+        if D == ring.far - 1:
+            grad_tokens[...] = grad_residual[...] + contract(grads[...], joint[...], 1, 1)
+    ring.step(1, 0)
+    ring.step(0, 0)
+    ring.deliver(1)
+    ring.deliver(0)
+    ring.finish(1)
+    ring.finish(0)
     for copy in pair:
         copy.wait_send()
 
 
-def settle(count, back, experts, gates, grad_logit, tokens, joint, grad_residual, grad_norms):
+def settle(count, back, experts, gates, grad_logit, tokens, joint, grad_residual, grad_norms, part_output):
     rows, width = tokens.shape
     shard_rows = width // count
     f32, bf = jnp.float32, jnp.bfloat16
     V = pltpu.VMEM
     return pl.pallas_call(
         functools.partial(settle_kernel, count),
-        out_shape=[jax.ShapeDtypeStruct((rows, width), f32), jax.ShapeDtypeStruct((shard_rows, JOINT), f32)],
-        in_specs=[VMEM] * 8,
-        out_specs=[VMEM] * 2,
+        out_shape=[jax.ShapeDtypeStruct((rows, width), f32), jax.ShapeDtypeStruct((shard_rows, JOINT), f32),
+                   jax.ShapeDtypeStruct((part_output.shape[1], width), f32)],
+        in_specs=[VMEM] * 8 + [ANY],
+        out_specs=[VMEM, VMEM, ANY],
         scratch_shapes=[V((rows, JOINT), bf), V((rows, JOINT // 2), bf), V((rows, width), bf), V((width, 2 * rows), bf), V((8, width), f32), V((width, LANES), f32)]
-        + Scatter.scratch(count, (SPLITS["joint"],), [shard_rows])
+        + Scatter.scratch(count, (SPLITS["joint"], SPLITS["output"]), [shard_rows, part_output.shape[1]])
         + [DMA((3,)), DMA((3,))],
         compiler_params=pltpu.CompilerParams(collective_id=5, has_side_effects=True, vmem_limit_bytes=60 << 20),
-    )(back, experts, gates, grad_logit, tokens, joint, grad_residual, grad_norms)
+    )(back, experts, gates, grad_logit, tokens, joint, grad_residual, grad_norms, part_output)
+
+
+def publish_kernel(joint_w, output_w, inner_w, outer_w, layer, tokens_in,
+                   query, key, value, value_router, output_router, norms, output_out, inner_out, outer_out, layer_out, tokens_out, sems):
+    half, small = inner_w.shape[1] // 2, CHUNK // 2
+    copies = [(output_w, output_out), (outer_w, outer_out), (layer, layer_out), (tokens_in, tokens_out)]
+    for core in range(2):
+        for chunk in range(half // small):
+            copies.append((inner_w.at[:, pl.ds(core * half + chunk * small, small)],
+                           inner_out.at[:, pl.ds(chunk * CHUNK + core * small, small)]))
+    copies = [pltpu.make_async_copy(src, dst, sems.at[i]) for i, (src, dst) in enumerate(copies)]
+    for copy in copies:
+        copy.start()
+    query[...] = joint_w[:, :QCOLS]
+    key[...] = joint_w[:, QCOLS : 2 * QCOLS]
+    value[...] = joint_w[:, 2 * QCOLS : ROUTERS]
+    value_router[...] = joint_w[:, ROUTERS : ROUTERS + HEADS * EXP]
+    output_router[...] = joint_w[:, ROUTERS + HEADS * EXP : NORM]
+    norms[...] = joint_w[:, NORM : NORM + 2]
+    for copy in copies:
+        copy.wait()
+
+
+def publish(joint_w, output_w, inner_w, outer_w, layer, tokens):
+    rows = joint_w.shape[0]
+    f32 = jnp.float32
+    columns = [QCOLS, QCOLS, VCOLS, HEADS * EXP, HEADS * EXP, 2]
+    rest = (output_w, inner_w, outer_w, layer, tokens)
+    return pl.pallas_call(
+        publish_kernel,
+        out_shape=[jax.ShapeDtypeStruct((rows, c), f32) for c in columns] + [jax.ShapeDtypeStruct(x.shape, x.dtype) for x in rest],
+        in_specs=[VMEM] + [ANY] * 5,
+        out_specs=[VMEM] * 6 + [ANY] * 5,
+        scratch_shapes=[DMA((4 + inner_w.shape[1] // (CHUNK // 2),))],
+    )(joint_w, *rest)
 
 
 def on_device(
@@ -1265,22 +1362,21 @@
         [value_router, output_router, norm_gain[:, None], norm_bias[:, None],
          jnp.zeros((query_weight.shape[0], JOINT - NORM - 2), jnp.bfloat16)], axis=1)
     routes = jnp.concatenate([value_routes[0].reshape(rows, -1), output_routes[0].reshape(rows, -1)], axis=1)
-    joint, qkv, experts, gates, norms, tables, turned = project(
-        count, query_weight, key_weight, value_weight, routers, inputs, routes, cont_gap)
-    splits = tuple(SPLITS[name] for name in ("output", "inner", "outer"))
-    att, store, outputs, logs, output_full, inner_full, outer_full = attend(
-        count, qkv, tables, (output_weight, inner_weight, outer_weight), splits)
-    layer_out, grad_residual, grad_att, grad_logit, grad_norms, *parts = feed(
-        att, gates, inputs, cotangent[0], norms, output_full.reshape(VCOLS, width), inner_full.reshape(width, -1),
+    joint, output_full, qkv, experts, gates, norms, tables, turned = project(
+        count, query_weight, key_weight, value_weight, routers, inputs, routes, output_weight, cont_gap)
+    att, store, outputs, logs, inner_full, outer_full = attend(
+        count, qkv, tables, (inner_weight, outer_weight), (SPLITS["inner"], SPLITS["outer"]))
+    layer, grad_residual, grad_att, grad_logit, grad_norms, part_output, part_inner, outer_w = feed(
+        count, att, gates, inputs, cotangent[0], norms, output_full.reshape(VCOLS, width), inner_full.reshape(width, -1),
         outer_full.reshape(-1, width))
-    parts = tuple(part.reshape(count, -1, part.shape[1]) for part in parts)
-    back, out_w, in_w, outer_w = retreat(count, grad_att, turned, store, outputs, logs, parts, splits)
-    grad_input, joint_w = settle(count, back, experts, gates, grad_logit, inputs, joint, grad_residual, grad_norms)
-    return (
-        layer_out[None], grad_input[None], joint_w[:, :QCOLS], joint_w[:, QCOLS : 2 * QCOLS], joint_w[:, 2 * QCOLS : ROUTERS],
-        joint_w[:, ROUTERS : ROUTERS + HEADS * EXP], joint_w[:, ROUTERS + HEADS * EXP : NORM], out_w, joint_w[:, NORM],
-        joint_w[:, NORM + 1], in_w, outer_w,
-    )
+    back, inner_w = retreat(
+        count, grad_att, turned, store, outputs, logs, part_inner.reshape(count, -1, part_inner.shape[1]), INNER_PARTS)
+    grad_input, joint_w, output_w = settle(
+        count, back, experts, gates, grad_logit, inputs, joint, grad_residual, grad_norms,
+        part_output.reshape(count, -1, part_output.shape[1]))
+    query, key, value, value_r, output_r, norm_w, output_w, inner_w, outer_w, layer, grad_input = publish(
+        joint_w, output_w, inner_w, outer_w, layer, grad_input)
+    return (layer[None], grad_input[None], query, key, value, value_r, output_r, output_w, norm_w[:, 0], norm_w[:, 1], inner_w, outer_w)
 
 
 def solution(mesh):

time: 511 us -> 771 us (1.51)
  Pallas kernels: 468 us -> 743 us
  local copies, waits for them, and re-layouts: 31.7 us -> 21.3 us
    pallas_call x1 -> x2, Pallas kernels: 61.3 us -> 372 us  [the longest x1 261 us: publish(): pl.pallas_call(publish_kernel, out_shape=[jax.ShapeDtypeStruct((rows, c),...]
    pallas_call x1, Pallas kernels: 155 us -> 109 us  [retreat(): pl.pallas_call(functools.partial(retreat_kernel, count, splits, steps), o...]
    pallas_call x1, Pallas kernels: 52.4 us -> 70.3 us  [project(): pl.pallas_call(functools.partial(project_kernel, count), out_shape=[jax.S...]
    unnamed x25 -> x12, local copies, waits for them, and re-layouts: 21.2 us -> 15 us
where the time goes in v2:
time: 771 us; the launch traced here: 765 us
  Pallas kernels  743 us (96%)
  local copies, waits for them, and re-layouts  21.3 us (3%)
    pallas_call x1, Pallas kernels, publish(): pl.pallas_call(publish_kernel, out_shape=[jax.ShapeDtypeStruct((rows, c),...  261 us
    pallas_call x1, Pallas kernels, attend(): pl.pallas_call(functools.partial(attend_kernel, count, splits, steps), ou...  114 us
    pallas_call x1, Pallas kernels, feed(): pl.pallas_call(functools.partial(feed_kernel, count), out_shape=[jax.Shap...  111 us
    pallas_call x1, Pallas kernels, retreat(): pl.pallas_call(functools.partial(retreat_kernel, count, splits, steps), o...  109 us
    pallas_call x1, Pallas kernels, settle(): pl.pallas_call(functools.partial(settle_kernel, count), out_shape=[jax.Sh...  77.1 us
    pallas_call x1, Pallas kernels, project(): pl.pallas_call(functools.partial(project_kernel, count), out_shape=[jax.S...  70.3 us

profile of v2, /device:TPU:0, one launch (start us, length us, event | category | flops | bytes accessed | tf_op | source)
XLA Modules:
  0.0 765.0 jit_solution(12300276637615982957)
XLA Ops:
  0.6 0.7 reshape_squeeze.6
  1.4 0.7 reshape_squeeze.7
  2.1 0.8 copy.55
  2.9 0.8 copy.56
  3.8 0.8 copy.57
  4.5 0.8 copy.58
  5.3 0.8 concatenate.6.routers
  6.1 1.7 copy.59.query
  7.8 1.7 copy.60.key
  9.4 0.8 copy.62.routes
  10.3 2.1 copy.61.value
  12.4 70.3 %shard_map.238 = (bf16[1024,3328]{1,0:T(8,128)(2,1)}, bf16[8,280,1024]{2,1,0:T(8,128)(2,1)}, bf16[4,3,512,128]{3,2,1,0:T(8,128)(2,1)}, bf16[20,512,128]{2,1,0:T(...) custom-call(bf16[128,448]{1,0:T(8,128)(2,1)} %copy.59.query, ...), custom_call_target="tpu_custom_call" | custom-call | tf_op jit(solution)/shard_map/pallas_call | solution.py:312
  82.7 113.9 %shard_map.239 = (bf16[4,512,128]{2,1,0:T(8,128)(2,1)}, bf16[7,2048,128]{2,1,0:T(8,128)(2,1)}, f32[2048,128]{1,0:T(8,128)}, f32[8,2048]{1,0:T(8,128)}, bf16[8,12...) custom-call(bf16[4,3,512,128]{3,2,1,0:T(8,128)(2,1)} %get-tuple-element.50.qkv, ...), custom_call_target="tpu_custom_call" | custom-call | tf_op jit(solution)/shard_map/pallas_call | solution.py:534
  196.6 111.2 %shard_map.240 = (bf16[512,1024]{1,0:T(8,128)(2,1)}, f32[512,1024]{1,0:T(8,128)}, bf16[4,512,128]{2,1,0:T(8,128)(2,1)}, f32[512,128]{1,0:T(8,128)}, f32[8,1024]{...) custom-call(bf16[4,512,128]{2,1,0:T(8,128)(2,1)} %get-tuple-element.52.att, ...), custom_call_target="tpu_custom_call" | custom-call | tf_op jit(solution)/shard_map/pallas_call | solution.py:1187
  307.9 109.0 %shard_map.241 = (bf16[4,3,512,128]{3,2,1,0:T(8,128)(2,1)}, f32[128,4096]{1,0:T(8,128)}) custom-call(bf16[4,512,128]{2,1,0:T(8,128)(2,1)} %get-tuple-element.58.grad_att, f32[3,128,5632]{2,1,0:T(8,128)} %get-tuple-element.59.turned, bf16[7,2048,128]{2,1,0:T(8,128)(2,1)} %get-tuple-element.60.store, f32[2048,128]{1,0:T(8,128)} %get-tuple-element.61.outputs, ...), custom_call_target="tpu_custom_call" | custom-call | tf_op jit(solution)/shard_map/pallas_call | solution.py:912
  416.8 77.1 %shard_map.242 = (f32[512,1024]{1,0:T(8,128)}, f32[128,3328]{1,0:T(8,128)}, f32[280,1024]{1,0:T(8,128)}) custom-call(bf16[4,3,512,128]{3,2,1,0:T(8,128)(2,1)} %get-tuple-element.64.back, bf16[20,512,128]{2,1,0:T(8,128)(2,1)} %get-tuple-element.65.experts, f32[2,512,128]{2,1,0:T(8,128)} %get-tuple-element.53.gates, f32[512,128]{1,0:T(8,128)} %get-tuple-element.66.grad_logit, ...), custom_call_target="tpu_custom_call" | custom-call | tf_op jit(solution)/shard_map/pallas_call | solution.py:1306
  494.0 261.1 %shard_map.243 = (f32[128,448]{1,0:T(8,128)}, f32[128,448]{1,0:T(8,128)}, f32[128,2240]{1,0:T(8,128)}, f32[128,20]{1,0:T(8,128)}, f32[128,20]{1,0:T(8,128)}, /*i...) custom-call(f32[128,3328]{1,0:T(8,128)} %get-tuple-element.71.joint_, ...), custom_call_target="tpu_custom_call" | custom-call | tf_op jit(solution)/shard_map/pallas_call | solution.py:1345
  755.0 0.0 copy-start
  755.1 1.7 slice_reduce_fusion
  756.7 1.5 copy.66
  758.2 1.5 copy.67
  759.7 1.8 copy.63
  761.5 1.8 copy.64
  763.3 0.0 copy-done
  763.3 1.4 copy.65
  (2 shorter events, 0.0 us)
Async XLA Ops:
  755.0 8.2 %copy-start = (f32[128,2240]{1,0:T(8,128)S(1)}, f32[128,2240]{1,0:T(8,128)}, u32[]{:S(2)}) copy-start(f32[128,2240]{1,0:T(8,128)} %get-tuple-element.116) | copy-start | bytes 3440644

commit v3 on v2

--- a/solution.py
+++ b/solution.py
@@ -321,7 +321,7 @@
             jax.ShapeDtypeStruct((3, LANES, TABLE), f32),
             jax.ShapeDtypeStruct((3, LANES, TABLE), f32),
         ],
-        in_specs=[VMEM] * 6 + [ANY, SMEM],
+        in_specs=[VMEM] * 7 + [SMEM],
         out_specs=[VMEM, ANY] + [VMEM] * 6,
         scratch_shapes=[pltpu.VMEM((shard_rows, JOINT), bf), pltpu.VMEM((rows, JOINT), f32)] + Gather.sems(count, 2),
         compiler_params=pltpu.CompilerParams(collective_id=1, has_side_effects=True, vmem_limit_bytes=56 << 20),
@@ -540,7 +540,7 @@
             jax.ShapeDtypeStruct((8, own), jnp.float32),
         ]
         + [jax.ShapeDtypeStruct((count,) + w.shape, w.dtype) for w in shards],
-        in_specs=[VMEM, VMEM] + [ANY] * T,
+        in_specs=[VMEM] * (2 + T),
         out_specs=[VMEM] * 4 + [ANY] * T,
         scratch_shapes=[
             pltpu.VMEM((own, LANES), jnp.float32),
@@ -1317,15 +1317,12 @@
 
 
 def publish_kernel(joint_w, output_w, inner_w, outer_w, layer, tokens_in,
-                   query, key, value, value_router, output_router, norms, output_out, inner_out, outer_out, layer_out, tokens_out, sems):
-    half, small = inner_w.shape[1] // 2, CHUNK // 2
-    copies = [(output_w, output_out), (outer_w, outer_out), (layer, layer_out), (tokens_in, tokens_out)]
-    for core in range(2):
-        for chunk in range(half // small):
-            copies.append((inner_w.at[:, pl.ds(core * half + chunk * small, small)],
-                           inner_out.at[:, pl.ds(chunk * CHUNK + core * small, small)]))
-    copies = [pltpu.make_async_copy(src, dst, sems.at[i]) for i, (src, dst) in enumerate(copies)]
-    for copy in copies:
+                   query, key, value, value_router, output_router, norms, output_out, inner_out, outer_out, layer_out, tokens_out,
+                   *refs):
+    held, load, store = refs[:-2], refs[-2], refs[-1]
+    sources = (tokens_in, inner_w, outer_w, layer, output_w)
+    loads = [pltpu.make_async_copy(src, buf, load.at[i]) for i, (src, buf) in enumerate(zip(sources, held))]
+    for copy in loads:
         copy.start()
     query[...] = joint_w[:, :QCOLS]
     key[...] = joint_w[:, QCOLS : 2 * QCOLS]
@@ -1333,7 +1330,19 @@
     value_router[...] = joint_w[:, ROUTERS : ROUTERS + HEADS * EXP]
     output_router[...] = joint_w[:, ROUTERS + HEADS * EXP : NORM]
     norms[...] = joint_w[:, NORM : NORM + 2]
-    for copy in copies:
+    half, small = inner_w.shape[1] // 2, CHUNK // 2
+    stores = []
+    for i, target in enumerate((tokens_out, inner_out, outer_out, layer_out, output_out)):
+        loads[i].wait()
+        pairs = [(held[i], target)]
+        if i == 1:
+            pairs = [(held[i].at[:, pl.ds(core * half + chunk * small, small)], target.at[:, pl.ds(chunk * CHUNK + core * small, small)])
+                     for core in range(2) for chunk in range(half // small)]
+        for src, dst in pairs:
+            copy = pltpu.make_async_copy(src, dst, store.at[len(stores)])
+            copy.start()
+            stores.append(copy)
+    for copy in stores:
         copy.wait()
 
 
@@ -1347,7 +1356,9 @@
         out_shape=[jax.ShapeDtypeStruct((rows, c), f32) for c in columns] + [jax.ShapeDtypeStruct(x.shape, x.dtype) for x in rest],
         in_specs=[VMEM] + [ANY] * 5,
         out_specs=[VMEM] * 6 + [ANY] * 5,
-        scratch_shapes=[DMA((4 + inner_w.shape[1] // (CHUNK // 2),))],
+        scratch_shapes=[pltpu.VMEM(x.shape, x.dtype) for x in (tokens, inner_w, outer_w, layer, output_w)]
+        + [DMA((5,)), DMA((4 + inner_w.shape[1] // (CHUNK // 2),))],
+        compiler_params=pltpu.CompilerParams(vmem_limit_bytes=32 << 20),
     )(joint_w, *rest)
 
 

time: 771 us -> 516 us (0.67)
  Pallas kernels: 743 us -> 486 us
    pallas_call x1, Pallas kernels: 261 us -> 4.44 us  [publish(): pl.pallas_call(publish_kernel, out_shape=[jax.ShapeDtypeStruct((rows, c),...]
    unnamed x12 -> x22, local copies, waits for them, and re-layouts: 15 us -> 18.5 us
where the time goes in v3:
time: 516 us; the launch traced here: 511 us
  Pallas kernels  486 us (94%)
  local copies, waits for them, and re-layouts  23.9 us (5%)
    pallas_call x1, Pallas kernels, attend(): pl.pallas_call(functools.partial(attend_kernel, count, splits, steps), ou...  114 us
    pallas_call x1, Pallas kernels, feed(): pl.pallas_call(functools.partial(feed_kernel, count), out_shape=[jax.Shap...  111 us
    pallas_call x1, Pallas kernels, retreat(): pl.pallas_call(functools.partial(retreat_kernel, count, splits, steps), o...  108 us
    pallas_call x1, Pallas kernels, settle(): pl.pallas_call(functools.partial(settle_kernel, count), out_shape=[jax.Sh...  76.9 us
    pallas_call x1, Pallas kernels, project(): pl.pallas_call(functools.partial(project_kernel, count), out_shape=[jax.S...  70.4 us
    unnamed x22, local copies, waits for them, and re-layouts  18.5 us

profile of v3, /device:TPU:0, one launch (start us, length us, event | category | flops | bytes accessed | tf_op | source)
XLA Modules:
  0.0 510.6 jit_solution(8518521391628594653)
XLA Ops:
  0.6 0.7 reshape_squeeze.6
  1.4 0.7 reshape_squeeze.7
  2.1 0.8 copy.55
  2.9 0.8 copy.56
  3.8 0.8 copy.57
  4.5 0.8 copy.58
  5.3 0.8 concatenate.6.routers
  6.1 1.7 copy.59.query
  7.8 1.7 copy.60.key
  9.4 0.8 copy.62.routes
  10.3 2.1 copy.61.value
  12.4 70.4 %shard_map.238 = (bf16[1024,3328]{1,0:T(8,128)(2,1)}, bf16[8,280,1024]{2,1,0:T(8,128)(2,1)}, bf16[4,3,512,128]{3,2,1,0:T(8,128)(2,1)}, bf16[20,512,128]{2,1,0:T(...) custom-call(bf16[128,448]{1,0:T(8,128)(2,1)} %copy.59.query, ...), custom_call_target="tpu_custom_call" | custom-call | tf_op jit(solution)/shard_map/pallas_call | solution.py:312
  82.8 114.4 %shard_map.239 = (bf16[4,512,128]{2,1,0:T(8,128)(2,1)}, bf16[7,2048,128]{2,1,0:T(8,128)(2,1)}, f32[2048,128]{1,0:T(8,128)}, f32[8,2048]{1,0:T(8,128)}, bf16[8,12...) custom-call(bf16[4,3,512,128]{3,2,1,0:T(8,128)(2,1)} %get-tuple-element.50.qkv, ...), custom_call_target="tpu_custom_call" | custom-call | tf_op jit(solution)/shard_map/pallas_call | solution.py:534
  197.2 111.2 %shard_map.240 = (bf16[512,1024]{1,0:T(8,128)(2,1)}, f32[512,1024]{1,0:T(8,128)}, bf16[4,512,128]{2,1,0:T(8,128)(2,1)}, f32[512,128]{1,0:T(8,128)}, f32[8,1024]{...) custom-call(bf16[4,512,128]{2,1,0:T(8,128)(2,1)} %get-tuple-element.52.att, ...), custom_call_target="tpu_custom_call" | custom-call | tf_op jit(solution)/shard_map/pallas_call | solution.py:1187
  308.4 108.3 %shard_map.241 = (bf16[4,3,512,128]{3,2,1,0:T(8,128)(2,1)}, f32[128,4096]{1,0:T(8,128)}) custom-call(bf16[4,512,128]{2,1,0:T(8,128)(2,1)} %get-tuple-element.58.grad_att, f32[3,128,5632]{2,1,0:T(8,128)} %get-tuple-element.59.turned, bf16[7,2048,128]{2,1,0:T(8,128)(2,1)} %get-tuple-element.60.store, f32[2048,128]{1,0:T(8,128)} %get-tuple-element.61.outputs, ...), custom_call_target="tpu_custom_call" | custom-call | tf_op jit(solution)/shard_map/pallas_call | solution.py:912
  416.6 0.0 copy-start
  416.6 76.9 %shard_map.242 = (f32[512,1024]{1,0:T(8,128)}, f32[128,3328]{1,0:T(8,128)}, f32[280,1024]{1,0:T(8,128)}) custom-call(bf16[4,3,512,128]{3,2,1,0:T(8,128)(2,1)} %get-tuple-element.64.back, bf16[20,512,128]{2,1,0:T(8,128)(2,1)} %get-tuple-element.65.experts, f32[2,512,128]{2,1,0:T(8,128)} %get-tuple-element.53.gates, f32[512,128]{1,0:T(8,128)} %get-tuple-element.66.grad_logit, ...), custom_call_target="tpu_custom_call" | custom-call | tf_op jit(solution)/shard_map/pallas_call | solution.py:1306
  493.5 0.0 copy-done
  493.5 0.0 copy-start.1
  493.6 1.6 copy-done.1
  495.1 0.0 copy-start.2
  495.1 1.6 copy-done.2
  496.7 0.0 copy-start.3
  496.7 1.5 copy-done.3
  498.2 0.0 copy-start.4
  498.2 1.3 copy-done.4
  499.4 0.0 copy-start.5
  499.4 1.2 copy-done.5
  500.7 4.4 shard_map.243
  505.1 0.7 slice_reduce_fusion
  505.8 0.7 copy.66
  506.5 0.7 copy.67
  507.2 0.8 copy.63
  508.0 0.8 copy.64
  508.8 1.4 copy.65
  (2 shorter events, 0.0 us)
Async XLA Ops:
  416.6 76.9 %copy-start = (f32[512,1024]{1,0:T(8,128)S(1)}, f32[512,1024]{1,0:T(8,128)}, u32[]{:S(2)}) copy-start(f32[512,1024]{1,0:T(8,128)} %get-tuple-element.74.outer_w) | copy-start | bytes 6291460
  493.5 1.6 copy-start.1
  495.1 1.6 copy-start.2
  496.7 1.5 copy-start.3
  498.2 1.3 copy-start.4
  499.4 1.2 copy-start.5

commit v4 on v3

--- a/solution.py
+++ b/solution.py
@@ -29,7 +29,7 @@
 NORM = ROUTERS + 2 * HEADS * EXP
 JOINT = 3328
 SPLITS = {"joint": (640, 512), "output": (256, 128), "inner": (768, 640), "outer": (256, 128)}
-INNER_PARTS = ((512, 256), (512, 256))
+INNER_PARTS = ((512, 768),)
 
 
 def ring_place(index, count):
@@ -200,8 +200,9 @@
     return hit.astype(jnp.float32)
 
 
-def project_kernel(count, query, key, value, routers, tokens, routes, output_shard, gaps, joint, output_w, qkv, experts, gates, norms, tables, turned_tables,
-                   shard, product, send, recv, local):
+def project_kernel(count, query, key, value, value_router, output_router, norm, tokens, routes, output_shard, gaps,
+                   joint, output_w, qkv, experts, gates, norms, tables, turned_tables,
+                   shard, query_v, key_v, value_v, routers_v, product, load, send, recv, local):
     rows = shard.shape[0]
     splits = (SPLITS["joint"], SPLITS["output"])
 
@@ -211,8 +212,18 @@
         return joint.at[pl.ds(pl.multiple_of(g * rows, rows), rows), cols]
 
     ring = Gather(count, splits, [shard, output_shard], at, send, recv, local)
-    wide = jnp.concatenate([ref[...].astype(jnp.float32) for ref in (query, key, value, routers)], axis=1)
-    shard[...] = wide.astype(jnp.bfloat16)
+    loads = [(query, query_v), (key, key_v), (value, value_v), (value_router, routers_v.at[0]), (output_router, routers_v.at[1])]
+    loads = [pltpu.make_async_copy(src, dst, load.at[i]) for i, (src, dst) in enumerate(loads)]
+    for copy in loads:
+        copy.start()
+    for copy in loads:
+        copy.wait()
+    turned_norm = jnp.concatenate([norm[...].astype(jnp.float32), jnp.zeros((LANES - 2, rows), jnp.float32)], axis=0).T
+    wide = [ref[...].astype(jnp.float32) for ref in (query_v, key_v, value_v)]
+    wide += [routers_v[0].astype(jnp.float32), routers_v[1].astype(jnp.float32), turned_norm[:, : JOINT - NORM]]
+    if JOINT - NORM > LANES:
+        wide.append(jnp.zeros((rows, JOINT - NORM - LANES), jnp.float32))
+    shard[...] = jnp.concatenate(wide, axis=1).astype(jnp.bfloat16)
     enter(ring.neighbours())
     ring.start(0)
     slope = jnp.float32(0.0)
@@ -239,7 +250,7 @@
                 target[which, :, pl.ds(start, 256)] = rolled[:, LANES:]
         return carry
 
-    late = max(1, ring.far - 1)
+    late = 1
     steps, later = [], []
     for k in range(1, ring.far + 1):
         steps.append(functools.partial(ring.arrive, 0, k))
@@ -252,8 +263,7 @@
             later.append(functools.partial(ring.plane_arrive, 1, k - 1))
     steps += [functools.partial(ring.plane_arrive, 0, ring.far), functools.partial(ring.finish, 0)]
     later += [functools.partial(ring.plane_arrive, 1, ring.far)]
-    early = later[:1]
-    later = later[1:]
+    early, later = later[:3], later[3:]
     steps = steps[:-1] + early + steps[-1:]
     cut = max(1, TABLE // 256 // len(steps))
     done = 0
@@ -306,9 +316,10 @@
     ring.finish(1)
 
 
-def project(count, query, key, value, routers, tokens, routes, output_shard, gaps):
+def project(count, query, key, value, value_router, output_router, norm, tokens, routes, output_shard, gaps):
     rows, (shard_rows, _) = tokens.shape[0], query.shape
     f32, bf = jnp.float32, jnp.bfloat16
+    V = pltpu.VMEM
     return pl.pallas_call(
         functools.partial(project_kernel, count),
         out_shape=[
@@ -321,11 +332,15 @@
             jax.ShapeDtypeStruct((3, LANES, TABLE), f32),
             jax.ShapeDtypeStruct((3, LANES, TABLE), f32),
         ],
-        in_specs=[VMEM] * 7 + [SMEM],
+        in_specs=[ANY] * 5 + [VMEM] * 4 + [SMEM],
         out_specs=[VMEM, ANY] + [VMEM] * 6,
-        scratch_shapes=[pltpu.VMEM((shard_rows, JOINT), bf), pltpu.VMEM((rows, JOINT), f32)] + Gather.sems(count, 2),
-        compiler_params=pltpu.CompilerParams(collective_id=1, has_side_effects=True, vmem_limit_bytes=56 << 20),
-    )(query, key, value, routers, tokens, routes, output_shard, gaps)
+        scratch_shapes=[
+            V((shard_rows, JOINT), bf), V(query.shape, bf), V(key.shape, bf), V(value.shape, bf), V((2,) + value_router.shape, bf),
+            V((rows, JOINT), f32), DMA((5,)),
+        ]
+        + Gather.sems(count, 2),
+        compiler_params=pltpu.CompilerParams(collective_id=1, has_side_effects=True, vmem_limit_bytes=62 << 20),
+    )(query, key, value, value_router, output_router, norm, tokens, routes, output_shard, gaps)
 
 
 def seq_mates(ring):
@@ -358,6 +373,16 @@
     return source, active, table, column
 
 
+STRIP = 512
+
+
+def near_first(ring, j):
+    odd, high = j % 2, j // 2
+    core = ring.core + odd - 2 * ring.core * odd
+    plane = ring.plane + high - 2 * ring.plane * high
+    return 2 * plane + core
+
+
 def block_rows(block):
     return pl.ds(pl.multiple_of(block * BLOCK, BLOCK), BLOCK)
 
@@ -395,10 +420,10 @@
     top[...] = jnp.full_like(top, NEGATIVE)
 
     def far_rows(piece, chunk):
-        return store.at[pl.ds(3 + 2 * piece, 2), block_rows(chunk)]
+        return store.at[pl.ds(3 + 2 * piece, 2), block_rows(near_first(ring, chunk))]
 
     def first_hop(chunk, way):
-        src = store.at[pl.ds(1, 2), block_rows(chunk)]
+        src = store.at[pl.ds(1, 2), block_rows(near_first(ring, chunk))]
         piece = slot % 2
         return remote(src, far_rows(piece, chunk), sh_send.at[4 * way + chunk], sh_recv.at[4 * piece + chunk],
                       x_mate if way == 0 else z_mate)
@@ -433,48 +458,62 @@
             remote(far_rows(piece, chunk), far_rows(piece, chunk), sh_send.at[chunk], sh_recv.at[4 * piece + chunk], x_mate).wait_recv()
 
     own_copy.wait()
-    share(seq)
-    for mate in mates:
+    share(0)
+    for chunk, mate in enumerate(mates):
         other = mate[0]
         src = store.at[pl.ds(1, 2), block_rows(other)]
         remote(src, src, kv_send.at[other], kv_recv.at[other], mate).wait_recv()
-        share(other)
+        share(1 + chunk)
     for mate in mates:
         src = store.at[0, block_rows(mate[0])]
         remote(src, src, q_send.at[mate[0]], q_recv.at[mate[0]], mate).wait_recv()
 
-    def tile(step):
-        phase, key_block, query_block = step // 16, (step // 4) % 4, step % 4
+    def tile(source, table, column, key_block, first, rows):
+        keys = store[1 + 2 * source, block_rows(key_block), :]
+        values = store[2 + 2 * source, block_rows(key_block), :]
+        for strip in range(rows // STRIP):
+            part = pl.ds(pl.multiple_of(first + strip * STRIP, STRIP), STRIP)
+            scores = lax.dot_general(store[0, part, :], keys, (((1,), (1,)), ((), ())), preferred_element_type=jnp.float32)
+            start = column + TABLE_ZERO - strip * STRIP
+            bias = [tables[table, :, pl.ds(pl.multiple_of(start - LANES * i, LANES), BLOCK)] for i in range(STRIP // LANES)]
+            scores = scores * (DH**-0.5 * LOG2E) + jnp.concatenate(bias, axis=0)
+            before = top[part, :]
+            after = jnp.maximum(before, jnp.max(scores, axis=1, keepdims=True))
+            terms = jnp.exp2(scores - after[:, :1])
+            acc[part, :] = acc[part, :] * jnp.exp2(before - after) + jnp.dot(
+                terms.astype(jnp.bfloat16), values, preferred_element_type=jnp.float32)
+            top[part, :] = after
+
+    def near_tile(step):
+        key_block, query_block = near_first(ring, step // 4), step % 4
+        source, active, table, column = tile_place(slot, seq, 0, key_block, query_block)
+
+        @pl.when(active)
+        def _():
+            tile(source, table, column, key_block, query_block * BLOCK, BLOCK)
+
+    def far_tile(step):
+        phase, key_block, query_block = step // 8, near_first(ring, (step // 2) % 4), 2 * (step % 2)
         source, active, table, column = tile_place(slot, seq, phase, key_block, query_block)
 
         @pl.when(active)
         def _():
-            rows = block_rows(query_block)
-            keys = store[1 + 2 * source, block_rows(key_block), :]
-            values = store[2 + 2 * source, block_rows(key_block), :]
-            scores = lax.dot_general(store[0, rows, :], keys, (((1,), (1,)), ((), ())), preferred_element_type=jnp.float32)
-            bias = jnp.concatenate(
-                [tables[table, :, pl.ds(pl.multiple_of(column + TABLE_ZERO - LANES * part, LANES), BLOCK)] for part in range(BLOCK // LANES)],
-                axis=0,
-            )
-            scores = scores * (DH**-0.5 * LOG2E) + bias
-            before = top[rows, :]
-            after = jnp.maximum(before, jnp.max(scores, axis=1, keepdims=True))
-            factor = jnp.exp2(before - after)
-            terms = jnp.exp2(scores - after[:, :1])
-            acc[rows, :] = acc[rows, :] * factor + jnp.dot(terms.astype(jnp.bfloat16), values, preferred_element_type=jnp.float32)
-            top[rows, :] = after
+            tile(source, table, column, key_block, query_block * BLOCK, 2 * BLOCK)
 
     events = {}
     for chunk in range(4):
-        events.setdefault(4 * chunk, []).append(functools.partial(pass_on, chunk))
-        events.setdefault(32 + 4 * chunk, []).append(functools.partial(last_piece, chunk))
-    begin, gap = steps
-    events.setdefault(begin, []).extend([functools.partial(ring.start, t) for t in range(T)])
+        events.setdefault(4 * chunk + 3, []).append(functools.partial(pass_on, chunk))
+        events.setdefault(24 + 2 * chunk, []).append(functools.partial(last_piece, chunk))
+    begin, first, gap = steps
+    for t in range(T):
+        if begin + t < 0:
+            ring.start(t)
+        else:
+            events.setdefault(begin + t, []).append(functools.partial(ring.start, t))
     rest = []
     for i, event in enumerate(ring.events()):
-        step = begin + gap * (i + 1)
-        if step < 48:
+        step = int(first + gap * i)
+        if step < 32:
             events.setdefault(step, []).append(event)
         else:
             rest.append(event)
@@ -485,10 +524,11 @@
             def _():
                 for action in actions:
                     action()
-        tile(step)
+        pl.when(step < 16)(lambda: near_tile(step))
+        pl.when(step >= 16)(lambda: far_tile(step - 8))
         return carry
 
-    lax.fori_loop(0, 48, step_body, 0)
+    lax.fori_loop(0, 32, step_body, 0)
     total = acc[:, DH : DH + 1]
     result = acc[...] / total
     outputs[...] = result
@@ -527,7 +567,7 @@
             second_hop(chunk).wait_send()
 
 
-def attend(count, qkv, tables, shards, splits, steps=(8, 2)):
+def attend(count, qkv, tables, shards, splits, steps=(0, 18, 2)):
     rows = qkv.shape[2]
     own = 4 * rows
     T = len(shards)
@@ -758,20 +798,18 @@
         sums = jnp.sum(grads[rows, :].astype(jnp.float32) * outputs[rows, :], axis=1, keepdims=True)
         delta[:, rows] = jnp.broadcast_to(sums, (BLOCK, LANES)).T[:8]
 
-    def tile(step):
-        phase, key_block, query_block = step // 16, (step // 4) % 4, step % 4
-        piece = jnp.where(slot == 2, 1 - phase, phase)
-        forward_phase = jnp.where(phase == 2, 0, jnp.where(slot == 3, 2 - piece, 1 + piece))
+    def tile(forward_phase, key_block, query_block, blocks):
         source, active, table, column = tile_place(slot, seq, forward_phase, key_block, query_block)
 
         @pl.when(active)
         def _():
-            rows, key_rows = block_rows(query_block), block_rows(key_block)
+            size = blocks * BLOCK
+            key_rows, rows = block_rows(key_block), pl.ds(pl.multiple_of(query_block * BLOCK, BLOCK), size)
             keys, values = store[1 + 2 * source, key_rows, :], store[2 + 2 * source, key_rows, :]
             queries, tops = store[0, rows, :], grads[rows, :]
             scores = lax.dot_general(keys, queries, (((1,), (1,)), ((), ())), preferred_element_type=jnp.float32)
             bias = jnp.concatenate(
-                [turned[table, :, pl.ds(pl.multiple_of(TURNED_ZERO - column - LANES * part, LANES), BLOCK)] for part in range(BLOCK // LANES)],
+                [turned[table, :, pl.ds(pl.multiple_of(TURNED_ZERO - column - LANES * part, LANES), size)] for part in range(BLOCK // LANES)],
                 axis=0,
             )
             weights = jnp.exp2(scores * (DH**-0.5 * LOG2E) + (bias - logs[:1, rows]))
@@ -781,6 +819,14 @@
             grad_kv[source, 0, key_rows, :] += jnp.dot(grad_scores, queries, preferred_element_type=jnp.float32)
             grad_q[rows, :] += lax.dot_general(grad_scores, keys, (((0,), (0,)), ((), ())), preferred_element_type=jnp.float32)
 
+    def far_tile(step):
+        phase = step // 8
+        piece = jnp.where(slot == 2, 1 - phase, phase)
+        tile(jnp.where(slot == 3, 2 - piece, 1 + piece), (step // 2) % 4, 2 * (step % 2), 2)
+
+    def near_tile(step):
+        tile(0, step // 4, step % 4, 1)
+
     scale = DH**-0.5
 
     def rounded(source, chunk, extra):
@@ -852,8 +898,8 @@
 
     events = {}
     for chunk in range(4):
-        events.setdefault(4 * chunk + 4, []).append(functools.partial(first_done, chunk))
-        events.setdefault(20 + 4 * chunk, []).append(functools.partial(second_done, chunk))
+        events.setdefault(2 * chunk + 2, []).append(functools.partial(first_done, chunk))
+        events.setdefault(10 + 2 * chunk, []).append(functools.partial(second_done, chunk))
     begin, ready, first, hop, lag = steps
     rest = []
     for t in range(T):
@@ -865,7 +911,7 @@
         plan.append((when, functools.partial(ring.deliver, t)))
         plan.append((when + hop, functools.partial(ring.finish, t)))
         for when, event in plan:
-            if when < 48:
+            if when < 32:
                 events.setdefault(int(when), []).append(event)
             else:
                 rest.append((when, event))
@@ -877,10 +923,11 @@
             def _():
                 for action in actions:
                     action()
-        tile(step)
+        pl.when(step < 16)(lambda: far_tile(step))
+        pl.when(step >= 16)(lambda: near_tile(step - 16))
         return carry
 
-    lax.fori_loop(0, 48, step_body, 0)
+    lax.fori_loop(0, 32, step_body, 0)
     for chunk in range(4):
         own_done(chunk)
     for mate in mates[1:] + mates[:1]:
@@ -905,7 +952,7 @@
             z_send(chunk).wait_send()
 
 
-def retreat(count, grad_att, turned, store, outputs, logs, part, splits, steps=(0, 1, 6, 6, 2)):
+def retreat(count, grad_att, turned, store, outputs, logs, part, splits, steps=(0, 1, 2, 3, 1)):
     rows = grad_att.shape[1]
     own = 4 * rows
     _, shard_rows, half = part.shape
@@ -1319,29 +1366,34 @@
 def publish_kernel(joint_w, output_w, inner_w, outer_w, layer, tokens_in,
                    query, key, value, value_router, output_router, norms, output_out, inner_out, outer_out, layer_out, tokens_out,
                    *refs):
-    held, load, store = refs[:-2], refs[-2], refs[-1]
-    sources = (tokens_in, inner_w, outer_w, layer, output_w)
+    held, parts, load, store = refs[:6], refs[6:-2], refs[-2], refs[-1]
+    sources = (joint_w, tokens_in, inner_w, outer_w, layer, output_w)
     loads = [pltpu.make_async_copy(src, buf, load.at[i]) for i, (src, buf) in enumerate(zip(sources, held))]
     for copy in loads:
         copy.start()
-    query[...] = joint_w[:, :QCOLS]
-    key[...] = joint_w[:, QCOLS : 2 * QCOLS]
-    value[...] = joint_w[:, 2 * QCOLS : ROUTERS]
-    value_router[...] = joint_w[:, ROUTERS : ROUTERS + HEADS * EXP]
-    output_router[...] = joint_w[:, ROUTERS + HEADS * EXP : NORM]
-    norms[...] = joint_w[:, NORM : NORM + 2]
     half, small = inner_w.shape[1] // 2, CHUNK // 2
     stores = []
+
+    def put(src, dst):
+        copy = pltpu.make_async_copy(src, dst, store.at[len(stores)])
+        copy.start()
+        stores.append(copy)
+
+    loads[0].wait()
+    spots = [(0, QCOLS), (QCOLS, QCOLS), (2 * QCOLS, VCOLS), (ROUTERS, HEADS * EXP), (ROUTERS + HEADS * EXP, HEADS * EXP)]
+    for (first, size), part, target in zip(spots, parts, (query, key, value, value_router, output_router)):
+        part[...] = held[0][:, first : first + size]
+        put(part, target)
+    norm_tile = NORM // LANES * LANES
+    norms[...] = held[0][:, norm_tile : norm_tile + LANES].T[NORM - norm_tile : NORM - norm_tile + 8]
     for i, target in enumerate((tokens_out, inner_out, outer_out, layer_out, output_out)):
-        loads[i].wait()
-        pairs = [(held[i], target)]
-        if i == 1:
-            pairs = [(held[i].at[:, pl.ds(core * half + chunk * small, small)], target.at[:, pl.ds(chunk * CHUNK + core * small, small)])
-                     for core in range(2) for chunk in range(half // small)]
-        for src, dst in pairs:
-            copy = pltpu.make_async_copy(src, dst, store.at[len(stores)])
-            copy.start()
-            stores.append(copy)
+        loads[1 + i].wait()
+        if i != 1:
+            put(held[1 + i], target)
+            continue
+        for core in range(2):
+            for chunk in range(half // small):
+                put(held[1 + i].at[:, pl.ds(core * half + chunk * small, small)], target.at[:, pl.ds(chunk * CHUNK + core * small, small)])
     for copy in stores:
         copy.wait()
 
@@ -1349,16 +1401,18 @@
 def publish(joint_w, output_w, inner_w, outer_w, layer, tokens):
     rows = joint_w.shape[0]
     f32 = jnp.float32
-    columns = [QCOLS, QCOLS, VCOLS, HEADS * EXP, HEADS * EXP, 2]
+    columns = [QCOLS, QCOLS, VCOLS, HEADS * EXP, HEADS * EXP]
     rest = (output_w, inner_w, outer_w, layer, tokens)
     return pl.pallas_call(
         publish_kernel,
-        out_shape=[jax.ShapeDtypeStruct((rows, c), f32) for c in columns] + [jax.ShapeDtypeStruct(x.shape, x.dtype) for x in rest],
-        in_specs=[VMEM] + [ANY] * 5,
-        out_specs=[VMEM] * 6 + [ANY] * 5,
-        scratch_shapes=[pltpu.VMEM(x.shape, x.dtype) for x in (tokens, inner_w, outer_w, layer, output_w)]
-        + [DMA((5,)), DMA((4 + inner_w.shape[1] // (CHUNK // 2),))],
-        compiler_params=pltpu.CompilerParams(vmem_limit_bytes=32 << 20),
+        out_shape=[jax.ShapeDtypeStruct((rows, c), f32) for c in columns] + [jax.ShapeDtypeStruct((8, rows), f32)]
+        + [jax.ShapeDtypeStruct(x.shape, x.dtype) for x in rest],
+        in_specs=[ANY] * 6,
+        out_specs=[ANY] * 5 + [VMEM] + [ANY] * 5,
+        scratch_shapes=[pltpu.VMEM(x.shape, x.dtype) for x in (joint_w, tokens, inner_w, outer_w, layer, output_w)]
+        + [pltpu.VMEM((rows, c), f32) for c in columns]
+        + [DMA((6,)), DMA((9 + inner_w.shape[1] // (CHUNK // 2),))],
+        compiler_params=pltpu.CompilerParams(vmem_limit_bytes=63 << 20),
     )(joint_w, *rest)
 
 
@@ -1369,12 +1423,10 @@
     count = lax.axis_size("fsdp")
     inputs = tokens[0]
     rows, width = inputs.shape
-    routers = jnp.concatenate(
-        [value_router, output_router, norm_gain[:, None], norm_bias[:, None],
-         jnp.zeros((query_weight.shape[0], JOINT - NORM - 2), jnp.bfloat16)], axis=1)
+    norm = jnp.stack([norm_gain, norm_bias])
     routes = jnp.concatenate([value_routes[0].reshape(rows, -1), output_routes[0].reshape(rows, -1)], axis=1)
     joint, output_full, qkv, experts, gates, norms, tables, turned = project(
-        count, query_weight, key_weight, value_weight, routers, inputs, routes, output_weight, cont_gap)
+        count, query_weight, key_weight, value_weight, value_router, output_router, norm, inputs, routes, output_weight, cont_gap)
     att, store, outputs, logs, inner_full, outer_full = attend(
         count, qkv, tables, (inner_weight, outer_weight), (SPLITS["inner"], SPLITS["outer"]))
     layer, grad_residual, grad_att, grad_logit, grad_norms, part_output, part_inner, outer_w = feed(
@@ -1387,7 +1439,7 @@
         part_output.reshape(count, -1, part_output.shape[1]))
     query, key, value, value_r, output_r, norm_w, output_w, inner_w, outer_w, layer, grad_input = publish(
         joint_w, output_w, inner_w, outer_w, layer, grad_input)
-    return (layer[None], grad_input[None], query, key, value, value_r, output_r, output_w, norm_w[:, 0], norm_w[:, 1], inner_w, outer_w)
+    return (layer[None], grad_input[None], query, key, value, value_r, output_r, output_w, norm_w[0], norm_w[1], inner_w, outer_w)
 
 
 def solution(mesh):

time: 516 us -> 496 us (0.961)
  Pallas kernels: 486 us -> 466 us
    pallas_call x1, Pallas kernels: 114 us -> 95.6 us  [attend(): pl.pallas_call(functools.partial(attend_kernel, count, splits, steps), ou...]
    pallas_call x1, Pallas kernels: 70.4 us -> 76.5 us  [project(): pl.pallas_call(functools.partial(project_kernel, count), out_shape=[jax.S...]
    unnamed x22 -> x10, local copies, waits for them, and re-layouts: 18.5 us -> 17.5 us
where the time goes in v4:
time: 496 us; the launch traced here: 490 us
  Pallas kernels  466 us (94%)
  local copies, waits for them, and re-layouts  21.1 us (4%)
    pallas_call x1, Pallas kernels, feed(): pl.pallas_call(functools.partial(feed_kernel, count), out_shape=[jax.Shap...  106 us
    pallas_call x1, Pallas kernels, retreat(): pl.pallas_call(functools.partial(retreat_kernel, count, splits, steps), o...  105 us
    pallas_call x1, Pallas kernels, attend(): pl.pallas_call(functools.partial(attend_kernel, count, splits, steps), ou...  95.6 us
    pallas_call x1, Pallas kernels, project(): pl.pallas_call(functools.partial(project_kernel, count), out_shape=[jax.S...  76.5 us
    pallas_call x1, Pallas kernels, settle(): pl.pallas_call(functools.partial(settle_kernel, count), out_shape=[jax.Sh...  75.3 us
    unnamed x10, local copies, waits for them, and re-layouts  17.5 us

profile of v4, /device:TPU:0, one launch (start us, length us, event | category | flops | bytes accessed | tf_op | source)
XLA Modules:
  0.0 489.7 jit_solution(2904469639161347695)
XLA Ops:
  0.6 1.2 pad_maximum_fusion.norm
  1.8 0.7 reshape_squeeze.6
  2.6 0.7 reshape_squeeze.7
  3.3 1.4 copy.54.value_router
  4.7 1.4 copy.55.output_router
  6.1 1.7 copy.51.query
  7.8 1.7 copy.52.key
  9.5 0.8 copy.56.routes
  10.3 2.1 copy.53.value
  12.4 76.5 %shard_map.238 = (bf16[1024,3328]{1,0:T(8,128)(2,1)}, bf16[8,280,1024]{2,1,0:T(8,128)(2,1)}, bf16[4,3,512,128]{3,2,1,0:T(8,128)(2,1)}, bf16[20,512,128]{2,1,0:T(...) custom-call(bf16[128,448]{1,0:T(8,128)(2,1)} %copy.51.query, ...), custom_call_target="tpu_custom_call" | custom-call | tf_op jit(solution)/shard_map/pallas_call | solution.py:323
  89.0 95.6 %shard_map.239 = (bf16[4,512,128]{2,1,0:T(8,128)(2,1)}, bf16[7,2048,128]{2,1,0:T(8,128)(2,1)}, f32[2048,128]{1,0:T(8,128)}, f32[8,2048]{1,0:T(8,128)}, bf16[8,12...) custom-call(bf16[4,3,512,128]{3,2,1,0:T(8,128)(2,1)} %get-tuple-element.50.qkv, ...), custom_call_target="tpu_custom_call" | custom-call | tf_op jit(solution)/shard_map/pallas_call | solution.py:574
  184.5 106.2 %shard_map.240 = (bf16[512,1024]{1,0:T(8,128)(2,1)}, f32[512,1024]{1,0:T(8,128)}, bf16[4,512,128]{2,1,0:T(8,128)(2,1)}, f32[512,128]{1,0:T(8,128)}, f32[8,1024]{...) custom-call(bf16[4,512,128]{2,1,0:T(8,128)(2,1)} %get-tuple-element.52.att, ...), custom_call_target="tpu_custom_call" | custom-call | tf_op jit(solution)/shard_map/pallas_call | solution.py:1234
  290.8 104.6 %shard_map.241 = (bf16[4,3,512,128]{3,2,1,0:T(8,128)(2,1)}, f32[128,4096]{1,0:T(8,128)}) custom-call(bf16[4,512,128]{2,1,0:T(8,128)(2,1)} %get-tuple-element.58.grad_att, f32[3,128,5632]{2,1,0:T(8,128)} %get-tuple-element.59.turned, bf16[7,2048,128]{2,1,0:T(8,128)(2,1)} %get-tuple-element.60.store, f32[2048,128]{1,0:T(8,128)} %get-tuple-element.61.outputs, ...), custom_call_target="tpu_custom_call" | custom-call | tf_op jit(solution)/shard_map/pallas_call | solution.py:959
  395.4 75.3 %shard_map.242 = (f32[512,1024]{1,0:T(8,128)}, f32[128,3328]{1,0:T(8,128)}, f32[280,1024]{1,0:T(8,128)}) custom-call(bf16[4,3,512,128]{3,2,1,0:T(8,128)(2,1)} %get-tuple-element.64.back, bf16[20,512,128]{2,1,0:T(8,128)(2,1)} %get-tuple-element.65.experts, f32[2,512,128]{2,1,0:T(8,128)} %get-tuple-element.53.gates, f32[512,128]{1,0:T(8,128)} %get-tuple-element.66.grad_logit, ...), custom_call_target="tpu_custom_call" | custom-call | tf_op jit(solution)/shard_map/pallas_call | solution.py:1353
  470.7 8.1 %shard_map.243 = (f32[128,448]{1,0:T(8,128)}, f32[128,448]{1,0:T(8,128)}, f32[128,2240]{1,0:T(8,128)}, f32[128,20]{1,0:T(8,128)}, f32[128,20]{1,0:T(8,128)}, /*i...) custom-call(f32[128,3328]{1,0:T(8,128)} %get-tuple-element.71.joint_, ...), custom_call_target="tpu_custom_call" | custom-call | tf_op jit(solution)/shard_map/pallas_call | solution.py:1406
  478.8 1.3 slice_bitcast_fusion
  480.1 1.5 copy.60
  481.6 1.5 copy.61
  483.1 1.8 copy.57
  484.9 1.8 copy.58
  486.6 2.6 copy.59
  (1 shorter events, 0.0 us)

commit v5 on v4

--- a/solution.py
+++ b/solution.py
@@ -200,30 +200,23 @@
     return hit.astype(jnp.float32)
 
 
-def project_kernel(count, query, key, value, value_router, output_router, norm, tokens, routes, output_shard, gaps,
-                   joint, output_w, qkv, experts, gates, norms, tables, turned_tables,
-                   shard, query_v, key_v, value_v, routers_v, product, load, send, recv, local):
+def project_kernel(count, query, key, value, value_router, output_router, norm, tokens, routes, gaps,
+                   joint_out, tables_out, turned_out, qkv, experts, gates, norms,
+                   shard, shard_t, joint, tables, turned_tables, product, load, store, send, recv, local):
     rows = shard.shape[0]
-    splits = (SPLITS["joint"], SPLITS["output"])
-
-    def at(t, g, cols):
-        if t:
-            return output_w.at[g, :, cols]
-        return joint.at[pl.ds(pl.multiple_of(g * rows, rows), rows), cols]
-
-    ring = Gather(count, splits, [shard, output_shard], at, send, recv, local)
-    loads = [(query, query_v), (key, key_v), (value, value_v), (value_router, routers_v.at[0]), (output_router, routers_v.at[1])]
-    loads = [pltpu.make_async_copy(src, dst, load.at[i]) for i, (src, dst) in enumerate(loads)]
-    for copy in loads:
-        copy.start()
+    splits = (SPLITS["joint"],)
+    at = lambda t, g, cols: joint.at[pl.ds(pl.multiple_of(g * rows, rows), rows), cols]
+    ring = Gather(count, splits, [shard], at, send, recv, local)
+    loads = []
+    for i, (src, first) in enumerate(((query, 0), (key, QCOLS), (value, 2 * QCOLS))):
+        loads.append(pltpu.make_async_copy(src, shard_t.at[pl.ds(first, src.shape[0])], load.at[i]))
+        loads[-1].start()
+    small = [ref[...].astype(jnp.float32) for ref in (value_router, output_router, norm)]
+    small.append(jnp.zeros((JOINT - NORM - 2, rows), jnp.float32))
+    shard_t[ROUTERS:, :] = jnp.concatenate(small, axis=0).astype(jnp.bfloat16)
     for copy in loads:
         copy.wait()
-    turned_norm = jnp.concatenate([norm[...].astype(jnp.float32), jnp.zeros((LANES - 2, rows), jnp.float32)], axis=0).T
-    wide = [ref[...].astype(jnp.float32) for ref in (query_v, key_v, value_v)]
-    wide += [routers_v[0].astype(jnp.float32), routers_v[1].astype(jnp.float32), turned_norm[:, : JOINT - NORM]]
-    if JOINT - NORM > LANES:
-        wide.append(jnp.zeros((rows, JOINT - NORM - LANES), jnp.float32))
-    shard[...] = jnp.concatenate(wide, axis=1).astype(jnp.bfloat16)
+    shard[...] = shard_t[...].T
     enter(ring.neighbours())
     ring.start(0)
     slope = jnp.float32(0.0)
@@ -250,40 +243,35 @@
                 target[which, :, pl.ds(start, 256)] = rolled[:, LANES:]
         return carry
 
-    late = 1
-    steps, later = [], []
+    events = []
     for k in range(1, ring.far + 1):
-        steps.append(functools.partial(ring.arrive, 0, k))
+        events.append(functools.partial(ring.arrive, 0, k))
         if k > 1:
-            steps.append(functools.partial(ring.plane_arrive, 0, k - 1))
-        if k == late:
-            steps.append(functools.partial(ring.start, 1))
-        later.append(functools.partial(ring.arrive, 1, k))
-        if k > 1:
-            later.append(functools.partial(ring.plane_arrive, 1, k - 1))
-    steps += [functools.partial(ring.plane_arrive, 0, ring.far), functools.partial(ring.finish, 0)]
-    later += [functools.partial(ring.plane_arrive, 1, ring.far)]
-    early, later = later[:3], later[3:]
-    steps = steps[:-1] + early + steps[-1:]
-    cut = max(1, TABLE // 256 // len(steps))
+            events.append(functools.partial(ring.plane_arrive, 0, k - 1))
+    events += [functools.partial(ring.plane_arrive, 0, ring.far), functools.partial(ring.finish, 0)]
+    cut = max(1, TABLE // 256 // (len(events) - 2))
     done = 0
-    for i, event in enumerate(steps):
-        upto = TABLE // 256 if i == len(steps) - 1 else min(TABLE // 256, (i + 1) * cut)
+    saves = [(tables, tables_out), (turned_tables, turned_out), (joint, joint_out)]
+    saves = [pltpu.make_async_copy(src, dst, store.at[i]) for i, (src, dst) in enumerate(saves)]
+    for i, event in enumerate(events):
+        upto = min(TABLE // 256, (i + 1) * cut)
+        if i == len(events) - 2:
+            upto = TABLE // 256
         if upto > done:
             lax.fori_loop(done, upto, table_column, 0)
             done = upto
+            if done == TABLE // 256:
+                saves[0].start()
+                saves[1].start()
         event()
+    saves[2].start()
 
     def column(step, carry):
         cols = pl.ds(pl.multiple_of(step * 256, 256), 256)
         product[:, cols] = jnp.dot(tokens[...], joint[:, cols], preferred_element_type=jnp.float32)
         return carry
 
-    columns = JOINT // 256
-    for i in range(3):
-        lax.fori_loop(i * columns // 3, (i + 1) * columns // 3, column, 0)
-        for event in later[i * len(later) // 4 : (i + 1) * len(later) // 4]:
-            event()
+    lax.fori_loop(0, JOINT // 256, column, 0)
     norm_tile = NORM // LANES * LANES
     turned_norm = joint[:, norm_tile : norm_tile + LANES].astype(jnp.float32).T
     norms[...] = turned_norm[NORM - norm_tile : NORM - norm_tile + 8]
@@ -311,36 +299,34 @@
             term = piece * gates[0, :, which : which + 1]
             total = term if total is None else total + term
         qkv[head, 2] = jnp.concatenate([total, ones], axis=1).astype(jnp.bfloat16)
-    for event in later[3 * len(later) // 4 :]:
-        event()
-    ring.finish(1)
-
-
-def project(count, query, key, value, value_router, output_router, norm, tokens, routes, output_shard, gaps):
-    rows, (shard_rows, _) = tokens.shape[0], query.shape
+    for copy in saves:
+        copy.wait()
+
+
+def project(count, query, key, value, value_router, output_router, norm, tokens, routes, gaps):
+    rows, shard_rows = tokens.shape[0], query.shape[1]
     f32, bf = jnp.float32, jnp.bfloat16
     V = pltpu.VMEM
     return pl.pallas_call(
         functools.partial(project_kernel, count),
         out_shape=[
             jax.ShapeDtypeStruct((shard_rows * count, JOINT), bf),
-            jax.ShapeDtypeStruct((count,) + output_shard.shape, bf),
+            jax.ShapeDtypeStruct((3, LANES, TABLE), f32),
+            jax.ShapeDtypeStruct((3, LANES, TABLE), f32),
             jax.ShapeDtypeStruct((HEADS, 3, rows, LANES), bf),
             jax.ShapeDtypeStruct((HEADS * EXP, rows, LANES), bf),
             jax.ShapeDtypeStruct((2, rows, LANES), f32),
             jax.ShapeDtypeStruct((8, shard_rows * count), f32),
-            jax.ShapeDtypeStruct((3, LANES, TABLE), f32),
-            jax.ShapeDtypeStruct((3, LANES, TABLE), f32),
         ],
-        in_specs=[ANY] * 5 + [VMEM] * 4 + [SMEM],
-        out_specs=[VMEM, ANY] + [VMEM] * 6,
+        in_specs=[ANY] * 3 + [VMEM] * 5 + [SMEM],
+        out_specs=[ANY] * 3 + [VMEM] * 4,
         scratch_shapes=[
-            V((shard_rows, JOINT), bf), V(query.shape, bf), V(key.shape, bf), V(value.shape, bf), V((2,) + value_router.shape, bf),
-            V((rows, JOINT), f32), DMA((5,)),
+            V((shard_rows, JOINT), bf), V((JOINT, shard_rows), bf), V((shard_rows * count, JOINT), bf),
+            V((3, LANES, TABLE), f32), V((3, LANES, TABLE), f32), V((rows, JOINT), f32), DMA((3,)), DMA((3,)),
         ]
-        + Gather.sems(count, 2),
+        + Gather.sems(count, 1),
         compiler_params=pltpu.CompilerParams(collective_id=1, has_side_effects=True, vmem_limit_bytes=62 << 20),
-    )(query, key, value, value_router, output_router, norm, tokens, routes, output_shard, gaps)
+    )(query, key, value, value_router, output_router, norm, tokens, routes, gaps)
 
 
 def seq_mates(ring):
@@ -387,14 +373,16 @@
     return pl.ds(pl.multiple_of(block * BLOCK, BLOCK), BLOCK)
 
 
-def attend_kernel(count, splits, steps, qkv, tables, *refs):
+def attend_kernel(count, splits, steps, qkv, tables_in, *refs):
     T = len(splits)
     shards, refs = refs[:T], refs[T:]
     att, store, outputs, logs = refs[:4]
     fulls, refs = refs[4 : 4 + T], refs[4 + T :]
-    acc, top, att_low, kv_send, kv_recv, q_send, q_recv, sh_send, sh_recv, out_send, out_recv, here = refs[:12]
+    acc, top, att_low, tables, kv_send, kv_recv, q_send, q_recv, sh_send, sh_recv, out_send, out_recv, here = refs[:13]
     at = lambda t, g, cols: fulls[t].at[g, :, cols]
-    ring = Gather(count, splits, shards, at, *refs[12:])
+    ring = Gather(count, splits, shards, at, *refs[13:])
+    table_load = pltpu.make_async_copy(tables_in, tables, here.at[2])
+    table_load.start()
     seq, slot = ring.seq, ring.fsdp % GSLOTS
     mates, (x_mate, z_mate) = seq_mates(ring), slot_mates(ring)
     enter(ring.neighbours() + mates[2:] + [x_mate, z_mate])
@@ -500,6 +488,7 @@
         def _():
             tile(source, table, column, key_block, query_block * BLOCK, 2 * BLOCK)
 
+    table_load.wait()
     events = {}
     for chunk in range(4):
         events.setdefault(4 * chunk + 3, []).append(functools.partial(pass_on, chunk))
@@ -580,13 +569,14 @@
             jax.ShapeDtypeStruct((8, own), jnp.float32),
         ]
         + [jax.ShapeDtypeStruct((count,) + w.shape, w.dtype) for w in shards],
-        in_specs=[VMEM] * (2 + T),
+        in_specs=[VMEM, ANY] + [VMEM] * T,
         out_specs=[VMEM] * 4 + [ANY] * T,
         scratch_shapes=[
             pltpu.VMEM((own, LANES), jnp.float32),
             pltpu.VMEM((own, LANES), jnp.float32),
             pltpu.VMEM((own, LANES), jnp.bfloat16),
-            DMA((4,)), DMA((4,)), DMA((4,)), DMA((4,)), DMA((12,)), DMA((8,)), DMA((4,)), DMA((4,)), DMA((2,)),
+            pltpu.VMEM((3, LANES, TABLE), jnp.float32),
+            DMA((4,)), DMA((4,)), DMA((4,)), DMA((4,)), DMA((12,)), DMA((8,)), DMA((4,)), DMA((4,)), DMA((3,)),
         ]
         + Gather.sems(count, T),
         compiler_params=pltpu.CompilerParams(collective_id=2, has_side_effects=True, vmem_limit_bytes=56 << 20),
@@ -761,11 +751,14 @@
         self.remote(ref, ref, self.end_s, self.end_r, 2 * t + 1, self.core_mate).wait_recv()
 
 
-def retreat_kernel(count, splits, steps, grad_att, turned, store, outputs, logs, part, back, out, *refs):
+def retreat_kernel(count, splits, steps, grad_att, turned_in, store_in, outputs, logs, part, back, out, *refs):
     T = len(splits)
     (grads, delta, grad_q, grad_kv, send_kv, kv_in0, kv_in1, low, in_send, in_recv, up_send, up_recv,
-     out_send, out_recv, here) = refs[:15]
-    refs = refs[15:]
+     turned, store, out_send, out_recv, here) = refs[:17]
+    refs = refs[17:]
+    loads = [pltpu.make_async_copy(turned_in, turned, here.at[2]), pltpu.make_async_copy(store_in, store, here.at[3])]
+    for copy in loads:
+        copy.start()
     halves = [a + 2 * b for a, b in splits]
     firsts = [sum(halves[:t]) for t in range(T)]
     ring = Scatter(
@@ -797,6 +790,9 @@
         rows = pl.ds(block * BLOCK, BLOCK)
         sums = jnp.sum(grads[rows, :].astype(jnp.float32) * outputs[rows, :], axis=1, keepdims=True)
         delta[:, rows] = jnp.broadcast_to(sums, (BLOCK, LANES)).T[:8]
+
+    for copy in loads:
+        copy.wait()
 
     def tile(forward_phase, key_block, query_block, blocks):
         source, active, table, column = tile_place(slot, seq, forward_phase, key_block, query_block)
@@ -959,7 +955,7 @@
     return pl.pallas_call(
         functools.partial(retreat_kernel, count, splits, steps),
         out_shape=[jax.ShapeDtypeStruct((HEADS, 3, rows, LANES), jnp.bfloat16), jax.ShapeDtypeStruct((shard_rows, 2 * half), jnp.float32)],
-        in_specs=[VMEM] * 5 + [ANY],
+        in_specs=[VMEM, ANY, ANY, VMEM, VMEM, ANY],
         out_specs=[VMEM, ANY],
         scratch_shapes=[
             pltpu.VMEM((own, LANES), jnp.bfloat16),
@@ -970,7 +966,9 @@
             pltpu.VMEM((2, own, LANES), jnp.bfloat16),
             pltpu.VMEM((2, own, LANES), jnp.bfloat16),
             pltpu.VMEM((3, own, LANES), jnp.bfloat16),
-            DMA((4,)), DMA((4,)), DMA((8,)), DMA((8,)), DMA((4,)), DMA((4,)), DMA((2,)),
+            DMA((4,)), DMA((4,)), DMA((8,)), DMA((8,)),
+            pltpu.VMEM((3, LANES, TABLE), jnp.float32), pltpu.VMEM((7, own, LANES), jnp.bfloat16),
+            DMA((4,)), DMA((4,)), DMA((4,)),
         ]
         + Scatter.scratch(count, splits, [shard_rows] * len(splits)),
         compiler_params=pltpu.CompilerParams(collective_id=3, has_side_effects=True, vmem_limit_bytes=60 << 20),
@@ -1260,13 +1258,16 @@
     )(att, gates, tokens, cotangent, norms, output_w, inner_w, outer_w)
 
 
-def settle_kernel(count, back, experts, gates, grad_logit, tokens, joint, grad_residual, grad_norms, part_output,
-                  grad_tokens, joint_out, output_out, grads, grads_in, tokens_in, tokens_t, norms_in, norm_columns, *refs):
+def settle_kernel(count, back, experts, gates, grad_logit, tokens, joint_in, residual_in, grad_norms, part_output,
+                  grad_tokens, joint_out, output_out, grads, grads_in, tokens_in, tokens_t, norms_in, norm_columns, joint, grad_residual, *refs):
     splits = (SPLITS["joint"], SPLITS["output"])
-    pair_s, pair_r = refs[-2:]
+    pair_s, pair_r, load = refs[-3:]
+    loads = [pltpu.make_async_copy(joint_in, joint, load.at[0]), pltpu.make_async_copy(residual_in, grad_residual, load.at[1])]
+    for copy in loads:
+        copy.start()
     half, output_half = JOINT // 2, part_output.shape[2]
     outs = [(joint_out, half, 0), (output_out, output_half, 0)]
-    ring = Scatter(count, splits, [None, (part_output, 0)], outs, refs[:14], refs[14:-2])
+    ring = Scatter(count, splits, [None, (part_output, 0)], outs, refs[:14], refs[14:-3])
     ring.start(1)
     enter(ring.neighbours())
     core = ring.core
@@ -1276,13 +1277,18 @@
 
     mine = pl.ds(pl.multiple_of(core * half, LANES), half)
     yours = pl.ds(pl.multiple_of((1 - core) * half, LANES), half)
-    pair = [remote(tokens, tokens_in, 0), remote(grad_norms, norms_in, 1), remote(grads.at[:, yours], grads_in, 2)]
+    pair = [remote(tokens, tokens_in, 0), remote(grad_norms, norms_in, 1)]
     pair[0].start()
     pair[1].start()
     ring.all_ready(1)
     rows = tokens.shape[0]
     lane = lax.broadcasted_iota(jnp.int32, (LANES, LANES), 1)
     width = HEADS * EXP
+
+    def hand_over(block):
+        part = pl.ds(pl.multiple_of(block * LANES, LANES), LANES)
+        return remote(grads.at[part, yours], grads_in.at[part], 2 + block)
+
 
     def assemble(block, carry):
         part = pl.ds(pl.multiple_of(block * LANES, LANES), LANES)
@@ -1298,13 +1304,13 @@
         pieces.append(jnp.where(lane < 2 * width, logit, 0.0))
         pieces.append(jnp.zeros((LANES, JOINT - ROUTERS - LANES), jnp.float32))
         grads[part, :] = jnp.concatenate(pieces, axis=1).astype(jnp.bfloat16)
+        hand_over(block).start()
         return carry
 
     lax.fori_loop(0, rows // LANES, assemble, 0)
-    pair[2].start()
     ring.step(1, ring.far)
     tokens_t[:, :rows] = tokens[...].T
-    for copy in pair[:2]:
+    for copy in pair:
         copy.wait_recv()
     tokens_t[:, rows:] = tokens_in[...].T
     norm_tile = NORM // LANES * LANES - half
@@ -1313,7 +1319,8 @@
     for block in range(both.shape[1] // LANES):
         columns = jnp.concatenate([both[:, block * LANES : (block + 1) * LANES], jnp.zeros((LANES - 8, LANES), jnp.float32)], axis=0)
         norm_columns[block * LANES : (block + 1) * LANES, :] = columns.T
-    pair[2].wait_recv()
+    for block in range(rows // LANES):
+        hand_over(block).wait_recv()
     shard_rows = tokens_t.shape[0] // count
     tile_lane = lax.broadcasted_iota(jnp.int32, (shard_rows, LANES), 1)
 
@@ -1334,6 +1341,8 @@
         ring.step(1, D)
         ring.step(0, D)
         if D == ring.far - 1:
+            for copy in loads:
+                copy.wait()
             grad_tokens[...] = grad_residual[...] + contract(grads[...], joint[...], 1, 1)
     ring.step(1, 0)
     ring.step(0, 0)
@@ -1343,6 +1352,8 @@
     ring.finish(0)
     for copy in pair:
         copy.wait_send()
+    for block in range(rows // LANES):
+        hand_over(block).wait_send()
 
 
 def settle(count, back, experts, gates, grad_logit, tokens, joint, grad_residual, grad_norms, part_output):
@@ -1354,11 +1365,12 @@
         functools.partial(settle_kernel, count),
         out_shape=[jax.ShapeDtypeStruct((rows, width), f32), jax.ShapeDtypeStruct((shard_rows, JOINT), f32),
                    jax.ShapeDtypeStruct((part_output.shape[1], width), f32)],
-        in_specs=[VMEM] * 8 + [ANY],
+        in_specs=[VMEM] * 5 + [ANY, ANY, VMEM, ANY],
         out_specs=[VMEM, VMEM, ANY],
-        scratch_shapes=[V((rows, JOINT), bf), V((rows, JOINT // 2), bf), V((rows, width), bf), V((width, 2 * rows), bf), V((8, width), f32), V((width, LANES), f32)]
+        scratch_shapes=[V((rows, JOINT), bf), V((rows, JOINT // 2), bf), V((rows, width), bf), V((width, 2 * rows), bf), V((8, width), f32), V((width, LANES), f32),
+                        V((width, JOINT), bf), V((rows, width), f32)]
         + Scatter.scratch(count, (SPLITS["joint"], SPLITS["output"]), [shard_rows, part_output.shape[1]])
-        + [DMA((3,)), DMA((3,))],
+        + [DMA((2 + rows // LANES,)), DMA((2 + rows // LANES,)), DMA((2,))],
         compiler_params=pltpu.CompilerParams(collective_id=5, has_side_effects=True, vmem_limit_bytes=60 << 20),
     )(back, experts, gates, grad_logit, tokens, joint, grad_residual, grad_norms, part_output)
 
@@ -1366,7 +1378,7 @@
 def publish_kernel(joint_w, output_w, inner_w, outer_w, layer, tokens_in,
                    query, key, value, value_router, output_router, norms, output_out, inner_out, outer_out, layer_out, tokens_out,
                    *refs):
-    held, parts, load, store = refs[:6], refs[6:-2], refs[-2], refs[-1]
+    held, turned, tail, load, store = refs[:6], refs[6], refs[7], refs[8], refs[9]
     sources = (joint_w, tokens_in, inner_w, outer_w, layer, output_w)
     loads = [pltpu.make_async_copy(src, buf, load.at[i]) for i, (src, buf) in enumerate(zip(sources, held))]
     for copy in loads:
@@ -1380,12 +1392,12 @@
         stores.append(copy)
 
     loads[0].wait()
-    spots = [(0, QCOLS), (QCOLS, QCOLS), (2 * QCOLS, VCOLS), (ROUTERS, HEADS * EXP), (ROUTERS + HEADS * EXP, HEADS * EXP)]
-    for (first, size), part, target in zip(spots, parts, (query, key, value, value_router, output_router)):
-        part[...] = held[0][:, first : first + size]
-        put(part, target)
-    norm_tile = NORM // LANES * LANES
-    norms[...] = held[0][:, norm_tile : norm_tile + LANES].T[NORM - norm_tile : NORM - norm_tile + 8]
+    turned[...] = held[0][...].T
+    for first, target in ((0, query), (QCOLS, key), (2 * QCOLS, value), (ROUTERS, value_router)):
+        put(turned.at[pl.ds(first, target.shape[0])], target)
+    tail[...] = turned[ROUTERS + HEADS * EXP : NORM, :]
+    put(tail, output_router)
+    norms[...] = turned[NORM : NORM + 8, :]
     for i, target in enumerate((tokens_out, inner_out, outer_out, layer_out, output_out)):
         loads[1 + i].wait()
         if i != 1:
@@ -1405,12 +1417,12 @@
     rest = (output_w, inner_w, outer_w, layer, tokens)
     return pl.pallas_call(
         publish_kernel,
-        out_shape=[jax.ShapeDtypeStruct((rows, c), f32) for c in columns] + [jax.ShapeDtypeStruct((8, rows), f32)]
+        out_shape=[jax.ShapeDtypeStruct((c, rows), f32) for c in columns] + [jax.ShapeDtypeStruct((8, rows), f32)]
         + [jax.ShapeDtypeStruct(x.shape, x.dtype) for x in rest],
         in_specs=[ANY] * 6,
         out_specs=[ANY] * 5 + [VMEM] + [ANY] * 5,
         scratch_shapes=[pltpu.VMEM(x.shape, x.dtype) for x in (joint_w, tokens, inner_w, outer_w, layer, output_w)]
-        + [pltpu.VMEM((rows, c), f32) for c in columns]
+        + [pltpu.VMEM((JOINT, rows), f32), pltpu.VMEM((HEADS * EXP, rows), f32)]
         + [DMA((6,)), DMA((9 + inner_w.shape[1] // (CHUNK // 2),))],
         compiler_params=pltpu.CompilerParams(vmem_limit_bytes=63 << 20),
     )(joint_w, *rest)
@@ -1425,10 +1437,10 @@
     rows, width = inputs.shape
     norm = jnp.stack([norm_gain, norm_bias])
     routes = jnp.concatenate([value_routes[0].reshape(rows, -1), output_routes[0].reshape(rows, -1)], axis=1)
-    joint, output_full, qkv, experts, gates, norms, tables, turned = project(
-        count, query_weight, key_weight, value_weight, value_router, output_router, norm, inputs, routes, output_weight, cont_gap)
-    att, store, outputs, logs, inner_full, outer_full = attend(
-        count, qkv, tables, (inner_weight, outer_weight), (SPLITS["inner"], SPLITS["outer"]))
+    joint, tables, turned, qkv, experts, gates, norms = project(
+        count, query_weight.T, key_weight.T, value_weight.T, value_router.T, output_router.T, norm, inputs, routes, cont_gap)
+    att, store, outputs, logs, inner_full, outer_full, output_full = attend(
+        count, qkv, tables, (inner_weight, outer_weight, output_weight), (SPLITS["inner"], SPLITS["outer"], SPLITS["output"]))
     layer, grad_residual, grad_att, grad_logit, grad_norms, part_output, part_inner, outer_w = feed(
         count, att, gates, inputs, cotangent[0], norms, output_full.reshape(VCOLS, width), inner_full.reshape(width, -1),
         outer_full.reshape(-1, width))
@@ -1439,7 +1451,7 @@
         part_output.reshape(count, -1, part_output.shape[1]))
     query, key, value, value_r, output_r, norm_w, output_w, inner_w, outer_w, layer, grad_input = publish(
         joint_w, output_w, inner_w, outer_w, layer, grad_input)
-    return (layer[None], grad_input[None], query, key, value, value_r, output_r, output_w, norm_w[0], norm_w[1], inner_w, outer_w)
+    return (layer[None], grad_input[None], query.T, key.T, value.T, value_r.T, output_r.T, output_w, norm_w[0], norm_w[1], inner_w, outer_w)
 
 
 def solution(mesh):

time: 496 us -> 462 us (0.931)
  Pallas kernels: 466 us -> 447 us
  local copies, waits for them, and re-layouts: 21.1 us -> 3.58 us
    pallas_call x1, Pallas kernels: 76.5 us -> 51.6 us  [project(): pl.pallas_call(functools.partial(project_kernel, count), out_shape=[jax.S...]
    unnamed x10 -> x0, local copies, waits for them, and re-layouts: 17.5 us -> none
    pallas_call x1, Pallas kernels: 95.6 us -> 107 us  [attend(): pl.pallas_call(functools.partial(attend_kernel, count, splits, steps), ou...]
where the time goes in v5:
time: 462 us; the launch traced here: 453 us
  Pallas kernels  447 us (97%)
    pallas_call x1, Pallas kernels, attend(): pl.pallas_call(functools.partial(attend_kernel, count, splits, steps), ou...  107 us
    pallas_call x1, Pallas kernels, feed(): pl.pallas_call(functools.partial(feed_kernel, count), out_shape=[jax.Shap...  106 us
    pallas_call x1, Pallas kernels, retreat(): pl.pallas_call(functools.partial(retreat_kernel, count, splits, steps), o...  101 us
    pallas_call x1, Pallas kernels, settle(): pl.pallas_call(functools.partial(settle_kernel, count), out_shape=[jax.Sh...  72.2 us
    pallas_call x1, Pallas kernels, project(): pl.pallas_call(functools.partial(project_kernel, count), out_shape=[jax.S...  51.6 us

profile of v5, /device:TPU:0, one launch (start us, length us, event | category | flops | bytes accessed | tf_op | source)
XLA Modules:
  0.0 452.6 jit_solution(14161970239091046733)
XLA Ops:
  0.6 1.2 pad_maximum_fusion.norm
  1.8 0.7 reshape_squeeze.6
  2.6 0.7 reshape_squeeze.7
  3.3 0.8 copy.31.routes
  4.2 51.6 %shard_map.238 = (bf16[1024,3328]{1,0:T(8,128)(2,1)}, f32[3,128,5632]{2,1,0:T(8,128)}, f32[3,128,5632]{2,1,0:T(8,128)}, bf16[4,3,512,128]{3,2,1,0:T(8,128)(2,1)}...) custom-call(bf16[448,128]{1,0:T(8,128)(2,1)} %bitcast.39, bf16[448,128]{1,0:T(8,128)(2,1)} %bitcast.40, ...), custom_call_target="tpu_custom_call" | custom-call | tf_op jit(solution)/shard_map/pallas_call | solution.py:310
  55.8 107.4 %shard_map.239 = (bf16[4,512,128]{2,1,0:T(8,128)(2,1)}, bf16[7,2048,128]{2,1,0:T(8,128)(2,1)}, f32[2048,128]{1,0:T(8,128)}, f32[8,2048]{1,0:T(8,128)}, bf16[8,12...) custom-call(bf16[4,3,512,128]{3,2,1,0:T(8,128)(2,1)} %get-tuple-element.50.qkv, ...), custom_call_target="tpu_custom_call" | custom-call | tf_op jit(solution)/shard_map/pallas_call | solution.py:563
  163.1 106.2 %shard_map.240 = (bf16[512,1024]{1,0:T(8,128)(2,1)}, f32[512,1024]{1,0:T(8,128)}, bf16[4,512,128]{2,1,0:T(8,128)(2,1)}, f32[512,128]{1,0:T(8,128)}, f32[8,1024]{...) custom-call(bf16[4,512,128]{2,1,0:T(8,128)(2,1)} %get-tuple-element.52.att, ...), custom_call_target="tpu_custom_call" | custom-call | tf_op jit(solution)/shard_map/pallas_call | solution.py:1232
  269.3 101.1 %shard_map.241 = (bf16[4,3,512,128]{3,2,1,0:T(8,128)(2,1)}, f32[128,4096]{1,0:T(8,128)}) custom-call(bf16[4,512,128]{2,1,0:T(8,128)(2,1)} %get-tuple-element.58.grad_att, f32[3,128,5632]{2,1,0:T(8,128)} %get-tuple-element.59.turned_in, bf16[7,2048,128]{2,1,0:T(8,128)(2,1)} %get-tuple-element.60.store_in, f32[2048,128]{1,0:T(8,128)} %get-tuple-element.61.outputs, ...), custom_call_target="tpu_custom_call" | custom-call | tf_op jit(solution)/shard_map/pallas_call | solution.py:955
  370.4 72.2 %shard_map.242 = (f32[512,1024]{1,0:T(8,128)}, f32[128,3328]{1,0:T(8,128)}, f32[280,1024]{1,0:T(8,128)}) custom-call(bf16[4,3,512,128]{3,2,1,0:T(8,128)(2,1)} %get-tuple-element.64.back, bf16[20,512,128]{2,1,0:T(8,128)(2,1)} %get-tuple-element.65.experts, f32[2,512,128]{2,1,0:T(8,128)} %get-tuple-element.53.gates, f32[512,128]{1,0:T(8,128)} %get-tuple-element.66.grad_logit, ...), custom_call_target="tpu_custom_call" | custom-call | tf_op jit(solution)/shard_map/pallas_call | solution.py:1364
  442.6 8.2 %shard_map.243 = (f32[448,128]{1,0:T(8,128)}, f32[448,128]{1,0:T(8,128)}, f32[2240,128]{1,0:T(8,128)}, f32[20,128]{1,0:T(8,128)}, f32[20,128]{1,0:T(8,128)}, /*i...) custom-call(f32[128,3328]{1,0:T(8,128)} %get-tuple-element.71.joint_, ...), custom_call_target="tpu_custom_call" | custom-call | tf_op jit(solution)/shard_map/pallas_call | solution.py:1418
  450.8 1.3 slice_bitcast_fusion
  (1 shorter events, 0.0 us)

commit v6 on v5

--- a/solution.py
+++ b/solution.py
@@ -976,6 +976,7 @@
 
 
 CHUNK = 512
+SPOTS = (2, 4, 7, 12)
 
 
 def gelu_pair(v):
@@ -1076,8 +1077,8 @@
     def act_copy(step, sub):
         return remote(acts.at[sub], act_in.at[step], act_s.at[sub], act_r.at[step])
 
-    def slope_copy(step, sub):
-        return remote(slopes.at[sub, :, small_yours], slope_in.at[step], slope_s.at[sub], slope_r.at[step])
+    def slope_copy(step):
+        return remote(slopes.at[step, :, small_yours], slope_in.at[step], slope_s.at[step], slope_r.at[step])
 
     def put_inner_copy(step, sub):
         cols = pl.ds(pl.multiple_of(chunk_of(step) * small, small), small)
@@ -1090,20 +1091,20 @@
         @pl.when(step > 1)
         def _():
             act_copy(step, sub).wait_send()
-            slope_copy(step, sub).wait_send()
 
         act, slope = gelu_pair(jnp.dot(scaled[...], w_in[sub], preferred_element_type=jnp.float32))
         acts[sub] = act.astype(jnp.bfloat16)
         act_copy(step, sub).start()
-        slopes[sub] = (contract(cotangent[...], w_up[sub], 1, 1) * slope).astype(jnp.bfloat16)
-        slope_copy(step, sub).start()
+        slopes[step] = (contract(cotangent[...], w_up[sub], 1, 1) * slope).astype(jnp.bfloat16)
+        slope_copy(step).start()
         acc[...] += jnp.dot(acts[sub], w_up[sub], preferred_element_type=jnp.float32)
-        grad_scaled[...] += contract(slopes[sub], w_in[sub], 1, 1)
+
+        following = (step + 2) % chunks
+        ffn_load(chunk_of(following), sub)[0].start()
 
         @pl.when(step + 2 < chunks)
         def _():
-            for copy in ffn_load(chunk_of(step + 2), sub):
-                copy.start()
+            ffn_load(chunk_of(following), sub)[1].start()
 
     def weight_parts(step, sub):
         remote(act_in.at[step], act_in.at[step], act_s.at[sub], act_r.at[step]).wait_recv()
@@ -1114,13 +1115,21 @@
         for q in range(shards):
             rel = (ring_place(chunk_of(step) * shards + q, count) - ring.place + count) % count
             ring.mine[0][rel] = turned[q * shard_rows : (q + 1) * shard_rows]
-        remote(slope_in.at[step], slope_in.at[step], slope_s.at[sub], slope_r.at[step]).wait_recv()
+
+    def backward(step, sub):
+        ffn_load(chunk_of(step), sub)[0].wait()
+        slope_copy(step).wait()
+        grad_scaled[...] += contract(slopes[step], w_in[sub], 1, 1)
+
+        @pl.when(step + 2 < chunks)
+        def _():
+            ffn_load(chunk_of(step + 2), sub)[0].start()
 
         @pl.when(step > 1)
         def _():
             put_inner_copy(step, sub).wait()
 
-        total = jnp.dot(scaled_t[:, :rows], slopes[sub, :, small_mine], preferred_element_type=jnp.float32)
+        total = jnp.dot(scaled_t[:, :rows], slopes[step, :, small_mine], preferred_element_type=jnp.float32)
         total = total + jnp.dot(scaled_t[:, rows:], slope_in[step], preferred_element_type=jnp.float32)
         stage_inner[sub] = total.astype(jnp.bfloat16)
         put_inner_copy(step, sub).start()
@@ -1130,35 +1139,43 @@
         for step, rel in enumerate(ring.order()):
             events.setdefault(step, []).append(functools.partial(ring.ready, 0, rel))
         for D in range(ring.far, 0, -1):
-            events.setdefault(2 * (ring.far - D) + 1, []).append(functools.partial(ring.step, 0, D))
-
-    def after_parts(step):
+            events.setdefault(SPOTS[min(ring.far - D, 3)], []).append(functools.partial(ring.step, 0, D))
+
+    def after(step):
         for when, actions in sorted(events.items()):
             @pl.when(step == when)
             def _():
                 for action in actions:
                     action()
 
-    def iteration(i, carry):
+    def first_pass(i, carry):
         forward_backward(2 * i, 0)
 
         @pl.when(i > 0)
         def _():
             weight_parts(2 * i - 1, 1)
-            after_parts(2 * i - 1)
+            after(2 * i - 1)
 
         forward_backward(2 * i + 1, 1)
         weight_parts(2 * i, 0)
-        after_parts(2 * i)
+        after(2 * i)
         return carry
 
-    lax.fori_loop(0, chunks // 2, iteration, 0)
+    def second_pass(i, carry):
+        for sub in range(2):
+            backward(2 * i + sub, sub)
+            after(chunks + 2 * i + sub)
+        return carry
+
+    lax.fori_loop(0, chunks // 2, first_pass, 0)
     weight_parts(chunks - 1, 1)
     if count == chunks:
         for action in events[chunks - 1]:
             action()
     else:
         ring.all_ready(0)
+    lax.fori_loop(0, chunks // 2, second_pass, 0)
+    if count != chunks:
         for D in range(ring.far, 0, -1):
             ring.step(0, D)
     layer_out[...] = acc[...].astype(jnp.bfloat16)
@@ -1216,7 +1233,6 @@
     for sub in range(2):
         put_inner_copy(sub, sub).wait()
         act_copy(sub, sub).wait_send()
-        slope_copy(sub, sub).wait_send()
     ring.finish(0)
     for copy in pair:
         copy.wait_send()
@@ -1245,12 +1261,12 @@
         out_specs=[VMEM] * 5 + [ANY] * 3,
         scratch_shapes=[
             V((experts, LANES, width), bf), V((2, width, CHUNK), bf), V((2, CHUNK, width), bf),
-            V((2, rows, CHUNK), bf), V((chunks, rows, CHUNK), bf), V((2, rows, CHUNK), bf), V((chunks, rows, CHUNK // 2), bf),
+            V((2, rows, CHUNK), bf), V((chunks, rows, CHUNK), bf), V((chunks, rows, CHUNK), bf), V((chunks, rows, CHUNK // 2), bf),
             V((rows, width), bf), V((rows, width), bf), V((width, 2 * rows), bf), V((rows, half), bf), V((half, 2 * rows), bf),
             V((rows, width), f32), V((rows, width), f32), V((rows, width), f32),
             V((rows, width), bf), V((rows, half), bf), V((half, 2 * rows), bf), V((HEADS, rows, LANES), bf), V((rows, LANES), f32),
             V((2, width, CHUNK // 2), bf), V((4, LANES, half), bf),
-            DMA((experts,)), DMA((2,)), DMA((2,)), DMA((5,)), DMA((5,)), DMA((2,)), DMA((chunks,)), DMA((2,)), DMA((chunks,)),
+            DMA((experts,)), DMA((2,)), DMA((2,)), DMA((5,)), DMA((5,)), DMA((2,)), DMA((chunks,)), DMA((chunks,)), DMA((chunks,)),
             DMA((2,)), DMA((4,)),
         ]
         + Scatter.scratch(count, (SPLITS["outer"],), [wide // count]),

time: 462 us -> 464 us (level)
  no operation moved by 1% of the time
where the time goes in v6:
time: 464 us; the launch traced here: 455 us
  Pallas kernels  449 us (97%)
    pallas_call x1, Pallas kernels, feed(): pl.pallas_call(functools.partial(feed_kernel, count), out_shape=[jax.Shap...  108 us
    pallas_call x1, Pallas kernels, attend(): pl.pallas_call(functools.partial(attend_kernel, count, splits, steps), ou...  107 us
    pallas_call x1, Pallas kernels, retreat(): pl.pallas_call(functools.partial(retreat_kernel, count, splits, steps), o...  101 us
    pallas_call x1, Pallas kernels, settle(): pl.pallas_call(functools.partial(settle_kernel, count), out_shape=[jax.Sh...  72.1 us
    pallas_call x1, Pallas kernels, project(): pl.pallas_call(functools.partial(project_kernel, count), out_shape=[jax.S...  51.6 us

profile of v6, /device:TPU:0, one launch (start us, length us, event | category | flops | bytes accessed | tf_op | source)
XLA Modules:
  0.0 454.8 jit_solution(796684805907176197)
XLA Ops:
  0.6 1.2 pad_maximum_fusion.norm
  1.8 0.7 reshape_squeeze.6
  2.6 0.7 reshape_squeeze.7
  3.3 0.8 copy.31.routes
  4.2 51.6 %shard_map.238 = (bf16[1024,3328]{1,0:T(8,128)(2,1)}, f32[3,128,5632]{2,1,0:T(8,128)}, f32[3,128,5632]{2,1,0:T(8,128)}, bf16[4,3,512,128]{3,2,1,0:T(8,128)(2,1)}...) custom-call(bf16[448,128]{1,0:T(8,128)(2,1)} %bitcast.39, bf16[448,128]{1,0:T(8,128)(2,1)} %bitcast.40, ...), custom_call_target="tpu_custom_call" | custom-call | tf_op jit(solution)/shard_map/pallas_call | solution.py:310
  55.8 107.4 %shard_map.239 = (bf16[4,512,128]{2,1,0:T(8,128)(2,1)}, bf16[7,2048,128]{2,1,0:T(8,128)(2,1)}, f32[2048,128]{1,0:T(8,128)}, f32[8,2048]{1,0:T(8,128)}, bf16[8,12...) custom-call(bf16[4,3,512,128]{3,2,1,0:T(8,128)(2,1)} %get-tuple-element.50.qkv, ...), custom_call_target="tpu_custom_call" | custom-call | tf_op jit(solution)/shard_map/pallas_call | solution.py:563
  163.1 108.4 %shard_map.240 = (bf16[512,1024]{1,0:T(8,128)(2,1)}, f32[512,1024]{1,0:T(8,128)}, bf16[4,512,128]{2,1,0:T(8,128)(2,1)}, f32[512,128]{1,0:T(8,128)}, f32[8,1024]{...) custom-call(bf16[4,512,128]{2,1,0:T(8,128)(2,1)} %get-tuple-element.52.att, ...), custom_call_target="tpu_custom_call" | custom-call | tf_op jit(solution)/shard_map/pallas_call | solution.py:1248
  271.6 101.2 %shard_map.241 = (bf16[4,3,512,128]{3,2,1,0:T(8,128)(2,1)}, f32[128,4096]{1,0:T(8,128)}) custom-call(bf16[4,512,128]{2,1,0:T(8,128)(2,1)} %get-tuple-element.58.grad_att, f32[3,128,5632]{2,1,0:T(8,128)} %get-tuple-element.59.turned_in, bf16[7,2048,128]{2,1,0:T(8,128)(2,1)} %get-tuple-element.60.store_in, f32[2048,128]{1,0:T(8,128)} %get-tuple-element.61.outputs, ...), custom_call_target="tpu_custom_call" | custom-call | tf_op jit(solution)/shard_map/pallas_call | solution.py:955
  372.8 72.1 %shard_map.242 = (f32[512,1024]{1,0:T(8,128)}, f32[128,3328]{1,0:T(8,128)}, f32[280,1024]{1,0:T(8,128)}) custom-call(bf16[4,3,512,128]{3,2,1,0:T(8,128)(2,1)} %get-tuple-element.64.back, bf16[20,512,128]{2,1,0:T(8,128)(2,1)} %get-tuple-element.65.experts, f32[2,512,128]{2,1,0:T(8,128)} %get-tuple-element.53.gates, f32[512,128]{1,0:T(8,128)} %get-tuple-element.66.grad_logit, ...), custom_call_target="tpu_custom_call" | custom-call | tf_op jit(solution)/shard_map/pallas_call | solution.py:1380
  444.9 8.2 %shard_map.243 = (f32[448,128]{1,0:T(8,128)}, f32[448,128]{1,0:T(8,128)}, f32[2240,128]{1,0:T(8,128)}, f32[20,128]{1,0:T(8,128)}, f32[20,128]{1,0:T(8,128)}, /*i...) custom-call(f32[128,3328]{1,0:T(8,128)} %get-tuple-element.71.joint_, ...), custom_call_target="tpu_custom_call" | custom-call | tf_op jit(solution)/shard_map/pallas_call | solution.py:1434
  453.1 1.3 slice_bitcast_fusion
  (1 shorter events, 0.0 us)

commit v7 on v5

--- a/solution.py
+++ b/solution.py
@@ -644,11 +644,14 @@
             self.load_copy(t, rel).wait()
         self.plane_copy(t, rel).start()
 
-    def all_ready(self, t):
-        for rel in self.order():
+    def open(self, t):
+        for rel in self.rels(self.far):
             self.ready(t, rel)
 
-    def step(self, t, D):
+    def step(self, t, D, ahead=True):
+        if ahead and D:
+            for rel in self.rels(D - 1):
+                self.ready(t, rel)
         self.combine(t, D)
         if D:
             self.chain(t, D)
@@ -686,7 +689,7 @@
             ref = self.plane_in[t].at[rel]
             self.remote(ref, ref, self.plane_s, self.plane_r, t * self.count + rel, self.plane_mate).wait_recv()
             own = self.own_ref(t, 1, rel)
-            own[...] = (own[...].astype(jnp.float32) + self.plane_in[t][rel].astype(jnp.float32)).astype(jnp.bfloat16)
+            own[...] = own[...] + self.plane_in[t][rel]
 
     def chain(self, t, D):
         for kind in self.kinds(t):
@@ -697,7 +700,7 @@
                     self.ring_wait(t, kind, way, D + 1)
                     rel = D % self.count if way == 0 else (-D) % self.count
                     ref = self.buffer(t, kind, self.slot(kind, way, D + 1))
-                    ref[...] = (ref[...].astype(jnp.float32) + self.own_ref(t, kind, rel)[...].astype(jnp.float32)).astype(jnp.bfloat16)
+                    ref[...] = ref[...] + self.own_ref(t, kind, rel)[...]
                 self.ring_copy(t, kind, way, D).start()
 
     def end_copy(self, t):
@@ -899,7 +902,7 @@
     begin, ready, first, hop, lag = steps
     rest = []
     for t in range(T):
-        plan = [(begin, functools.partial(ring.start, t)), (ready, functools.partial(ring.all_ready, t))]
+        plan = [(begin, functools.partial(ring.start, t)), (ready, functools.partial(ring.open, t))]
         when = first + lag * t
         for D in range(ring.far, -1, -1):
             plan.append((when, functools.partial(ring.step, t, D)))
@@ -1130,7 +1133,7 @@
         for step, rel in enumerate(ring.order()):
             events.setdefault(step, []).append(functools.partial(ring.ready, 0, rel))
         for D in range(ring.far, 0, -1):
-            events.setdefault(2 * (ring.far - D) + 1, []).append(functools.partial(ring.step, 0, D))
+            events.setdefault(2 * (ring.far - D) + 1, []).append(functools.partial(ring.step, 0, D, False))
 
     def after_parts(step):
         for when, actions in sorted(events.items()):
@@ -1158,7 +1161,7 @@
         for action in events[chunks - 1]:
             action()
     else:
-        ring.all_ready(0)
+        ring.open(0)
         for D in range(ring.far, 0, -1):
             ring.step(0, D)
     layer_out[...] = acc[...].astype(jnp.bfloat16)
@@ -1280,7 +1283,7 @@
     pair = [remote(tokens, tokens_in, 0), remote(grad_norms, norms_in, 1)]
     pair[0].start()
     pair[1].start()
-    ring.all_ready(1)
+    ring.open(1)
     rows = tokens.shape[0]
     lane = lax.broadcasted_iota(jnp.int32, (LANES, LANES), 1)
     width = HEADS * EXP
@@ -1333,9 +1336,10 @@
         tile = total[:, norm_tile : norm_tile + LANES] + extra * core.astype(jnp.float32)
         ring.mine[0][rel, :, norm_tile : norm_tile + LANES] = tile.astype(jnp.bfloat16)
 
-    for rel in ring.order():
+    for i, rel in enumerate(ring.order()):
         fill(rel)
-        ring.ready(0, rel)
+        if i == 0:
+            ring.open(0)
     ring.step(0, ring.far)
     for D in range(ring.far - 1, 0, -1):
         ring.step(1, D)

time: 462 us -> 462 us (level)
  no operation moved by 1% of the time
where the time goes in v7:
time: 462 us; the launch traced here: 454 us
  Pallas kernels  448 us (97%)
    pallas_call x1, Pallas kernels, attend(): pl.pallas_call(functools.partial(attend_kernel, count, splits, steps), ou...  107 us
    pallas_call x1, Pallas kernels, feed(): pl.pallas_call(functools.partial(feed_kernel, count), out_shape=[jax.Shap...  106 us
    pallas_call x1, Pallas kernels, retreat(): pl.pallas_call(functools.partial(retreat_kernel, count, splits, steps), o...  101 us
    pallas_call x1, Pallas kernels, settle(): pl.pallas_call(functools.partial(settle_kernel, count), out_shape=[jax.Sh...  73.5 us
    pallas_call x1, Pallas kernels, project(): pl.pallas_call(functools.partial(project_kernel, count), out_shape=[jax.S...  51.6 us

profile of v7, /device:TPU:0, one launch (start us, length us, event | category | flops | bytes accessed | tf_op | source)
XLA Modules:
  0.0 453.6 jit_solution(13426762910269571264)
XLA Ops:
  0.6 1.2 pad_maximum_fusion.norm
  1.8 0.7 reshape_squeeze.6
  2.6 0.7 reshape_squeeze.7
  3.3 0.8 copy.31.routes
  4.2 51.6 %shard_map.238 = (bf16[1024,3328]{1,0:T(8,128)(2,1)}, f32[3,128,5632]{2,1,0:T(8,128)}, f32[3,128,5632]{2,1,0:T(8,128)}, bf16[4,3,512,128]{3,2,1,0:T(8,128)(2,1)}...) custom-call(bf16[448,128]{1,0:T(8,128)(2,1)} %bitcast.39, bf16[448,128]{1,0:T(8,128)(2,1)} %bitcast.40, ...), custom_call_target="tpu_custom_call" | custom-call | tf_op jit(solution)/shard_map/pallas_call | solution.py:310
  55.8 107.4 %shard_map.239 = (bf16[4,512,128]{2,1,0:T(8,128)(2,1)}, bf16[7,2048,128]{2,1,0:T(8,128)(2,1)}, f32[2048,128]{1,0:T(8,128)}, f32[8,2048]{1,0:T(8,128)}, bf16[8,12...) custom-call(bf16[4,3,512,128]{3,2,1,0:T(8,128)(2,1)} %get-tuple-element.50.qkv, ...), custom_call_target="tpu_custom_call" | custom-call | tf_op jit(solution)/shard_map/pallas_call | solution.py:563
  163.1 106.1 %shard_map.240 = (bf16[512,1024]{1,0:T(8,128)(2,1)}, f32[512,1024]{1,0:T(8,128)}, bf16[4,512,128]{2,1,0:T(8,128)(2,1)}, f32[512,128]{1,0:T(8,128)}, f32[8,1024]{...) custom-call(bf16[4,512,128]{2,1,0:T(8,128)(2,1)} %get-tuple-element.52.att, ...), custom_call_target="tpu_custom_call" | custom-call | tf_op jit(solution)/shard_map/pallas_call | solution.py:1235
  269.3 100.9 %shard_map.241 = (bf16[4,3,512,128]{3,2,1,0:T(8,128)(2,1)}, f32[128,4096]{1,0:T(8,128)}) custom-call(bf16[4,512,128]{2,1,0:T(8,128)(2,1)} %get-tuple-element.58.grad_att, f32[3,128,5632]{2,1,0:T(8,128)} %get-tuple-element.59.turned_in, bf16[7,2048,128]{2,1,0:T(8,128)(2,1)} %get-tuple-element.60.store_in, f32[2048,128]{1,0:T(8,128)} %get-tuple-element.61.outputs, ...), custom_call_target="tpu_custom_call" | custom-call | tf_op jit(solution)/shard_map/pallas_call | solution.py:958
  370.2 73.5 %shard_map.242 = (f32[512,1024]{1,0:T(8,128)}, f32[128,3328]{1,0:T(8,128)}, f32[280,1024]{1,0:T(8,128)}) custom-call(bf16[4,3,512,128]{3,2,1,0:T(8,128)(2,1)} %get-tuple-element.64.back, bf16[20,512,128]{2,1,0:T(8,128)(2,1)} %get-tuple-element.65.experts, f32[2,512,128]{2,1,0:T(8,128)} %get-tuple-element.53.gates, f32[512,128]{1,0:T(8,128)} %get-tuple-element.66.grad_logit, ...), custom_call_target="tpu_custom_call" | custom-call | tf_op jit(solution)/shard_map/pallas_call | solution.py:1368
  443.7 8.2 %shard_map.243 = (f32[448,128]{1,0:T(8,128)}, f32[448,128]{1,0:T(8,128)}, f32[2240,128]{1,0:T(8,128)}, f32[20,128]{1,0:T(8,128)}, f32[20,128]{1,0:T(8,128)}, /*i...) custom-call(f32[128,3328]{1,0:T(8,128)} %get-tuple-element.71.joint_, ...), custom_call_target="tpu_custom_call" | custom-call | tf_op jit(solution)/shard_map/pallas_call | solution.py:1422
  451.9 1.3 slice_bitcast_fusion
  (1 shorter events, 0.0 us)

commit v8 on v7

--- a/solution.py
+++ b/solution.py
@@ -1177,7 +1177,6 @@
     branch_low[...] = total.astype(jnp.bfloat16)
     pair[4].start()
     branch_t[:, :rows] = branch_low[:, mine].T
-    ring.step(0, 0)
     lane = lax.broadcasted_iota(jnp.int32, (rows, LANES), 1)
     logit = jnp.zeros((rows, LANES), jnp.float32)
     head_total = None
@@ -1195,7 +1194,7 @@
         sums = jnp.sum(grad_mixed * att[head].astype(jnp.float32), axis=1, keepdims=True)
         logit = jnp.where(lane == experts + which, sums, logit)
     grad_logit[...] = logit * gates[1]
-    ring.deliver(0)
+    ring.step(0, 0)
     pair[0].wait_recv()
     pair[1].wait_recv()
     pair[4].wait_recv()
@@ -1214,6 +1213,7 @@
                 put_output_copy(which - 4).wait()
             stage_output[which % 4] = turned[side * LANES : (side + 1) * LANES]
             put_output_copy(which).start()
+    ring.deliver(0)
     for which in range(experts - 4, experts):
         put_output_copy(which).wait()
     for sub in range(2):
@@ -1395,13 +1395,6 @@
         copy.start()
         stores.append(copy)
 
-    loads[0].wait()
-    turned[...] = held[0][...].T
-    for first, target in ((0, query), (QCOLS, key), (2 * QCOLS, value), (ROUTERS, value_router)):
-        put(turned.at[pl.ds(first, target.shape[0])], target)
-    tail[...] = turned[ROUTERS + HEADS * EXP : NORM, :]
-    put(tail, output_router)
-    norms[...] = turned[NORM : NORM + 8, :]
     for i, target in enumerate((tokens_out, inner_out, outer_out, layer_out, output_out)):
         loads[1 + i].wait()
         if i != 1:
@@ -1410,6 +1403,13 @@
         for core in range(2):
             for chunk in range(half // small):
                 put(held[1 + i].at[:, pl.ds(core * half + chunk * small, small)], target.at[:, pl.ds(chunk * CHUNK + core * small, small)])
+    loads[0].wait()
+    turned[...] = held[0][...].T
+    for first, target in ((0, query), (QCOLS, key), (2 * QCOLS, value), (ROUTERS, value_router)):
+        put(turned.at[pl.ds(first, target.shape[0])], target)
+    tail[...] = turned[ROUTERS + HEADS * EXP : NORM, :]
+    put(tail, output_router)
+    norms[...] = turned[NORM : NORM + 8, :]
     for copy in stores:
         copy.wait()
 

time: 462 us -> 456 us (0.987)
  Pallas kernels: 448 us -> 442 us
    pallas_call x1, Pallas kernels: 106 us -> 100 us  [feed(): pl.pallas_call(functools.partial(feed_kernel, count), out_shape=[jax.Shap...]
where the time goes in v8:
time: 456 us; the launch traced here: 448 us
  Pallas kernels  442 us (97%)
    pallas_call x1, Pallas kernels, attend(): pl.pallas_call(functools.partial(attend_kernel, count, splits, steps), ou...  107 us
    pallas_call x1, Pallas kernels, retreat(): pl.pallas_call(functools.partial(retreat_kernel, count, splits, steps), o...  100 us
    pallas_call x1, Pallas kernels, feed(): pl.pallas_call(functools.partial(feed_kernel, count), out_shape=[jax.Shap...  100 us
    pallas_call x1, Pallas kernels, settle(): pl.pallas_call(functools.partial(settle_kernel, count), out_shape=[jax.Sh...  73.5 us
    pallas_call x1, Pallas kernels, project(): pl.pallas_call(functools.partial(project_kernel, count), out_shape=[jax.S...  51.6 us

profile of v8, /device:TPU:0, one launch (start us, length us, event | category | flops | bytes accessed | tf_op | source)
XLA Modules:
  0.0 447.5 jit_solution(6880466176172065204)
XLA Ops:
  0.6 1.2 pad_maximum_fusion.norm
  1.8 0.7 reshape_squeeze.6
  2.6 0.7 reshape_squeeze.7
  3.3 0.8 copy.31.routes
  4.2 51.6 %shard_map.238 = (bf16[1024,3328]{1,0:T(8,128)(2,1)}, f32[3,128,5632]{2,1,0:T(8,128)}, f32[3,128,5632]{2,1,0:T(8,128)}, bf16[4,3,512,128]{3,2,1,0:T(8,128)(2,1)}...) custom-call(bf16[448,128]{1,0:T(8,128)(2,1)} %bitcast.39, bf16[448,128]{1,0:T(8,128)(2,1)} %bitcast.40, ...), custom_call_target="tpu_custom_call" | custom-call | tf_op jit(solution)/shard_map/pallas_call | solution.py:310
  55.8 107.4 %shard_map.239 = (bf16[4,512,128]{2,1,0:T(8,128)(2,1)}, bf16[7,2048,128]{2,1,0:T(8,128)(2,1)}, f32[2048,128]{1,0:T(8,128)}, f32[8,2048]{1,0:T(8,128)}, bf16[8,12...) custom-call(bf16[4,3,512,128]{3,2,1,0:T(8,128)(2,1)} %get-tuple-element.50.qkv, ...), custom_call_target="tpu_custom_call" | custom-call | tf_op jit(solution)/shard_map/pallas_call | solution.py:563
  163.1 100.2 %shard_map.240 = (bf16[512,1024]{1,0:T(8,128)(2,1)}, f32[512,1024]{1,0:T(8,128)}, bf16[4,512,128]{2,1,0:T(8,128)(2,1)}, f32[512,128]{1,0:T(8,128)}, f32[8,1024]{...) custom-call(bf16[4,512,128]{2,1,0:T(8,128)(2,1)} %get-tuple-element.52.att, ...), custom_call_target="tpu_custom_call" | custom-call | tf_op jit(solution)/shard_map/pallas_call | solution.py:1235
  263.3 100.4 %shard_map.241 = (bf16[4,3,512,128]{3,2,1,0:T(8,128)(2,1)}, f32[128,4096]{1,0:T(8,128)}) custom-call(bf16[4,512,128]{2,1,0:T(8,128)(2,1)} %get-tuple-element.58.grad_att, f32[3,128,5632]{2,1,0:T(8,128)} %get-tuple-element.59.turned_in, bf16[7,2048,128]{2,1,0:T(8,128)(2,1)} %get-tuple-element.60.store_in, f32[2048,128]{1,0:T(8,128)} %get-tuple-element.61.outputs, ...), custom_call_target="tpu_custom_call" | custom-call | tf_op jit(solution)/shard_map/pallas_call | solution.py:958
  363.7 73.5 %shard_map.242 = (f32[512,1024]{1,0:T(8,128)}, f32[128,3328]{1,0:T(8,128)}, f32[280,1024]{1,0:T(8,128)}) custom-call(bf16[4,3,512,128]{3,2,1,0:T(8,128)(2,1)} %get-tuple-element.64.back, bf16[20,512,128]{2,1,0:T(8,128)(2,1)} %get-tuple-element.65.experts, f32[2,512,128]{2,1,0:T(8,128)} %get-tuple-element.53.gates, f32[512,128]{1,0:T(8,128)} %get-tuple-element.66.grad_logit, ...), custom_call_target="tpu_custom_call" | custom-call | tf_op jit(solution)/shard_map/pallas_call | solution.py:1368
  437.3 8.5 %shard_map.243 = (f32[448,128]{1,0:T(8,128)}, f32[448,128]{1,0:T(8,128)}, f32[2240,128]{1,0:T(8,128)}, f32[20,128]{1,0:T(8,128)}, f32[20,128]{1,0:T(8,128)}, /*i...) custom-call(f32[128,3328]{1,0:T(8,128)} %get-tuple-element.71.joint_, ...), custom_call_target="tpu_custom_call" | custom-call | tf_op jit(solution)/shard_map/pallas_call | solution.py:1422
  445.8 1.3 slice_bitcast_fusion
  (1 shorter events, 0.0 us)

commit v9 on v8

--- a/solution.py
+++ b/solution.py
@@ -279,7 +279,8 @@
     local_rows = tokens.shape[0]
     wide = jnp.concatenate([logits, jnp.zeros((local_rows, LANES - 2 * HEADS * EXP), jnp.float32)], axis=1)
     lane = lax.broadcasted_iota(jnp.int32, (local_rows, LANES), 1)
-    mask = route_lanes(routes[...], lane)
+    chosen = jnp.concatenate([routes[...].astype(jnp.float32), jnp.zeros((LANES - routes.shape[0], local_rows), jnp.float32)], axis=0)
+    mask = route_lanes(chosen.T.astype(jnp.int32), lane)
     gate = 1.0 / (1.0 + jnp.exp(-wide))
     gates[0] = gate * mask
     gates[1] = gate * mask * (1.0 - gate)
@@ -1310,8 +1311,10 @@
         hand_over(block).start()
         return carry
 
-    lax.fori_loop(0, rows // LANES, assemble, 0)
+    split = rows // LANES // 2
+    lax.fori_loop(0, split, assemble, 0)
     ring.step(1, ring.far)
+    lax.fori_loop(split, rows // LANES, assemble, 0)
     tokens_t[:, :rows] = tokens[...].T
     for copy in pair:
         copy.wait_recv()
@@ -1340,17 +1343,18 @@
         fill(rel)
         if i == 0:
             ring.open(0)
+    if ring.far > 1:
+        ring.step(1, ring.far - 1)
     ring.step(0, ring.far)
+    for copy in loads:
+        copy.wait()
     for D in range(ring.far - 1, 0, -1):
-        ring.step(1, D)
+        ring.step(1, D - 1)
         ring.step(0, D)
         if D == ring.far - 1:
-            for copy in loads:
-                copy.wait()
             grad_tokens[...] = grad_residual[...] + contract(grads[...], joint[...], 1, 1)
-    ring.step(1, 0)
+    ring.deliver(1)
     ring.step(0, 0)
-    ring.deliver(1)
     ring.deliver(0)
     ring.finish(1)
     ring.finish(0)
@@ -1440,7 +1444,7 @@
     inputs = tokens[0]
     rows, width = inputs.shape
     norm = jnp.stack([norm_gain, norm_bias])
-    routes = jnp.concatenate([value_routes[0].reshape(rows, -1), output_routes[0].reshape(rows, -1)], axis=1)
+    routes = jnp.concatenate([r[0].transpose(1, 2, 0).reshape(-1, rows) for r in (value_routes, output_routes)], axis=0)
     joint, tables, turned, qkv, experts, gates, norms = project(
         count, query_weight.T, key_weight.T, value_weight.T, value_router.T, output_router.T, norm, inputs, routes, cont_gap)
     att, store, outputs, logs, inner_full, outer_full, output_full = attend(

time: 456 us -> 453 us (level)
  no operation moved by 1% of the time
where the time goes in v9:
time: 453 us; the launch traced here: 445 us
  Pallas kernels  439 us (97%)
    pallas_call x1, Pallas kernels, attend(): pl.pallas_call(functools.partial(attend_kernel, count, splits, steps), ou...  107 us
    pallas_call x1, Pallas kernels, retreat(): pl.pallas_call(functools.partial(retreat_kernel, count, splits, steps), o...  100 us
    pallas_call x1, Pallas kernels, feed(): pl.pallas_call(functools.partial(feed_kernel, count), out_shape=[jax.Shap...  100 us
    pallas_call x1, Pallas kernels, settle(): pl.pallas_call(functools.partial(settle_kernel, count), out_shape=[jax.Sh...  71 us
    pallas_call x1, Pallas kernels, project(): pl.pallas_call(functools.partial(project_kernel, count), out_shape=[jax.S...  51.5 us

profile of v9, /device:TPU:0, one launch (start us, length us, event | category | flops | bytes accessed | tf_op | source)
XLA Modules:
  0.0 444.7 jit_solution(11244018066432057238)
XLA Ops:
  0.6 1.2 pad_maximum_fusion.norm
  1.8 0.7 reshape.45
  2.6 0.7 reshape.46
  3.3 0.6 pad_add_fusion.routes
  3.9 51.5 %shard_map.238 = (bf16[1024,3328]{1,0:T(8,128)(2,1)}, f32[3,128,5632]{2,1,0:T(8,128)}, f32[3,128,5632]{2,1,0:T(8,128)}, bf16[4,3,512,128]{3,2,1,0:T(8,128)(2,1)}...) custom-call(bf16[448,128]{1,0:T(8,128)(2,1)} %bitcast.41, bf16[448,128]{1,0:T(8,128)(2,1)} %bitcast.42, ...), custom_call_target="tpu_custom_call" | custom-call | tf_op jit(solution)/shard_map/pallas_call | solution.py:311
  55.5 107.4 %shard_map.239 = (bf16[4,512,128]{2,1,0:T(8,128)(2,1)}, bf16[7,2048,128]{2,1,0:T(8,128)(2,1)}, f32[2048,128]{1,0:T(8,128)}, f32[8,2048]{1,0:T(8,128)}, bf16[8,12...) custom-call(bf16[4,3,512,128]{3,2,1,0:T(8,128)(2,1)} %get-tuple-element.50.qkv, ...), custom_call_target="tpu_custom_call" | custom-call | tf_op jit(solution)/shard_map/pallas_call | solution.py:564
  162.9 100.2 %shard_map.240 = (bf16[512,1024]{1,0:T(8,128)(2,1)}, f32[512,1024]{1,0:T(8,128)}, bf16[4,512,128]{2,1,0:T(8,128)(2,1)}, f32[512,128]{1,0:T(8,128)}, f32[8,1024]{...) custom-call(bf16[4,512,128]{2,1,0:T(8,128)(2,1)} %get-tuple-element.52.att, ...), custom_call_target="tpu_custom_call" | custom-call | tf_op jit(solution)/shard_map/pallas_call | solution.py:1236
  263.0 100.5 %shard_map.241 = (bf16[4,3,512,128]{3,2,1,0:T(8,128)(2,1)}, f32[128,4096]{1,0:T(8,128)}) custom-call(bf16[4,512,128]{2,1,0:T(8,128)(2,1)} %get-tuple-element.58.grad_att, f32[3,128,5632]{2,1,0:T(8,128)} %get-tuple-element.59.turned_in, bf16[7,2048,128]{2,1,0:T(8,128)(2,1)} %get-tuple-element.60.store_in, f32[2048,128]{1,0:T(8,128)} %get-tuple-element.61.outputs, ...), custom_call_target="tpu_custom_call" | custom-call | tf_op jit(solution)/shard_map/pallas_call | solution.py:959
  363.5 71.0 %shard_map.242 = (f32[512,1024]{1,0:T(8,128)}, f32[128,3328]{1,0:T(8,128)}, f32[280,1024]{1,0:T(8,128)}) custom-call(bf16[4,3,512,128]{3,2,1,0:T(8,128)(2,1)} %get-tuple-element.64.back, bf16[20,512,128]{2,1,0:T(8,128)(2,1)} %get-tuple-element.65.experts, f32[2,512,128]{2,1,0:T(8,128)} %get-tuple-element.53.gates, f32[512,128]{1,0:T(8,128)} %get-tuple-element.66.grad_logit, ...), custom_call_target="tpu_custom_call" | custom-call | tf_op jit(solution)/shard_map/pallas_call | solution.py:1372
  434.5 8.5 %shard_map.243 = (f32[448,128]{1,0:T(8,128)}, f32[448,128]{1,0:T(8,128)}, f32[2240,128]{1,0:T(8,128)}, f32[20,128]{1,0:T(8,128)}, f32[20,128]{1,0:T(8,128)}, /*i...) custom-call(f32[128,3328]{1,0:T(8,128)} %get-tuple-element.71.joint_, ...), custom_call_target="tpu_custom_call" | custom-call | tf_op jit(solution)/shard_map/pallas_call | solution.py:1426
  443.0 1.3 slice_bitcast_fusion
